TPU v7x, 32 devices: a whole 2x2x4 slice. The times are simulated.
32 devices in a mesh: dp: 4 (over y, x), tensor: 8 (over z, core).
Axes of the slice: x: 2, y: 2, z: 4, core: 2. Of those that a mesh axis runs over, the one named last changes fastest.
Arguments:
- hidden: bfloat16 [4096, 1280], P(('dp', 'tensor')), may hold values from -6 to 6
- lengths: int32 [4, 8], P('dp'), may hold values from 1 to 512, 1024 in all within a row
- request_prompt: int32 [4, 8], P('dp'), may hold values from 0 to 31
- request_adapter: int32 [4, 8], P('dp'), may hold values from 0 to 63
- prompt_page_table: int32 [32, 4], replicated, may hold values from 0 to 15
- prefix_page_cache: bfloat16 [16, 64, 2048], P('dp', None, 'tensor'), may hold values from -6 to 6
- query_key_value_weight: bfloat16 [1280, 3072], P(None, 'tensor'), may hold values from -0.15625 to 0.15625
- adapter_down: bfloat16 [64, 1280, 16], P('dp'), may hold values from -0.15625 to 0.15625
- adapter_up: bfloat16 [64, 16, 3072], P('dp', None, 'tensor'), may hold values from -1.5 to 1.5
- attention_scale: float32 [1024], P('tensor'), may hold values from 0.5 to 1.5
- output_matrix: bfloat16 [1024, 1280], P('tensor'), may hold values from -0.1875 to 0.1875
- attention_rate: float32 [1280], replicated, may hold values from 0.05 to 0.5
- up_matrix: bfloat16 [1280, 5120], P(None, 'tensor'), may hold values from -0.15625 to 0.15625
- gate_matrix: bfloat16 [1280, 5120], P(None, 'tensor'), may hold values from -0.15625 to 0.15625
- up_scaling: float32 [5120], P('tensor'), may hold values from 0.5 to 2
- gate_scaling: float32 [5120], P('tensor'), may hold values from 0.5 to 2
- down_matrix: bfloat16 [5120, 1280], P('tensor'), may hold values from -0.078125 to 0.078125
- feedforward_rate: float32 [1280], replicated, may hold values from 0.05 to 0.5
Outputs:
- hidden_out: bfloat16 [4096, 1280], P(('dp', 'tensor'))
Inputs may be any that keep to these rules, and one draw needn't show every extreme that they name: Each group's lengths sum to 1024.
All inputs are finite; a program needn't handle non-finite values.
Results may differ from a plain program's by a relative error of at most 0.015.
Values may be sent and summed in bfloat16 or wider, within the bound.
No kernel may reach another device: no remote copies, remote signals or barrier semaphores. Data moves between devices by JAX's collectives and lax.ppermute only.
A program may use at most 64 MiB of HBM per device.

v0:
```python
import math

import jax
import jax.numpy as jnp
from jax import lax
from jax.sharding import PartitionSpec as P

MODEL_WIDTH = 1280
HEAD_WIDTH = 64
ADAPTER_RANK = 16
GROUP_REQUESTS = 8
PAGE = 64
PREFIX_LEN = 256


adapter_scale = 0.5
epsilon = 1e-06


def renorm(matrix):
    return matrix * lax.rsqrt(jnp.mean(matrix * matrix, axis=-1, keepdims=True) + epsilon)


def to_unit(vectors):
    return vectors * lax.rsqrt(jnp.sum(vectors * vectors, axis=-1, keepdims=True) + epsilon)


def rotate(vectors, position):
    half_size = vectors.shape[-1] // 2
    frequency = jnp.exp(
        jnp.arange(half_size).astype(jnp.float32) * (-2.0 * math.log(10000.0) / vectors.shape[-1])
    )
    angles = position[:, None] * frequency[None, :]
    cosine = jnp.cos(angles)[:, None, :]
    sines = jnp.sin(angles)[:, None, :]
    first_half = vectors[..., :half_size]
    second_half = vectors[..., half_size:]
    return jnp.concatenate(
        [first_half * cosine - second_half * sines, first_half * sines + second_half * cosine],
        axis=-1,
    )


def layout(counts, total_rows):
    row_ends = jnp.cumsum(counts)
    starts = row_ends - counts
    row_ids = jnp.arange(total_rows, dtype=jnp.int32)
    request_number = jnp.sum((row_ids[:, None] >= row_ends[None, :]).astype(jnp.int32), axis=1)
    selected_adapter = (
        request_number[:, None] == jnp.arange(counts.shape[0], dtype=jnp.int32)[None, :]
    )
    offset = row_ids - jnp.sum(jnp.where(selected_adapter, starts[None, :], 0), axis=1)
    return (request_number, offset)


def attend(queries, key_all, value_all, request_number, key_request, key_row):
    rows_total = queries.shape[0]
    block_rows = min(512, rows_total)
    score_scale = math.sqrt(queries.shape[-1])
    row_ids = jnp.arange(rows_total, dtype=jnp.int32)

    def one_block(block_index):
        first_row = block_index * block_rows
        query_block = lax.dynamic_slice_in_dim(queries, first_row, block_rows, 0)
        request_block = lax.dynamic_slice_in_dim(request_number, first_row, block_rows, 0)
        row_block = lax.dynamic_slice_in_dim(row_ids, first_row, block_rows, 0)
        scores = (
            jnp.einsum("qhd,khd->hqk", query_block, key_all, preferred_element_type=jnp.float32)
            * score_scale
        )
        allowed = (request_block[:, None] == key_request[None, :]) & (
            key_row[None, :] <= row_block[:, None]
        )
        exp_scores = jnp.where(allowed[None], jnp.exp(scores), 0.0)
        weights = (exp_scores / jnp.sum(exp_scores, axis=-1, keepdims=True)).astype(jnp.bfloat16)
        mixed_block = jnp.einsum(
            "hqk,khd->qhd", weights, value_all, preferred_element_type=jnp.float32
        )
        return mixed_block.reshape(block_rows, -1).astype(jnp.bfloat16)

    blocks = lax.map(one_block, jnp.arange(rows_total // block_rows, dtype=jnp.int32))
    return blocks.reshape(rows_total, -1)


def hidden_units(row_values, up_matrix, gate_matrix, up_scaling, gate_scaling):
    up_part = jnp.dot(row_values, up_matrix, preferred_element_type=jnp.float32) * up_scaling
    gate_part = jnp.dot(row_values, gate_matrix, preferred_element_type=jnp.float32) * gate_scaling
    return (up_part * jax.nn.silu(gate_part)).astype(jnp.bfloat16)


def local(
    hidden,
    lengths,
    request_prompt,
    request_adapter,
    prompt_page_table,
    prefix_page_cache,
    query_key_value_weight,
    adapter_down,
    adapter_up,
    attention_scale,
    output_matrix,
    attention_rate,
    up_matrix,
    gate_matrix,
    up_scaling,
    gate_scaling,
    down_matrix,
    feedforward_rate,
):
    tok_rows = hidden.shape[0]
    group_rows = tok_rows * lax.axis_size("tensor")
    heads_here = query_key_value_weight.shape[1] // (3 * HEAD_WIDTH)
    gain_qk = attention_scale.reshape(heads_here, HEAD_WIDTH)
    request_number, offset = layout(lengths[0], group_rows)
    position = offset.astype(jnp.float32) + PREFIX_LEN
    local_cache = prefix_page_cache.reshape(
        prefix_page_cache.shape[0], PAGE, heads_here, 2, HEAD_WIDTH
    )
    local_keys = (to_unit(local_cache[:, :, :, 0, :].astype(jnp.float32)) * gain_qk).astype(
        jnp.bfloat16
    )
    prepared = jnp.stack([local_keys, local_cache[:, :, :, 1, :]], axis=3).reshape(
        prefix_page_cache.shape
    )
    all_pages = lax.all_gather(prepared, "dp", axis=0, tiled=True)
    down_all, up_all = (
        lax.all_gather(adapter_down, "dp", axis=0, tiled=True),
        lax.all_gather(adapter_up, "dp", axis=0, tiled=True),
    )
    every_row = lax.all_gather(hidden, "tensor", axis=0, tiled=True)
    adapter_count = down_all.shape[0]
    onehot = (
        request_adapter[0][:, None] == jnp.arange(adapter_count, dtype=jnp.int32)[None, :]
    ).astype(jnp.bfloat16)
    selected_down = jnp.dot(
        onehot, down_all.reshape(adapter_count, -1), preferred_element_type=jnp.float32
    ).astype(jnp.bfloat16)
    selected_down = jnp.transpose(
        selected_down.reshape(GROUP_REQUESTS, MODEL_WIDTH, ADAPTER_RANK), (1, 0, 2)
    ).reshape(MODEL_WIDTH, GROUP_REQUESTS * ADAPTER_RANK)
    selected_up = jnp.dot(
        onehot, up_all.reshape(adapter_count, -1), preferred_element_type=jnp.float32
    ).astype(jnp.bfloat16)
    selected_up = selected_up.reshape(GROUP_REQUESTS * ADAPTER_RANK, heads_here * 3 * HEAD_WIDTH)
    request_of_slot = jnp.arange(GROUP_REQUESTS * ADAPTER_RANK, dtype=jnp.int32) // ADAPTER_RANK
    plain_projection = jnp.dot(
        every_row, query_key_value_weight, preferred_element_type=jnp.float32
    )
    adapter_middle = jnp.dot(every_row, selected_down, preferred_element_type=jnp.float32)
    adapter_middle = jnp.where(
        request_number[:, None] == request_of_slot[None, :], adapter_middle, 0.0
    ).astype(jnp.bfloat16)
    query_key_value = (
        plain_projection
        + adapter_scale * jnp.dot(adapter_middle, selected_up, preferred_element_type=jnp.float32)
    ).reshape(group_rows, heads_here, 3, HEAD_WIDTH)
    queries = (to_unit(rotate(query_key_value[:, :, 0, :], position)) * gain_qk).astype(
        jnp.bfloat16
    )
    key_own = (to_unit(rotate(query_key_value[:, :, 1, :], position)) * gain_qk).astype(
        jnp.bfloat16
    )
    value_own = query_key_value[:, :, 2, :].astype(jnp.bfloat16)
    page_list = prompt_page_table[request_prompt[0]].reshape(-1)
    picked = jnp.take(all_pages, page_list, axis=0).reshape(
        GROUP_REQUESTS * PREFIX_LEN, heads_here, 2, HEAD_WIDTH
    )
    key_all = jnp.concatenate([picked[:, :, 0, :], key_own], axis=0)
    value_all = jnp.concatenate([picked[:, :, 1, :], value_own], axis=0)
    key_request = jnp.concatenate(
        [jnp.arange(GROUP_REQUESTS * PREFIX_LEN, dtype=jnp.int32) // PREFIX_LEN, request_number],
        axis=0,
    )
    key_row = jnp.concatenate(
        [
            jnp.full((GROUP_REQUESTS * PREFIX_LEN,), -1, jnp.int32),
            jnp.arange(group_rows, dtype=jnp.int32),
        ],
        axis=0,
    )
    attn = attend(queries, key_all, value_all, request_number, key_request, key_row)
    attn_sum = lax.psum_scatter(
        jnp.dot(attn, output_matrix, preferred_element_type=jnp.float32).astype(jnp.bfloat16),
        "tensor",
        scatter_dimension=0,
        tiled=True,
    ).astype(jnp.float32)
    base_rows = hidden.astype(jnp.float32)
    mixed = renorm(base_rows + attention_rate * (renorm(attn_sum) - base_rows)).astype(jnp.bfloat16)
    unit_values = hidden_units(
        lax.all_gather(mixed, "tensor", axis=0, tiled=True),
        up_matrix,
        gate_matrix,
        up_scaling,
        gate_scaling,
    )
    mlp_sum = lax.psum_scatter(
        jnp.dot(unit_values, down_matrix, preferred_element_type=jnp.float32).astype(jnp.bfloat16),
        "tensor",
        scatter_dimension=0,
        tiled=True,
    ).astype(jnp.float32)
    mixed_rows = mixed.astype(jnp.float32)
    return renorm(mixed_rows + feedforward_rate * (renorm(mlp_sum) - mixed_rows)).astype(
        jnp.bfloat16
    )


def solution(mesh):
    placed = (
        P(("dp", "tensor"), None),
        P("dp", None),
        P("dp", None),
        P("dp", None),
        P(),
        P("dp", None, "tensor"),
        P(None, "tensor"),
        P("dp", None, None),
        P("dp", None, "tensor"),
        P("tensor"),
        P("tensor", None),
        P(),
        P(None, "tensor"),
        P(None, "tensor"),
        P("tensor"),
        P("tensor"),
        P("tensor", None),
        P(),
    )
    return jax.shard_map(
        local, mesh=mesh, in_specs=placed, out_specs=P(("dp", "tensor"), None), check_vma=False
    )
```

profile of v0, /device:TPU:0, one launch (start us, length us, event | category | flops | bytes accessed | tf_op | source)
XLA Modules:
  0.0 265.0 jit_solution(16601916856202040985)
XLA Ops:
  11.1 17.9 %all_gather.17 = bf16[64,16,384]{2,1,0:T(8,128)(2,1)S(1)} all-gather(bf16[16,16,384]{2,1,0:T(8,128)(2,1)} %param.28), channel_id=1, replica_groups=mesh['dp'=4,'tensor'=8] {'dp'}, dimensions={0}, use_global_device_ids=true | all-gather | bytes 983040 | tf_op jit(solution)/shard_map/all_gather | solution.py:129
  33.5 11.8 %all_gather.18 = bf16[16,64,256]{2,1,0:T(8,128)(2,1)S(1)} all-gather(bf16[4,64,256]{2,1,0:T(8,128)(2,1)S(1)} %reshape.324), channel_id=1, replica_groups=mesh['dp'=4,'tensor'=8] {'dp'}, dimensions={0}, use_global_device_ids=true | all-gather | bytes 655360 | tf_op jit(solution)/shard_map/all_gather | solution.py:126
  45.9 1.9 reshape.343
  47.7 4.6 %copy.54 = bf16[2048,2,2,64]{0,3,2,1:T(8,128)(2,1)S(1)} copy(bf16[2048,2,2,64]{3,2,1,0:T(2,128)(2,1)} %reshape.343) | data formatting | bytes 2097152 | tf_op jit(solution)/shard_map/jit(_take)/gather | solution.py:166
  53.3 1.2 multiply_cosine_fusion
  54.7 1.1 slice_bitcast_fusion
  55.7 9.7 %copy.46 = bf16[64,1280,16]{0,2,1:T(8,128)(2,1)} copy(bf16[64,1280,16]{1,2,0:T(8,128)(2,1)} %all-gather.6.cloned.1.call-done) | data formatting | bytes 5242880 | tf_op jit(solution)/shard_map/all_gather | solution.py:128
  65.5 4.0 %convolution_convert_fusion = bf16[8,20480]{1,0:T(8,128)(2,1)S(1)} fusion(bf16[64,20480]{0,1:T(8,128)(2,1)} %bitcast.68, s32[8]{0:T(128)S(1)} %bitcast.78), kind=kOutput, calls=%fused_computation.14 | convolution fusion | flops 21135872 | bytes 2949152 | tf_op jit(solution)/shard_map/dot_general | solution.py:136
  69.4 3.7 %reshape.316 = bf16[8,1280,16]{2,1,0:T(8,128)(2,1)} reshape(bf16[8,20480]{1,0:T(8,128)(2,1)S(1)} %convolution_convert_fusion) | data formatting | bytes 655360 | tf_op jit(solution)/shard_map/reshape | solution.py:140
  73.1 2.1 copy.47
  75.2 16.0 %all-gather.4.cloned.1.call-done = bf16[1024,1280]{1,0:T(8,128)(2,1)} async-done(((bf16[128,1280]{1,0:T(8,128)(2,1)}), bf16[1024,1280]{1,0:T(8,128)(2,1)}) %all-gather.4.cloned.1.call-update) | async-done | bytes 2621456 | tf_op jit(solution)/shard_map/all_gather | solution.py:131
  91.2 4.1 %fusion.30 = f32[1024,384]{0,1:T(8,128)} fusion(bf16[1024,1280]{1,0:T(8,128)(2,1)} %all-gather.4.cloned.1.call-done, bf16[1280,384]{1,0:T(8,128)(2,1)S(1)} %copy-done.15), kind=kOutput, calls=%fused_computation.109 | convolution fusion | flops 1006632960 | bytes 5177344 | tf_op jit(solution)/shard_map/dot_general | solution.py:147
  95.3 3.4 %multiply_add_fusion = f32[1024,384]{0,1:T(8,128)S(1)} fusion(f32[1024,384]{0,1:T(8,128)} %fusion.30, bf16[128,384]{1,0:T(8,128)(2,1)} %reshape.319, bf16[1280,128]{0,1:T(8,128)(2,1)S(1)} %bitcast.75, bf16[1024,1280]{1,0:T(8,128)(2,1)} %all-gather.4.cloned.1.call-done, s32[1024]{0:T(1024)S(1)} %convert_reduce_fusion, s32[128]{0:T(128)} %and_select_fusion), kind=kOutput, calls=%fused_computation.19 | convolution fusion | flops 437387264 | bytes 6197760 | tf_op jit(solution)/shard_map/dot_general | solution.py:156
  101.1 24.1 %while.11 = (s32[]{:T(128)}, bf16[2,512,128]{2,1,0:T(8,128)(2,1)}, s32[2]{0:T(128)S(1)}, s32[1024]{0:T(1024)S(1)}, s32[3072]{0:T(1024)S(1)}, /*index=5*/s32[1024...) while((s32[]{:T(128)}, bf16[2,512,128]{2,1,0:T(8,128)(2,1)}, ...), condition=%wide.region_8.9_spmd, body=%wide.region_6.8_spmd.sunk | while | flops 832109568 | bytes 32289484 | solution.py:81
  102.6 1.5 compare_and_fusion.3
  104.2 5.0 %fusion.55 = (f32[2,512]{1,0:T(2,128)S(1)}, f32[2,512,3072]{2,1,0:T(8,128)S(1)}) fusion(pred[512,3072]{1,0:T(8,128)(4,1)S(1)} %compare_and_fusion.3, bf16[3072,2,64]{0,2,1:T(8,128)(2,1)S(1)} %get-tuple-element.215, bf16[1024,2,64]{0,2,1:T(8,128)(2,1)} %get-tuple-element.214, s32[]{:T(128)S(6)} %select_n.105), kind=kOutput, calls=%fused_computation.4.clone.1 | convolution fusion | flops 412089344 | bytes 15077380 | tf_op jit(solution)/shard_map/while/body/eval_jaxpr/qhd,khd->hqk/dot_general | solution.py:68
  109.2 3.3 %fusion.56 = bf16[2,512,64]{1,2,0:T(8,128)(2,1)S(1)} fusion(bf16[3072,2,64]{0,2,1:T(8,128)(2,1)S(1)} %get-tuple-element.216, f32[2,512,3072]{2,1,0:T(8,128)S(1)} %get-tuple-element.178, f32[2,512]{1,0:T(2,128)S(1)} %get-tuple-element.179, pred[512,3072]{1,0:T(8,128)(4,1)S(1)} %compare_and_fusion.3), kind=kOutput, calls=%fused_computation.7.clone.1 | convolution fusion | flops 415301632 | bytes 15077376 | tf_op jit(solution)/shard_map/while/body/eval_jaxpr/hqk,khd->qhd/dot_general | solution.py:76
  114.6 1.5 compare_and_fusion.3
  116.1 5.0 %fusion.55 = (f32[2,512]{1,0:T(2,128)S(1)}, f32[2,512,3072]{2,1,0:T(8,128)S(1)}) fusion(pred[512,3072]{1,0:T(8,128)(4,1)S(1)} %compare_and_fusion.3, bf16[3072,2,64]{0,2,1:T(8,128)(2,1)S(1)} %get-tuple-element.215, bf16[1024,2,64]{0,2,1:T(8,128)(2,1)} %get-tuple-element.214, s32[]{:T(128)S(6)} %select_n.105), kind=kOutput, calls=%fused_computation.4.clone.1 | convolution fusion | flops 412089344 | bytes 15077380 | tf_op jit(solution)/shard_map/while/body/eval_jaxpr/qhd,khd->hqk/dot_general | solution.py:68
  121.1 3.3 %fusion.56 = bf16[2,512,64]{1,2,0:T(8,128)(2,1)S(1)} fusion(bf16[3072,2,64]{0,2,1:T(8,128)(2,1)S(1)} %get-tuple-element.216, f32[2,512,3072]{2,1,0:T(8,128)S(1)} %get-tuple-element.178, f32[2,512]{1,0:T(2,128)S(1)} %get-tuple-element.179, pred[512,3072]{1,0:T(8,128)(4,1)S(1)} %compare_and_fusion.3), kind=kOutput, calls=%fused_computation.7.clone.1 | convolution fusion | flops 415301632 | bytes 15077376 | tf_op jit(solution)/shard_map/while/body/eval_jaxpr/hqk,khd->qhd/dot_general | solution.py:76
  125.2 3.4 %convolution_convert_fusion.3 = bf16[1024,1280]{1,0:T(8,128)(2,1)} fusion(bf16[1024,128]{1,0:T(8,128)(2,1)} %bitcast.76, bf16[128,1280]{1,0:T(8,128)(2,1)} %param.30), kind=kOutput, calls=%fused_computation.17 | convolution fusion | flops 336855040 | bytes 3211264 | tf_op jit(solution)/shard_map/dot_general | solution.py:184
  128.7 36.6 %reduce-scatter.3.cloned.1.call-done = bf16[128,1280]{1,0:T(8,128)(2,1)} async-done(((bf16[1024,1280]{1,0:T(8,128)(2,1)}), bf16[128,1280]{1,0:T(8,128)(2,1)}) %reduce-scatter.3.cloned.1.call-update) | async-done | bytes 327696 | tf_op jit(solution)/shard_map/reduce_scatter | solution.py:183
  165.4 1.1 fusion.11
  166.5 1.3 multiply_reduce_fusion.1
  167.8 2.1 multiply_convert_fusion.2
  170.0 32.9 %all-gather.8.cloned.1.call-done = bf16[1024,1280]{1,0:T(8,128)(2,1)} async-done(((bf16[128,1280]{1,0:T(8,128)(2,1)}), bf16[1024,1280]{1,0:T(8,128)(2,1)}) %all-gather.8.cloned.1.call-update) | async-done | bytes 2621456 | tf_op jit(solution)/shard_map/all_gather | solution.py:192
  202.9 5.9 %fusion.31 = f32[1024,640]{1,0:T(8,128)} fusion(bf16[1024,1280]{1,0:T(8,128)(2,1)} %all-gather.8.cloned.1.call-done, bf16[1280,640]{1,0:T(8,128)(2,1)} %param.32), kind=kOutput, calls=%fused_computation.110 | convolution fusion | flops 1677721600 | bytes 6881280 | tf_op jit(solution)/shard_map/dot_general | solution.py:86
  208.8 8.4 %convolution_convert_fusion.2 = bf16[1024,1280]{1,0:T(8,128)(2,1)} fusion(bf16[640,1280]{1,0:T(8,128)(2,1)S(1)} %copy-done, f32[1024,640]{1,0:T(8,128)} %fusion.31, bf16[1024,1280]{1,0:T(8,128)(2,1)} %all-gather.8.cloned.1.call-done, bf16[1280,640]{1,0:T(8,128)(2,1)S(1)} %copy-done.14, f32[640]{0:T(1024)S(1)} %copy-done.16, f32[640]{0:T(1024)S(1)} %copy-done.17), kind=kOutput, calls=%fused_computation.16 | convolution fusion | flops 3361996800 | bytes 11146240 | tf_op jit(solution)/shard_map/dot_general | solution.py:199
  217.3 36.7 %reduce-scatter.5.cloned.1.call-done = bf16[128,1280]{1,0:T(8,128)(2,1)} async-done(((bf16[1024,1280]{1,0:T(8,128)(2,1)}), bf16[128,1280]{1,0:T(8,128)(2,1)}) %reduce-scatter.5.cloned.1.call-update) | async-done | bytes 327696 | tf_op jit(solution)/shard_map/reduce_scatter | solution.py:198
  253.9 1.1 fusion.13
  255.1 1.3 multiply_reduce_fusion
  256.4 2.1 multiply_convert_fusion.1
  (112 shorter events, 16.0 us)
Async XLA Ops:
  6.5 202.3 %copy-start = (bf16[640,1280]{1,0:T(8,128)(2,1)S(1)}, bf16[640,1280]{1,0:T(8,128)(2,1)}, u32[]{:S(2)}) copy-start(bf16[640,1280]{1,0:T(8,128)(2,1)} %param.36) | copy-start | bytes 4915204
  6.5 22.6 %copy-start.13 = (s32[1,8]{1,0:T(1,128)S(1)}, s32[1,8]{1,0:T(1,128)}, u32[]{:S(2)}) copy-start(s32[1,8]{1,0:T(1,128)} %param.23) | copy-start | bytes 100
  6.5 23.6 %copy-start.18 = (f32[128]{0:T(128)S(1)}, f32[128]{0:T(128)}, u32[]{:S(2)}) copy-start(f32[128]{0:T(128)} %param.29) | copy-start | bytes 1540
  6.5 23.7 %copy-start.8 = (bf16[4,64,256]{2,1,0:T(8,128)(2,1)S(1)}, bf16[4,64,256]{2,1,0:T(8,128)(2,1)}, u32[]{:S(2)}) copy-start(bf16[4,64,256]{2,1,0:T(8,128)(2,1)} %param.25) | copy-start | bytes 393220
  6.5 49.2 %all-gather.6.cloned.1.call-start = ((), (), s32[]{:S(2)}) async-start(), calls=%async_computation.3 | async-start | bytes 3276800 | tf_op jit(solution)/shard_map/all_gather | solution.py:128
  7.3 83.9 %all-gather.4.cloned.1.call-start = ((), (), s32[]{:S(2)}) async-start(), calls=%async_computation.2 | async-start | bytes 2949120 | tf_op jit(solution)/shard_map/all_gather | solution.py:131
  8.0 157.3 %reduce-scatter.3.cloned.1.call-start = ((), (), s32[]{:S(2)}) async-start(), calls=%async_computation.4 | async-start | bytes 2949120 | tf_op jit(solution)/shard_map/reduce_scatter | solution.py:183
  30.2 3.0 %copy-start.11 = (f32[2,64]{1,0:T(2,128)}, f32[2,64]{1,0:T(2,128)S(1)}, u32[]{:S(2)}) copy-start(f32[2,64]{1,0:T(2,128)S(1)} %mul.265) | copy-start | bytes 1540
  45.9 7.3 %copy-start.19 = (s32[1,8]{1,0:T(1,128)S(1)}, s32[1,8]{1,0:T(1,128)}, u32[]{:S(2)}) copy-start(s32[1,8]{1,0:T(1,128)} %param.21) | copy-start | bytes 100
  69.4 21.7 %copy-start.15 = (bf16[1280,384]{1,0:T(8,128)(2,1)S(1)}, bf16[1280,384]{1,0:T(8,128)(2,1)}, u32[]{:S(2)}) copy-start(bf16[1280,384]{1,0:T(8,128)(2,1)} %param.26) | copy-start | bytes 2949124
  98.7 0.9 copy-start.5
  98.8 1.0 copy-start.6
  98.9 1.2 copy-start.12
  99.0 1.9 copy-start.4
  99.9 1.1 copy-start.3
  100.0 1.1 copy-start.7
  125.2 41.3 %copy-start.2 = (bf16[128,1280]{1,0:T(8,128)(2,1)S(1)}, bf16[128,1280]{1,0:T(8,128)(2,1)}, u32[]{:S(2)}) copy-start(bf16[128,1280]{1,0:T(8,128)(2,1)} %param.20) | copy-start | bytes 983044
  125.2 41.3 %copy-start.9 = (f32[1280]{0:T(1024)S(1)}, f32[1280]{0:T(1024)}, u32[]{:S(2)}) copy-start(f32[1280]{0:T(1024)} %param.31) | copy-start | bytes 15364
  128.7 74.2 %all-gather.8.cloned.1.call-start = ((), (), s32[]{:S(2)}) async-start(), calls=%async_computation.5 | async-start | bytes 2949120 | tf_op jit(solution)/shard_map/all_gather | solution.py:192
  169.9 38.9 %copy-start.14 = (bf16[1280,640]{1,0:T(8,128)(2,1)S(1)}, bf16[1280,640]{1,0:T(8,128)(2,1)}, u32[]{:S(2)}) copy-start(bf16[1280,640]{1,0:T(8,128)(2,1)} %param.33) | copy-start | bytes 4915204
  169.9 38.9 %copy-start.16 = (f32[640]{0:T(1024)S(1)}, f32[640]{0:T(1024)}, u32[]{:S(2)}) copy-start(f32[640]{0:T(1024)} %param.35) | copy-start | bytes 7684
  169.9 38.9 %copy-start.17 = (f32[640]{0:T(1024)S(1)}, f32[640]{0:T(1024)}, u32[]{:S(2)}) copy-start(f32[640]{0:T(1024)} %param.34) | copy-start | bytes 7684
  170.0 84.0 %reduce-scatter.5.cloned.1.call-start = ((), (), s32[]{:S(2)}) async-start(), calls=%async_computation.6 | async-start | bytes 2949120 | tf_op jit(solution)/shard_map/reduce_scatter | solution.py:198
  217.2 37.8 %copy-start.1 = (bf16[128,1280]{1,0:T(8,128)(2,1)S(1)}, bf16[128,1280]{1,0:T(8,128)(2,1)}, u32[]{:S(2)}) copy-start(bf16[128,1280]{1,0:T(8,128)(2,1)} %multiply_convert_fusion.2) | copy-start | bytes 983044
  217.2 37.8 %copy-start.10 = (f32[1280]{0:T(1024)S(1)}, f32[1280]{0:T(1024)}, u32[]{:S(2)}) copy-start(f32[1280]{0:T(1024)} %param.37) | copy-start | bytes 15364
Sparse Core Ops, SparseCore 0:
  9.2 46.3 all-gather.5
  57.2 33.8 all-gather.3
  128.8 36.5 reduce-scatter.2
  170.0 32.8 all-gather.7
  217.4 36.4 reduce-scatter.4
where the time goes:
time: 266 us; the launch traced here: 265 us
  waiting for transfers between devices  124 us (47%)
  matrix products  46.1 us (17%)
  local copies, waits for them, and re-layouts  31 us (12%)
  blocking collectives  29.7 us (11%)
  other arithmetic  19.5 us (7%)
  between operations  13.6 us (5%)
    reduce_scatter x1, waiting for transfers between devices, local(): lax.psum_scatter(jnp.dot(unit_values, down_matrix, preferred_element_type...  36.7 us
    reduce_scatter x1, waiting for transfers between devices, local(): lax.psum_scatter(jnp.dot(attn, output_matrix, preferred_element_type=jnp....  36.6 us
    all_gather x1, waiting for transfers between devices, local(): lax.all_gather(mixed, 'tensor', axis=0, tiled=True)  32.9 us
    all_gather x1, blocking collectives, local(): lax.all_gather(adapter_up, 'dp', axis=0, tiled=True)  17.9 us
    all_gather x1, waiting for transfers between devices, local(): every_row = lax.all_gather(hidden, 'tensor', axis=0, tiled=True)  16 us
    all_gather x1, blocking collectives, local(): all_pages = lax.all_gather(prepared, 'dp', axis=0, tiled=True)  11.8 us
    dot_general x2, matrix products, one_block(): jnp.einsum('qhd,khd->hqk', query_block, key_all, preferred_element_type=j...  10 us
    all_gather x1, local copies, waits for them, and re-layouts, local(): lax.all_gather(adapter_down, 'dp', axis=0, tiled=True)  9.72 us
  transfers between devices with their start and end apart: 5, of which 4 were waited for; matrix products, arithmetic and copies ran while one was open for 14% of the time, Pallas kernels for 0%

commit v1 on v0

--- a/solution.py
+++ b/solution.py
@@ -1,8 +1,11 @@
+import functools
 import math
 
 import jax
 import jax.numpy as jnp
 from jax import lax
+from jax.experimental import pallas as pl
+from jax.experimental.pallas import tpu as pltpu
 from jax.sharding import PartitionSpec as P
 
 MODEL_WIDTH = 1280
@@ -88,7 +91,7 @@
     return (up_part * jax.nn.silu(gate_part)).astype(jnp.bfloat16)
 
 
-def local(
+def local_generic(
     hidden,
     lengths,
     request_prompt,
@@ -207,6 +210,409 @@
     )
 
 
+CHIP_ROWS = 256
+SCORE_LOG2 = math.sqrt(HEAD_WIDTH) / math.log(2.0)
+VMEM = pl.BlockSpec(memory_space=pltpu.VMEM)
+SMEM = pl.BlockSpec(memory_space=pltpu.SMEM)
+BF16 = jnp.bfloat16
+F32 = jnp.float32
+
+
+def call(kernel, outs, operands, scalars, scratch=(), limit=32, flops=10**8, moved=10**6):
+    return pl.pallas_call(
+        kernel,
+        out_shape=outs,
+        in_specs=[SMEM] * scalars + [VMEM] * (len(operands) - scalars),
+        out_specs=jax.tree.map(lambda _: VMEM, outs),
+        scratch_shapes=list(scratch),
+        compiler_params=pltpu.CompilerParams(vmem_limit_bytes=limit * 1024 * 1024),
+        cost_estimate=pl.CostEstimate(flops=flops, bytes_accessed=moved, transcendentals=0),
+    )(*operands)
+
+
+def shape(rows, columns, kind=BF16):
+    return jax.ShapeDtypeStruct((rows, columns), kind)
+
+
+def iota(dims, axis):
+    return lax.broadcasted_iota(jnp.int32, dims, axis)
+
+
+def first_head(rows):
+    return iota((rows, 2 * HEAD_WIDTH), 1) < HEAD_WIDTH
+
+
+def unit_heads(vectors, gain):
+    low = first_head(vectors.shape[0])
+    squares = vectors * vectors
+    sum_low = jnp.sum(jnp.where(low, squares, 0.0), axis=-1, keepdims=True)
+    sum_high = jnp.sum(jnp.where(low, 0.0, squares), axis=-1, keepdims=True)
+    return vectors * lax.rsqrt(jnp.where(low, sum_low, sum_high) + epsilon) * gain
+
+
+def dot(left, right):
+    return jnp.dot(left, right, preferred_element_type=F32)
+
+
+def dot_nt(left, right):
+    return lax.dot_general(
+        left, right, (((1,), (1,)), ((), ())), preferred_element_type=F32
+    )
+
+
+def prepare_kernel(ids, pages, up, down, gain, out):
+    rows = pages.shape[0]
+    low = first_head(rows)
+    left = pages[:, 0:128].astype(F32)
+    right = pages[:, 128:256].astype(F32)
+    keys = jnp.where(low, left, pltpu.roll(right, HEAD_WIDTH, 1))
+    values = jnp.where(low, pltpu.roll(left, HEAD_WIDTH, 1), right)
+    out[0:rows, 0:128] = unit_heads(keys, gain[...]).astype(BF16)
+    out[0:rows, 128:256] = values.astype(BF16)
+    out[0:rows, 256:640] = up[...]
+    row, column = iota((32, 256), 0), iota((32, 256), 1)
+    source = (row // 2) * ADAPTER_RANK + 2 * ids[0] + row % 2
+    picked = dot((column == source).astype(BF16), down[...]).astype(BF16)
+    out[rows : rows + 32, :] = picked[:, 0:640]
+    out[rows + 32 : rows + 64, :] = picked[:, 640:1280]
+
+
+def by_request(index, scalars):
+    picked = jnp.zeros_like(index)
+    for request in range(GROUP_REQUESTS):
+        picked = jnp.where(index == request, scalars[0, request], picked)
+    return picked
+
+
+def select_kernel(ids, adapters, g0, g1, g2, g3, down_out, up_out):
+    tensor, dp = ids[0], ids[1]
+    row, column = iota((16, 32), 0), iota((16, 32), 1)
+    adapter = by_request(row // 2, adapters)
+    source = (adapter % 16) * 2 + row % 2
+    owner = (adapter // 16) ^ dp
+    up_row, up_column = iota((128, 256), 0), iota((128, 256), 1)
+    up_adapter = by_request((up_row % 16) // 2, adapters)
+    up_source = (up_adapter % 16) * 16 + 2 * ((up_row // 16) ^ tensor) + up_row % 2
+    up_owner = (up_adapter // 16) ^ dp
+    left = right = up_total = 0.0
+    for m, g in enumerate((g0, g1, g2, g3)):
+        hot = ((column == source) & (owner == m)).astype(BF16)
+        left = left + dot(hot, g[256:288, :])
+        right = right + dot(hot, g[288:320, :])
+        up_hot = ((up_column == up_source) & (up_owner == m)).astype(BF16)
+        up_total = up_total + dot(up_hot, g[0:256, 256:640])
+    down_out[:, 0:640] = left.astype(BF16)
+    down_out[:, 640:1280] = right.astype(BF16)
+    up_out[...] = up_total.astype(BF16)
+
+
+def qkv_kernel(j, ids, lengths, xa, xb, weight, down, up, cosines, sines, gain, q, k, v):
+    core = ids[0] % 2
+    block = (ids[0] // 2) ^ j
+    rows = jnp.concatenate([xa[...], xb[...]], axis=0)
+    own = pl.multiple_of(core * 128, 128)
+    other = pl.multiple_of((1 - core) * 128, 128)
+    row = iota((CHIP_ROWS, 128), 0)
+    row = block * CHIP_ROWS + jnp.where(row < 128, row + own, row - 128 + other)
+    request = (iota((CHIP_ROWS, 128), 1) % 16) // 2
+    start = jnp.int32(0)
+    first, end = jnp.zeros_like(row), jnp.zeros_like(row)
+    for i in range(GROUP_REQUESTS):
+        first = jnp.where(request == i, start, first)
+        start = start + lengths[0, i]
+        end = jnp.where(request == i, start, end)
+    middle = dot_nt(rows, down[...])
+    middle = jnp.where((row >= first) & (row < end), middle, 0.0).astype(BF16)
+    total = dot(rows, weight[...]) + adapter_scale * dot(middle, up[...])
+    part0, part1, part2 = total[:, 0:128], total[:, 128:256], total[:, 256:384]
+    low = first_head(CHIP_ROWS)
+    query = jnp.where(low, part0, part1)
+    key = pltpu.roll(jnp.where(low, part2, part0), HEAD_WIDTH, 1)
+    value = jnp.where(low, part1, part2).astype(BF16)
+    spots = [
+        pl.multiple_of(block * CHIP_ROWS + own, 128),
+        pl.multiple_of(block * CHIP_ROWS + other, 128),
+    ]
+    cosine = jnp.concatenate([cosines[pl.ds(s, 128), :] for s in spots], axis=0)
+    sine = jnp.concatenate([sines[pl.ds(s, 128), :] for s in spots], axis=0)
+    half = HEAD_WIDTH // 2
+    head_low = (iota((CHIP_ROWS, 128), 1) % HEAD_WIDTH) < half
+
+    def finish(x):
+        turned = jnp.where(head_low, pltpu.roll(x, 128 - half, 1), pltpu.roll(x, half, 1))
+        return unit_heads(x * cosine + turned * sine, gain[...]).astype(BF16)
+
+    for out, result in ((q, finish(query)), (k, finish(key)), (v, value)):
+        out[pl.ds(own, 128), :] = result[0:128]
+        out[pl.ds(other, 128), :] = result[128:256]
+
+
+def attend_kernel(
+    ids, lengths, prompts, table,
+    q0, q1, q2, q3, k0, k1, k2, k3, v0, v1, v2, v3, g0, g1, g2, g3,
+    out, queries, keys, values, pages, starts,
+):
+    chip, dp = ids[0] // 2, ids[1]
+    for target, parts in (
+        (queries, (q0, q1, q2, q3)),
+        (keys, (k0, k1, k2, k3)),
+        (values, (v0, v1, v2, v3)),
+    ):
+        for j, part in enumerate(parts):
+            target[pl.ds(pl.multiple_of((chip ^ j) * CHIP_ROWS, CHIP_ROWS), CHIP_ROWS), :] = part[...]
+    for m, g in enumerate((g0, g1, g2, g3)):
+        pages[pl.ds(pl.multiple_of((dp ^ m) * 256, 256), 256), :] = g[0:256, 0:256]
+    begins = []
+    start = jnp.int32(0)
+    for i in range(GROUP_REQUESTS):
+        starts[i] = start
+        begins.append(start)
+        start = start + lengths[0, i]
+    starts[GROUP_REQUESTS] = start
+    low = first_head(128)
+    tile_row = iota((256, 1), 0) % 128
+
+    def one_tile(tile, carry):
+        base = pl.multiple_of(tile * 128, 128)
+        query = queries[pl.ds(base, 128), :]
+        zero = jnp.zeros_like(query)
+        both = jnp.concatenate(
+            [jnp.where(low, query, zero), jnp.where(low, zero, query)], axis=0
+        )
+        row = base + tile_row
+        row_start = jnp.zeros_like(row)
+        first = jnp.int32(0)
+        last = jnp.int32(0)
+        for i in range(1, GROUP_REQUESTS):
+            row_start = jnp.where(row >= begins[i], begins[i], row_start)
+            first = first + (begins[i] <= base).astype(jnp.int32)
+            last = last + (begins[i] <= base + 127).astype(jnp.int32)
+
+        def add(state, key, value, mask):
+            total, norm = state
+            weights = jnp.where(mask, jnp.exp2(dot_nt(both, key) * SCORE_LOG2), 0.0)
+            return (
+                total + dot(weights.astype(BF16), value),
+                norm + jnp.sum(weights, axis=-1, keepdims=True),
+            )
+
+        def own_block(block, state):
+            spot = pl.multiple_of(block * 128, 128)
+            column = spot + iota((256, 128), 1)
+            mask = (column >= row_start) & (column <= row)
+            return add(state, keys[pl.ds(spot, 128), :], values[pl.ds(spot, 128), :], mask)
+
+        def prefix(request, state):
+            prompt = prompts[0, request]
+            spots = [pl.multiple_of(table[prompt, p] * PAGE, PAGE) for p in range(4)]
+            key = jnp.concatenate([pages[pl.ds(s, PAGE), 0:128] for s in spots], axis=0)
+            value = jnp.concatenate([pages[pl.ds(s, PAGE), 128:256] for s in spots], axis=0)
+            mask = (row >= starts[request]) & (row < starts[request + 1])
+            return add(state, key, value, jnp.broadcast_to(mask, (256, PREFIX_LEN)))
+
+        state = (jnp.zeros((256, 128), F32), jnp.zeros((256, 1), F32))
+        state = prefix(first, state)
+        state = own_block(tile, state)
+        state = lax.fori_loop(starts[first] // 128, tile, own_block, state)
+        total, norm = lax.fori_loop(first + 1, last + 1, prefix, state)
+        total = total / norm
+        out[pl.ds(base, 128), :] = jnp.where(low, total[0:128], total[128:256]).astype(BF16)
+        return carry
+
+    lax.fori_loop(0, out.shape[0] // 128, one_tile, 0)
+
+
+def collect_kernel(ids, o0, o1, o2, o3, p0, p1, p2, p3, out):
+    dp = ids[1]
+    for side, parts in enumerate(((o0, o1, o2, o3), (p0, p1, p2, p3))):
+        for m, part in enumerate(parts):
+            spot = pl.multiple_of((dp ^ m) * 32, 32)
+            for j in range(4):
+                out[2 * j + side, pl.ds(spot, 32), :] = part[j]
+
+
+def mlp_kernel(
+    j, ids, a0, a1, a2, a3, a4, a5, a6, a7, output, xa, xb, rate,
+    up, gate, up_scale, gate_scale, down, keep, send, *rest,
+):
+    result = rest[-1]
+    core = ids[0] % 2
+    spot = pl.multiple_of(((ids[0] // 2) ^ j) * CHIP_ROWS, CHIP_ROWS)
+    heads = jnp.concatenate(
+        [a[pl.ds(spot, CHIP_ROWS), :] for a in (a0, a1, a2, a3, a4, a5, a6, a7)], axis=1
+    )
+    attn_sum = dot(heads, output[...])
+    own = pl.multiple_of(core * 128, 128)
+    other = pl.multiple_of((1 - core) * 128, 128)
+    result[pl.ds(own, 128), :] = xa[...].astype(F32)
+    result[pl.ds(other, 128), :] = xb[...].astype(F32)
+    base = result[...]
+    mixed = renorm(base + rate[...] * (renorm(attn_sum) - base)).astype(BF16)
+    up_part = dot(mixed, up[...]) * up_scale[...]
+    gate_part = dot(mixed, gate[...]) * gate_scale[...]
+    unit_values = (up_part * (gate_part / (1.0 + jnp.exp(-gate_part)))).astype(BF16)
+    if j == 0:
+        result[...] = mixed.astype(F32)
+        rest[0][...] = result[pl.ds(own, 128), :].astype(BF16)
+    result[...] = dot(unit_values, down[...])
+    keep[...] = result[pl.ds(own, 128), :].astype(BF16)
+    send[...] = result[pl.ds(other, 128), :].astype(BF16)
+
+
+def final_kernel(mixed, keep, got, r1, r2, r3, rate, out):
+    mlp_sum = keep[...].astype(F32) + got[...].astype(F32)
+    for r in (r1, r2, r3):
+        mlp_sum = mlp_sum + r[...].astype(F32)
+    base = mixed[...].astype(F32)
+    out[...] = renorm(base + rate[...] * (renorm(mlp_sum) - base)).astype(BF16)
+
+
+def swap(values, distance, axis="tensor"):
+    size = lax.axis_size(axis)
+    return lax.ppermute(values, axis, [(i, i ^ distance) for i in range(size)])
+
+
+def local_pairwise(
+    hidden,
+    lengths,
+    request_prompt,
+    request_adapter,
+    prompt_page_table,
+    prefix_page_cache,
+    query_key_value_weight,
+    adapter_down,
+    adapter_up,
+    attention_scale,
+    output_matrix,
+    attention_rate,
+    up_matrix,
+    gate_matrix,
+    up_scaling,
+    gate_scaling,
+    down_matrix,
+    feedforward_rate,
+):
+    group_rows = hidden.shape[0] * lax.axis_size("tensor")
+    tensor, dp = lax.axis_index("tensor"), lax.axis_index("dp")
+    ids = jnp.stack([tensor, dp]).astype(jnp.int32)
+    gain = attention_scale.reshape(1, -1)
+
+    far = {j: swap(hidden, 2 * j) for j in (2, 3, 1)}
+
+    prepared = call(
+        prepare_kernel,
+        shape(320, 640),
+        (
+            ids,
+            prefix_page_cache.reshape(-1, prefix_page_cache.shape[2]),
+            adapter_up.reshape(-1, adapter_up.shape[2]),
+            jnp.swapaxes(adapter_down, 1, 2).reshape(-1, MODEL_WIDTH),
+            gain,
+        ),
+        1,
+    )
+    shared = [prepared] + [swap(prepared, m, "dp") for m in (1, 2, 3)]
+    down_own, up_all = call(
+        select_kernel, (shape(16, MODEL_WIDTH), shape(128, 384)), (ids, request_adapter, *shared), 2
+    )
+    down_pair = jnp.concatenate([down_own, swap(down_own, 1)], axis=0)
+    down_all = jnp.concatenate([down_pair] + [swap(down_pair, 2 * j) for j in (1, 2, 3)], axis=0)
+
+    row_ids = jnp.arange(group_rows, dtype=jnp.int32)
+    starts = jnp.cumsum(lengths[0]) - lengths[0]
+    row_start = jnp.max(
+        jnp.where(row_ids[:, None] >= starts[None, :], starts[None, :], 0), axis=1
+    )
+    position = (row_ids - row_start).astype(F32) + PREFIX_LEN
+    half = HEAD_WIDTH // 2
+    lanes = jnp.arange(2 * HEAD_WIDTH, dtype=jnp.int32) % HEAD_WIDTH
+    frequency = jnp.exp((lanes % half).astype(F32) * (-2.0 * math.log(10000.0) / HEAD_WIDTH))
+    angles = position[:, None] * frequency[None, :]
+    cosines = jnp.cos(angles)
+    sines = jnp.where(lanes[None, :] < half, -1.0, 1.0) * jnp.sin(angles)
+
+    rows = {0: (hidden, swap(hidden, 1))}
+    for j in (1, 2, 3):
+        rows[j] = (far[j], swap(far[j], 1))
+    query, key, value = {}, {}, {}
+    for j in range(4):
+        query[j], key[j], value[j] = call(
+            functools.partial(qkv_kernel, j),
+            (shape(CHIP_ROWS, 128),) * 3,
+            (ids, lengths, *rows[j], query_key_value_weight, down_all, up_all, cosines, sines, gain),
+            2,
+            flops=4 * 10**8,
+            moved=3 * 10**6,
+        )
+
+    quarter = output_matrix.shape[0] // 4
+    own_quarter = lax.dynamic_slice_in_dim(output_matrix, dp * quarter, quarter, 0)
+    quarters = jnp.stack([own_quarter] + [swap(own_quarter, 2 * j) for j in (1, 2, 3)])
+    blocks = [quarters] + [swap(quarters, m, "dp") for m in (1, 2, 3)]
+    others = [swap(b, 1) for b in blocks]
+    output_all = call(
+        collect_kernel,
+        jax.ShapeDtypeStruct((8, 4 * quarter, MODEL_WIDTH), BF16),
+        (ids, *blocks, *others),
+        1,
+    ).reshape(-1, MODEL_WIDTH)
+
+    attn = call(
+        attend_kernel,
+        shape(group_rows, 128),
+        (
+            ids, lengths, request_prompt, prompt_page_table,
+            *[query[j] for j in range(4)], *[key[j] for j in range(4)],
+            *[value[j] for j in range(4)], *shared,
+        ),
+        4,
+        scratch=(
+            pltpu.VMEM((group_rows, 128), BF16),
+            pltpu.VMEM((group_rows, 128), BF16),
+            pltpu.VMEM((group_rows, 128), BF16),
+            pltpu.VMEM((1024, 256), BF16),
+            pltpu.SMEM((GROUP_REQUESTS + 1,), jnp.int32),
+        ),
+        flops=4 * 10**9,
+        moved=2 * 10**6,
+    )
+
+    heads = {0: (attn, swap(attn, 1))}
+    for j in (2, 3, 1):
+        got = swap(attn, 2 * j)
+        heads[j] = (got, swap(got, 1))
+    all_heads = [heads[j][side] for j in range(4) for side in (0, 1)]
+
+    keep, other = {}, {}
+    for j in (2, 3, 1, 0):
+        outs = (shape(128, MODEL_WIDTH),) * (3 if j == 0 else 2)
+        keep[j], send, *rest = call(
+            functools.partial(mlp_kernel, j),
+            outs,
+            (
+                ids, *all_heads, output_all, *rows[j], attention_rate.reshape(1, -1),
+                up_matrix, gate_matrix, up_scaling.reshape(1, -1), gate_scaling.reshape(1, -1),
+                down_matrix,
+            ),
+            1,
+            scratch=(pltpu.VMEM((CHIP_ROWS, MODEL_WIDTH), F32),),
+            limit=40,
+            flops=2 * 10**9,
+            moved=10**7,
+        )
+        other[j] = swap(send, 1)
+    mixed = rest[0]
+    received = [
+        swap((keep[j].astype(F32) + other[j].astype(F32)).astype(BF16), 2 * j) for j in (2, 3, 1)
+    ]
+    return call(
+        final_kernel,
+        shape(*hidden.shape),
+        (mixed, keep[0], other[0], *received, feedforward_rate.reshape(1, -1)),
+        0,
+    )
+
+
 def solution(mesh):
     placed = (
         P(("dp", "tensor"), None),
@@ -228,6 +634,7 @@
         P("tensor", None),
         P(),
     )
+    pairwise = mesh.shape["dp"] == 4 and mesh.shape["tensor"] == 8
     return jax.shard_map(
-        local, mesh=mesh, in_specs=placed, out_specs=P(("dp", "tensor"), None), check_vma=False
-    )
+        local_pairwise if pairwise else local_generic, mesh=mesh, in_specs=placed, out_specs=P(("dp", "tensor"), None), check_vma=False
+    )

time: 266 us -> 170 us (0.64)
  matrix products: 46.1 us -> 0 us
  waiting for transfers between devices: 124 us -> 83.5 us
  Pallas kernels: 0 us -> 39.3 us
  starting transfers between devices: 0.19 us -> 36.4 us
  blocking collectives: 29.7 us -> 0 us
  local copies, waits for them, and re-layouts: 31 us -> 6.51 us
  other arithmetic: 19.5 us -> 3.86 us
  between operations: 13.6 us -> 0.45 us
    ppermute x0 -> x38, waiting for transfers between devices: none -> 83.5 us  [swap(): return lax.ppermute(values, axis, [(i, i ^ distance) for i in range(size)])]
    reduce_scatter x2 -> x0, waiting for transfers between devices: 73.3 us -> none  [the longest x1 36.7 us: local(): lax.psum_scatter(jnp.dot(unit_values, down_matrix, preferred_element_type...]
    all_gather x3 -> x0, waiting for transfers between devices: 48.8 us -> none  [the longest x1 32.9 us: local(): lax.all_gather(mixed, 'tensor', axis=0, tiled=True)]
    dot_general x11 -> x0, matrix products: 46.1 us -> none  [the longest x2 10 us: one_block(): jnp.einsum('qhd,khd->hqk', query_block, key_all, preferred_element_type=j...]
    pallas_call x0 -> x13, Pallas kernels: none -> 39.3 us  [call(): pl.pallas_call(kernel, out_shape=outs, in_specs=[SMEM] * scalars + [VMEM]...]
    ppermute x0 -> x38, starting transfers between devices: none -> 36.4 us  [swap(): return lax.ppermute(values, axis, [(i, i ^ distance) for i in range(size)])]
    all_gather x2 -> x0, blocking collectives: 29.7 us -> none  [the longest x1 17.9 us: local(): lax.all_gather(adapter_up, 'dp', axis=0, tiled=True)]
    all_gather x1 -> x0, local copies, waits for them, and re-layouts: 9.72 us -> none  [local(): lax.all_gather(adapter_down, 'dp', axis=0, tiled=True)]
  transfers between devices with their start and end apart: 5 -> 38, of which waited for: 4 -> 13; matrix products, arithmetic and copies ran while one was open for 14% -> 3% of each run, Pallas kernels for 0% -> 20%
where the time goes in v1:
time: 170 us
  waiting for transfers between devices  83.5 us (49%)
  Pallas kernels  39.3 us (23%)
  starting transfers between devices  36.4 us (21%)
  local copies, waits for them, and re-layouts  6.51 us (4%)
  other arithmetic  3.86 us (2%)
    ppermute x38, waiting for transfers between devices, swap(): return lax.ppermute(values, axis, [(i, i ^ distance) for i in range(size)])  83.5 us
    pallas_call x13, Pallas kernels, call(): pl.pallas_call(kernel, out_shape=outs, in_specs=[SMEM] * scalars + [VMEM]...  39.3 us
    ppermute x38, starting transfers between devices, swap(): return lax.ppermute(values, axis, [(i, i ^ distance) for i in range(size)])  36.4 us
    unnamed x40, local copies, waits for them, and re-layouts  6.47 us
  transfers between devices with their start and end apart: 38, of which 13 were waited for; matrix products, arithmetic and copies ran while one was open for 3% of the time, Pallas kernels for 20%

profile of v1, /device:TPU:0, one launch (start us, length us, event | category | flops | bytes accessed | tf_op | source)
XLA Modules:
  0.0 170.0 jit_solution(17107759679136876785)
XLA Ops:
  1.0 4.0 %collective-permute-start.22 = (bf16[32,1280]{1,0:T(8,128)(2,1)S(1)}, bf16[32,1280]{1,0:T(8,128)(2,1)S(1)}, u32[]{:S(2)}, u32[]{:S(2)}) collective-permute-start(bf16[32,1280]{1,0:T(8,128)(2,1)S(1)} %constant_dynamic-slice_fusion), channel_id=1, source_target_pairs={{0,4},{1,5},{2,6},{3,7},{4,0},{5,1},{6,2},{7,3},{8,12},{9,13},{10,... | collective-permute-start | bytes 245768 | tf_op jit(solution)/shard_map/ppermute | solution.py:472
  5.0 1.3 collective-permute-start.23
  10.8 1.6 collective-permute-start.1
  12.4 1.5 collective-permute-start.2
  16.7 1.9 %fusion = (f32[1024,128]{1,0:T(8,128)S(1)}, f32[1024,128]{1,0:T(8,128)S(1)}) fusion(f32[128]{0:T(128)S(1)} %get-tuple-element.57, f32[128]{0:T(128)S(1)} %get-tuple-element.58, f32[1024]{0:T(1024)S(1)} %convert_add_fusion), kind=kLoop, calls=%fused_computation.5 | loop fusion | flops 262144 | bytes 1053696 | tf_op jit(solution)/shard_map/mul | solution.py:532
  18.7 4.6 %collective-permute-done.1.g1 = bf16[320,640]{1,0:T(8,128)(2,1)S(1)} collective-permute-done((bf16[320,640]{1,0:T(8,128)(2,1)S(1)}, bf16[320,640]{1,0:T(8,128)(2,1)S(1)}, u32[]{:S(2)}, u32[]{:S(2)}) %collective-permute-start.1) | collective-permute-done | bytes 409632 | tf_op jit(solution)/shard_map/ppermute | solution.py:472
  23.5 8.0 %collective-permute-done.2.g2 = bf16[320,640]{1,0:T(8,128)(2,1)S(1)} collective-permute-done((bf16[320,640]{1,0:T(8,128)(2,1)S(1)}, bf16[320,640]{1,0:T(8,128)(2,1)S(1)}, u32[]{:S(2)}, u32[]{:S(2)}) %collective-permute-start.2) | collective-permute-done | bytes 409632 | tf_op jit(solution)/shard_map/ppermute | solution.py:472
  31.5 2.5 %collective-permute-start.12 = (bf16[128,1280]{1,0:T(8,128)(2,1)S(1)}, bf16[128,1280]{1,0:T(8,128)(2,1)S(1)}, u32[]{:S(2)}, u32[]{:S(2)}) collective-permute-start(bf16[128,1280]{1,0:T(8,128)(2,1)S(1)} %copy-done.5), channel_id=1, source_target_pairs={{0,6},{1,7},{2,4},{3,5},{4,2},{5,3},{6,0},{7,1},{8,14},{9,15},{10,... | collective-permute-start | bytes 983048 | tf_op jit(solution)/shard_map/ppermute | solution.py:472
  36.3 2.0 %collective-permute-start.8 = (bf16[128,1280]{1,0:T(8,128)(2,1)S(1)}, bf16[128,1280]{1,0:T(8,128)(2,1)S(1)}, u32[]{:S(2)}, u32[]{:S(2)}) collective-permute-start(bf16[128,1280]{1,0:T(8,128)(2,1)S(1)} %copy-done.5), channel_id=1, source_target_pairs={{0,2},{1,3},{2,0},{3,1},{4,6},{5,7},{6,4},{7,5},{8,10},{9,11},{10,... | collective-permute-start | bytes 983048 | tf_op jit(solution)/shard_map/ppermute | solution.py:472
  38.5 17.8 %collective-permute-done.5 = bf16[32,1280]{1,0:T(8,128)(2,1)S(1)} collective-permute-done((bf16[32,1280]{1,0:T(8,128)(2,1)S(1)}, bf16[32,1280]{1,0:T(8,128)(2,1)S(1)}, u32[]{:S(2)}, u32[]{:S(2)}) %collective-permute-start.5) | collective-permute-done | bytes 81952 | tf_op jit(solution)/shard_map/ppermute | solution.py:472
  56.9 2.0 %collective-permute-start.25 = (bf16[4,32,1280]{2,1,0:T(8,128)(2,1)S(1)}, bf16[4,32,1280]{2,1,0:T(8,128)(2,1)S(1)}, u32[]{:S(2)}, u32[]{:S(2)}) collective-permute-start(bf16[4,32,1280]{2,1,0:T(8,128)(2,1)S(1)} %pad_maximum_fusion.o0), channel_id=1, source_target_pairs={{0,16},{8,24},{16,0},{24,8},{1,17},{9,25},{17,1},{25,9},{2,18},{10... | collective-permute-start | bytes 983048 | tf_op jit(solution)/shard_map/ppermute | solution.py:472
  59.5 3.1 %collective-permute-done.6 = bf16[32,1280]{1,0:T(8,128)(2,1)S(1)} collective-permute-done((bf16[32,1280]{1,0:T(8,128)(2,1)S(1)}, bf16[32,1280]{1,0:T(8,128)(2,1)S(1)}, u32[]{:S(2)}, u32[]{:S(2)}) %collective-permute-start.6) | collective-permute-done | bytes 81952 | tf_op jit(solution)/shard_map/ppermute | solution.py:472
  62.5 2.6 %collective-permute-start.7 = (bf16[32,1280]{1,0:T(8,128)(2,1)S(1)}, bf16[32,1280]{1,0:T(8,128)(2,1)S(1)}, u32[]{:S(2)}, u32[]{:S(2)}) collective-permute-start(bf16[32,1280]{1,0:T(8,128)(2,1)S(1)} %get-tuple-element.51), channel_id=1, source_target_pairs={{0,6},{1,7},{2,4},{3,5},{4,2},{5,3},{6,0},{7,1},{8,14},{9,15},{10,... | collective-permute-start | bytes 245768 | tf_op jit(solution)/shard_map/ppermute | solution.py:472
  65.1 3.7 %collective-permute-done.7 = bf16[32,1280]{1,0:T(8,128)(2,1)S(1)} collective-permute-done((bf16[32,1280]{1,0:T(8,128)(2,1)S(1)}, bf16[32,1280]{1,0:T(8,128)(2,1)S(1)}, u32[]{:S(2)}, u32[]{:S(2)}) %collective-permute-start.7) | collective-permute-done | bytes 81952 | tf_op jit(solution)/shard_map/ppermute | solution.py:472
  68.8 2.0 %shard_map.174 = (bf16[256,128]{1,0:T(8,128)(2,1)S(1)}, bf16[256,128]{1,0:T(8,128)(2,1)S(1)}, bf16[256,128]{1,0:T(8,128)(2,1)S(1)}) custom-call(s32[2]{0:T(128)S(1)} %pad_add_fusion.ids, s32[1,8]{1,0:T(1,128)S(1)} %copy-done.11, bf16[128,1280]{1,0:T(8,128)(2,1)S(1)} %copy-done.5, bf16[128,1280]{1,0:T(8,128)(2,1)S(1)} %collective-permute-done.xb, ...), custom_call_target="tpu_custom_call" | custom-call | flops 400000000 | bytes 3000000 | tf_op jit(solution)/shard_map/pallas_call | solution.py:222
  70.8 1.6 collective-permute-start.26
  72.4 2.0 %shard_map.177 = (bf16[256,128]{1,0:T(8,128)(2,1)S(1)}, bf16[256,128]{1,0:T(8,128)(2,1)S(1)}, bf16[256,128]{1,0:T(8,128)(2,1)S(1)}) custom-call(s32[2]{0:T(128)S(1)} %pad_add_fusion.ids, s32[1,8]{1,0:T(1,128)S(1)} %copy-done.11, bf16[128,1280]{1,0:T(8,128)(2,1)S(1)} %collective-permute-done.12.xa, bf16[128,1280]{1,0:T(8,128)(2,1)S(1)} %collective-permute-done.13.xb, ...), custom_call_target="tpu_custom_call" | custom-call | flops 400000000 | bytes 3000000 | tf_op jit(solution)/shard_map/pallas_call | solution.py:222
  75.2 2.0 %shard_map.176 = (bf16[256,128]{1,0:T(8,128)(2,1)S(1)}, bf16[256,128]{1,0:T(8,128)(2,1)S(1)}, bf16[256,128]{1,0:T(8,128)(2,1)S(1)}) custom-call(s32[2]{0:T(128)S(1)} %pad_add_fusion.ids, s32[1,8]{1,0:T(1,128)S(1)} %copy-done.11, bf16[128,1280]{1,0:T(8,128)(2,1)S(1)} %collective-permute-done.10.xa, bf16[128,1280]{1,0:T(8,128)(2,1)S(1)} %collective-permute-done.11.xb, ...), custom_call_target="tpu_custom_call" | custom-call | flops 400000000 | bytes 3000000 | tf_op jit(solution)/shard_map/pallas_call | solution.py:222
  77.3 2.0 %shard_map.175 = (bf16[256,128]{1,0:T(8,128)(2,1)S(1)}, bf16[256,128]{1,0:T(8,128)(2,1)S(1)}, bf16[256,128]{1,0:T(8,128)(2,1)S(1)}) custom-call(s32[2]{0:T(128)S(1)} %pad_add_fusion.ids, s32[1,8]{1,0:T(1,128)S(1)} %copy-done.11, bf16[128,1280]{1,0:T(8,128)(2,1)S(1)} %collective-permute-done.8.xa, bf16[128,1280]{1,0:T(8,128)(2,1)S(1)} %collective-permute-done.9.xb, ...), custom_call_target="tpu_custom_call" | custom-call | flops 400000000 | bytes 3000000 | tf_op jit(solution)/shard_map/pallas_call | solution.py:222
  79.3 11.6 %shard_map.178.a0 = bf16[1024,128]{1,0:T(8,128)(2,1)S(1)} custom-call(s32[2]{0:T(128)S(1)} %pad_add_fusion.ids, s32[1,8]{1,0:T(1,128)S(1)} %copy-done.11, s32[1,8]{1,0:T(1,128)S(1)} %copy-done.13, s32[32,4]{1,0:T(8,128)S(1)} %copy.20.table, bf16[256,128]{1,0:T(8,128)(2,1)S(1)} %get-tuple-element.30.q0, bf16[256,128]{1,0:T(8,128)(2,1)S(1)} %get-tuple-element.31.q1, ...), custom_call_target="tpu_custom_call" | custom-call | flops 4000000000 | bytes 2000000 | tf_op jit(solution)/shard_map/pallas_call | solution.py:222
  91.0 3.1 %collective-permute-start.17 = (bf16[1024,128]{1,0:T(8,128)(2,1)S(1)}, bf16[1024,128]{1,0:T(8,128)(2,1)S(1)}, u32[]{:S(2)}, u32[]{:S(2)}) collective-permute-start(bf16[1024,128]{1,0:T(8,128)(2,1)S(1)} %shard_map.178.a0), channel_id=1, source_target_pairs={{0,4},{1,5},{2,6},{3,7},{4,0},{5,1},{6,2},{7,3},{8,12},{9,13},{10,... | collective-permute-start | bytes 786440 | tf_op jit(solution)/shard_map/ppermute | solution.py:472
  95.9 8.8 %collective-permute-done.15.a2 = bf16[1024,128]{1,0:T(8,128)(2,1)S(1)} collective-permute-done((bf16[1024,128]{1,0:T(8,128)(2,1)S(1)}, bf16[1024,128]{1,0:T(8,128)(2,1)S(1)}, u32[]{:S(2)}, u32[]{:S(2)}) %collective-permute-start.15) | collective-permute-done | bytes 262176 | tf_op jit(solution)/shard_map/ppermute | solution.py:472
  104.7 7.8 %collective-permute-done.17.a4 = bf16[1024,128]{1,0:T(8,128)(2,1)S(1)} collective-permute-done((bf16[1024,128]{1,0:T(8,128)(2,1)S(1)}, bf16[1024,128]{1,0:T(8,128)(2,1)S(1)}, u32[]{:S(2)}, u32[]{:S(2)}) %collective-permute-start.17) | collective-permute-done | bytes 262176 | tf_op jit(solution)/shard_map/ppermute | solution.py:472
  115.5 3.9 %shard_map.183 = (bf16[128,1280]{1,0:T(8,128)(2,1)S(1)}, bf16[128,1280]{1,0:T(8,128)(2,1)S(1)}) custom-call(s32[2]{0:T(128)S(1)} %pad_add_fusion.ids, bf16[1024,128]{1,0:T(8,128)(2,1)S(1)} %shard_map.178.a0, bf16[1024,128]{1,0:T(8,128)(2,1)S(1)} %collective-permute-done.14.a1, bf16[1024,128]{1,0:T(8,128)(2,1)S(1)} %collective-permute-done.15.a2, ...), custom_call_target="tpu_custom_call" | custom-call | flops 2000000000 | bytes 10000000 | tf_op jit(solution)/shard_map/pallas_call | solution.py:222
  119.5 3.9 %shard_map.182 = (bf16[128,1280]{1,0:T(8,128)(2,1)S(1)}, bf16[128,1280]{1,0:T(8,128)(2,1)S(1)}) custom-call(s32[2]{0:T(128)S(1)} %pad_add_fusion.ids, bf16[1024,128]{1,0:T(8,128)(2,1)S(1)} %shard_map.178.a0, bf16[1024,128]{1,0:T(8,128)(2,1)S(1)} %collective-permute-done.14.a1, bf16[1024,128]{1,0:T(8,128)(2,1)S(1)} %collective-permute-done.15.a2, ...), custom_call_target="tpu_custom_call" | custom-call | flops 2000000000 | bytes 10000000 | tf_op jit(solution)/shard_map/pallas_call | solution.py:222
  124.1 3.9 %shard_map.181 = (bf16[128,1280]{1,0:T(8,128)(2,1)S(1)}, bf16[128,1280]{1,0:T(8,128)(2,1)S(1)}) custom-call(s32[2]{0:T(128)S(1)} %pad_add_fusion.ids, bf16[1024,128]{1,0:T(8,128)(2,1)S(1)} %shard_map.178.a0, bf16[1024,128]{1,0:T(8,128)(2,1)S(1)} %collective-permute-done.14.a1, bf16[1024,128]{1,0:T(8,128)(2,1)S(1)} %collective-permute-done.15.a2, ...), custom_call_target="tpu_custom_call" | custom-call | flops 2000000000 | bytes 10000000 | tf_op jit(solution)/shard_map/pallas_call | solution.py:222
  128.1 4.1 %shard_map.180 = (bf16[128,1280]{1,0:T(8,128)(2,1)S(1)}, bf16[128,1280]{1,0:T(8,128)(2,1)S(1)}, bf16[128,1280]{1,0:T(8,128)(2,1)S(1)}) custom-call(s32[2]{0:T(128)S(1)} %pad_add_fusion.ids, bf16[1024,128]{1,0:T(8,128)(2,1)S(1)} %shard_map.178.a0, bf16[1024,128]{1,0:T(8,128)(2,1)S(1)} %collective-permute-done.14.a1, ...), custom_call_target="tpu_custom_call" | custom-call | flops 2000000000 | bytes 10000000 | tf_op jit(solution)/shard_map/pallas_call | solution.py:222
  132.8 5.2 %collective-permute-start.37 = (bf16[128,1280]{1,0:T(8,128)(2,1)S(1)}, bf16[128,1280]{1,0:T(8,128)(2,1)S(1)}, u32[]{:S(2)}, u32[]{:S(2)}) collective-permute-start(bf16[128,1280]{1,0:T(8,128)(2,1)S(1)} %add_convert_fusion), channel_id=1, source_target_pairs={{0,2},{1,3},{2,0},{3,1},{4,6},{5,7},{6,4},{7,5},{8,10},{9,11},{10,... | collective-permute-start | bytes 983048 | tf_op jit(solution)/shard_map/ppermute | solution.py:472
  138.1 2.5 %collective-permute-start.35 = (bf16[128,1280]{1,0:T(8,128)(2,1)S(1)}, bf16[128,1280]{1,0:T(8,128)(2,1)S(1)}, u32[]{:S(2)}, u32[]{:S(2)}) collective-permute-start(bf16[128,1280]{1,0:T(8,128)(2,1)S(1)} %add_convert_fusion.1), channel_id=1, source_target_pairs={{0,6},{1,7},{2,4},{3,5},{4,2},{5,3},{6,0},{7,1},{8,14},{9,15},{10,... | collective-permute-start | bytes 983048 | tf_op jit(solution)/shard_map/ppermute | solution.py:472
  140.8 5.6 %collective-permute-done.37.r3 = bf16[128,1280]{1,0:T(8,128)(2,1)S(1)} collective-permute-done((bf16[128,1280]{1,0:T(8,128)(2,1)S(1)}, bf16[128,1280]{1,0:T(8,128)(2,1)S(1)}, u32[]{:S(2)}, u32[]{:S(2)}) %collective-permute-start.37) | collective-permute-done | bytes 327712 | tf_op jit(solution)/shard_map/ppermute | solution.py:472
  146.3 9.7 %collective-permute-done.35.r2 = bf16[128,1280]{1,0:T(8,128)(2,1)S(1)} collective-permute-done((bf16[128,1280]{1,0:T(8,128)(2,1)S(1)}, bf16[128,1280]{1,0:T(8,128)(2,1)S(1)}, u32[]{:S(2)}, u32[]{:S(2)}) %collective-permute-start.35) | collective-permute-done | bytes 327712 | tf_op jit(solution)/shard_map/ppermute | solution.py:472
  156.1 12.7 %collective-permute-done.33.r1 = bf16[128,1280]{1,0:T(8,128)(2,1)S(1)} collective-permute-done((bf16[128,1280]{1,0:T(8,128)(2,1)S(1)}, bf16[128,1280]{1,0:T(8,128)(2,1)S(1)}, u32[]{:S(2)}, u32[]{:S(2)}) %collective-permute-start.33) | collective-permute-done | bytes 327712 | tf_op jit(solution)/shard_map/ppermute | solution.py:472
  (116 shorter events, 20.5 us)
Async XLA Ops:
  1.0 35.3 %collective-permute-start.22 = (bf16[32,1280]{1,0:T(8,128)(2,1)S(1)}, bf16[32,1280]{1,0:T(8,128)(2,1)S(1)}, u32[]{:S(2)}, u32[]{:S(2)}) collective-permute-start(bf16[32,1280]{1,0:T(8,128)(2,1)S(1)} %constant_dynamic-slice_fusion), channel_id=1, source_target_pairs={{0,4},{1,5},{2,6},{3,7},{4,0},{5,1},{6,2},{7,3},{8,12},{9,13},{10,... | collective-permute-start | bytes 245768 | tf_op jit(solution)/shard_map/ppermute | solution.py:472
  5.0 33.3 %collective-permute-start.23 = (bf16[32,1280]{1,0:T(8,128)(2,1)S(1)}, bf16[32,1280]{1,0:T(8,128)(2,1)S(1)}, u32[]{:S(2)}, u32[]{:S(2)}) collective-permute-start(bf16[32,1280]{1,0:T(8,128)(2,1)S(1)} %constant_dynamic-slice_fusion), channel_id=1, source_target_pairs={{0,6},{1,7},{2,4},{3,5},{4,2},{5,3},{6,0},{7,1},{8,14},{9,15},{10,... | collective-permute-start | bytes 245768 | tf_op jit(solution)/shard_map/ppermute | solution.py:472
  10.8 12.5 %collective-permute-start.1 = (bf16[320,640]{1,0:T(8,128)(2,1)S(1)}, bf16[320,640]{1,0:T(8,128)(2,1)S(1)}, u32[]{:S(2)}, u32[]{:S(2)}) collective-permute-start(bf16[320,640]{1,0:T(8,128)(2,1)S(1)} %shard_map.172.g0), channel_id=1, source_target_pairs={{0,8},{8,0},{16,24},{24,16},{1,9},{9,1},{17,25},{25,17},{2,10},{10... | collective-permute-start | bytes 1228808 | tf_op jit(solution)/shard_map/ppermute | solution.py:472
  12.4 19.2 %collective-permute-start.2 = (bf16[320,640]{1,0:T(8,128)(2,1)S(1)}, bf16[320,640]{1,0:T(8,128)(2,1)S(1)}, u32[]{:S(2)}, u32[]{:S(2)}) collective-permute-start(bf16[320,640]{1,0:T(8,128)(2,1)S(1)} %shard_map.172.g0), channel_id=1, source_target_pairs={{0,16},{8,24},{16,0},{24,8},{1,17},{9,25},{17,1},{25,9},{2,18},{10... | collective-permute-start | bytes 1228808 | tf_op jit(solution)/shard_map/ppermute | solution.py:472
  13.9 20.1 %collective-permute-start.3 = (bf16[320,640]{1,0:T(8,128)(2,1)S(1)}, bf16[320,640]{1,0:T(8,128)(2,1)S(1)}, u32[]{:S(2)}, u32[]{:S(2)}) collective-permute-start(bf16[320,640]{1,0:T(8,128)(2,1)S(1)} %shard_map.172.g0), channel_id=1, source_target_pairs={{0,24},{8,16},{16,8},{24,0},{1,25},{9,17},{17,9},{25,1},{2,26},{10... | collective-permute-start | bytes 1228808 | tf_op jit(solution)/shard_map/ppermute | solution.py:472
  23.3 15.0 %collective-permute-start.21 = (bf16[32,1280]{1,0:T(8,128)(2,1)S(1)}, bf16[32,1280]{1,0:T(8,128)(2,1)S(1)}, u32[]{:S(2)}, u32[]{:S(2)}) collective-permute-start(bf16[32,1280]{1,0:T(8,128)(2,1)S(1)} %constant_dynamic-slice_fusion), channel_id=1, source_target_pairs={{0,2},{1,3},{2,0},{3,1},{4,6},{5,7},{6,4},{7,5},{8,10},{9,11},{10,... | collective-permute-start | bytes 245768 | tf_op jit(solution)/shard_map/ppermute | solution.py:472
  31.5 25.3 %collective-permute-start.12 = (bf16[128,1280]{1,0:T(8,128)(2,1)S(1)}, bf16[128,1280]{1,0:T(8,128)(2,1)S(1)}, u32[]{:S(2)}, u32[]{:S(2)}) collective-permute-start(bf16[128,1280]{1,0:T(8,128)(2,1)S(1)} %copy-done.5), channel_id=1, source_target_pairs={{0,6},{1,7},{2,4},{3,5},{4,2},{5,3},{6,0},{7,1},{8,14},{9,15},{10,... | collective-permute-start | bytes 983048 | tf_op jit(solution)/shard_map/ppermute | solution.py:472
  36.3 20.6 %collective-permute-start.10 = (bf16[128,1280]{1,0:T(8,128)(2,1)S(1)}, bf16[128,1280]{1,0:T(8,128)(2,1)S(1)}, u32[]{:S(2)}, u32[]{:S(2)}) collective-permute-start(bf16[128,1280]{1,0:T(8,128)(2,1)S(1)} %copy-done.5), channel_id=1, source_target_pairs={{0,4},{1,5},{2,6},{3,7},{4,0},{5,1},{6,2},{7,3},{8,12},{9,13},{10,... | collective-permute-start | bytes 983048 | tf_op jit(solution)/shard_map/ppermute | solution.py:472
  36.3 22.6 %collective-permute-start.8 = (bf16[128,1280]{1,0:T(8,128)(2,1)S(1)}, bf16[128,1280]{1,0:T(8,128)(2,1)S(1)}, u32[]{:S(2)}, u32[]{:S(2)}) collective-permute-start(bf16[128,1280]{1,0:T(8,128)(2,1)S(1)} %copy-done.5), channel_id=1, source_target_pairs={{0,2},{1,3},{2,0},{3,1},{4,6},{5,7},{6,4},{7,5},{8,10},{9,11},{10,... | collective-permute-start | bytes 983048 | tf_op jit(solution)/shard_map/ppermute | solution.py:472
  38.3 20.6 %collective-permute-start = (bf16[128,1280]{1,0:T(8,128)(2,1)S(1)}, bf16[128,1280]{1,0:T(8,128)(2,1)S(1)}, u32[]{:S(2)}, u32[]{:S(2)}) collective-permute-start(bf16[128,1280]{1,0:T(8,128)(2,1)S(1)} %copy-done.5), channel_id=1, source_target_pairs={{0,1},{1,0},{2,3},{3,2},{4,5},{5,4},{6,7},{7,6},{8,9},{9,8},{10,11... | collective-permute-start | bytes 983048 | tf_op jit(solution)/shard_map/ppermute | solution.py:472
  38.3 18.0 %collective-permute-start.5 = (bf16[32,1280]{1,0:T(8,128)(2,1)S(1)}, bf16[32,1280]{1,0:T(8,128)(2,1)S(1)}, u32[]{:S(2)}, u32[]{:S(2)}) collective-permute-start(bf16[32,1280]{1,0:T(8,128)(2,1)S(1)} %get-tuple-element.51), channel_id=1, source_target_pairs={{0,2},{1,3},{2,0},{3,1},{4,6},{5,7},{6,4},{7,5},{8,10},{9,11},{10,... | collective-permute-start | bytes 245768 | tf_op jit(solution)/shard_map/ppermute | solution.py:472
  56.8 17.6 %collective-permute-start.24 = (bf16[4,32,1280]{2,1,0:T(8,128)(2,1)S(1)}, bf16[4,32,1280]{2,1,0:T(8,128)(2,1)S(1)}, u32[]{:S(2)}, u32[]{:S(2)}) collective-permute-start(bf16[4,32,1280]{2,1,0:T(8,128)(2,1)S(1)} %pad_maximum_fusion.o0), channel_id=1, source_target_pairs={{0,8},{8,0},{16,24},{24,16},{1,9},{9,1},{17,25},{25,17},{2,10},{10... | collective-permute-start | bytes 983048 | tf_op jit(solution)/shard_map/ppermute | solution.py:472
  56.9 17.8 %collective-permute-start.25 = (bf16[4,32,1280]{2,1,0:T(8,128)(2,1)S(1)}, bf16[4,32,1280]{2,1,0:T(8,128)(2,1)S(1)}, u32[]{:S(2)}, u32[]{:S(2)}) collective-permute-start(bf16[4,32,1280]{2,1,0:T(8,128)(2,1)S(1)} %pad_maximum_fusion.o0), channel_id=1, source_target_pairs={{0,16},{8,24},{16,0},{24,8},{1,17},{9,25},{17,1},{25,9},{2,18},{10... | collective-permute-start | bytes 983048 | tf_op jit(solution)/shard_map/ppermute | solution.py:472
  59.0 11.9 %collective-permute-start.13 = (bf16[128,1280]{1,0:T(8,128)(2,1)S(1)}, bf16[128,1280]{1,0:T(8,128)(2,1)S(1)}, u32[]{:S(2)}, u32[]{:S(2)}) collective-permute-start(bf16[128,1280]{1,0:T(8,128)(2,1)S(1)} %collective-permute-done.12.xa), channel_id=1, source_target_pairs={{0,1},{1,0},{2,3},{3,2},{4,5},{5,4},{6,7},{7,6},{8,9},{9,8},{10,11... | collective-permute-start | bytes 983048 | tf_op jit(solution)/shard_map/ppermute | solution.py:472
  59.0 16.0 %collective-permute-start.11 = (bf16[128,1280]{1,0:T(8,128)(2,1)S(1)}, bf16[128,1280]{1,0:T(8,128)(2,1)S(1)}, u32[]{:S(2)}, u32[]{:S(2)}) collective-permute-start(bf16[128,1280]{1,0:T(8,128)(2,1)S(1)} %collective-permute-done.10.xa), channel_id=1, source_target_pairs={{0,1},{1,0},{2,3},{3,2},{4,5},{5,4},{6,7},{7,6},{8,9},{9,8},{10,11... | collective-permute-start | bytes 983048 | tf_op jit(solution)/shard_map/ppermute | solution.py:472
  70.8 20.2 %collective-permute-start.26 = (bf16[4,32,1280]{2,1,0:T(8,128)(2,1)S(1)}, bf16[4,32,1280]{2,1,0:T(8,128)(2,1)S(1)}, u32[]{:S(2)}, u32[]{:S(2)}) collective-permute-start(bf16[4,32,1280]{2,1,0:T(8,128)(2,1)S(1)} %pad_maximum_fusion.o0), channel_id=1, source_target_pairs={{0,24},{8,16},{16,8},{24,0},{1,25},{9,17},{17,9},{25,1},{2,26},{10... | collective-permute-start | bytes 983048 | tf_op jit(solution)/shard_map/ppermute | solution.py:472
  74.4 19.7 %collective-permute-start.27 = (bf16[4,32,1280]{2,1,0:T(8,128)(2,1)S(1)}, bf16[4,32,1280]{2,1,0:T(8,128)(2,1)S(1)}, u32[]{:S(2)}, u32[]{:S(2)}) collective-permute-start(bf16[4,32,1280]{2,1,0:T(8,128)(2,1)S(1)} %pad_maximum_fusion.o0), channel_id=1, source_target_pairs={{0,1},{1,0},{2,3},{3,2},{4,5},{5,4},{6,7},{7,6},{8,9},{9,8},{10,11... | collective-permute-start | bytes 983048 | tf_op jit(solution)/shard_map/ppermute | solution.py:472
  74.7 20.7 %collective-permute-start.28 = (bf16[4,32,1280]{2,1,0:T(8,128)(2,1)S(1)}, bf16[4,32,1280]{2,1,0:T(8,128)(2,1)S(1)}, u32[]{:S(2)}, u32[]{:S(2)}) collective-permute-start(bf16[4,32,1280]{2,1,0:T(8,128)(2,1)S(1)} %collective-permute-done.24.o1), channel_id=1, source_target_pairs={{0,1},{1,0},{2,3},{3,2},{4,5},{5,4},{6,7},{7,6},{8,9},{9,8},{10,11... | collective-permute-start | bytes 983048 | tf_op jit(solution)/shard_map/ppermute | solution.py:472
  75.0 20.4 %collective-permute-start.29 = (bf16[4,32,1280]{2,1,0:T(8,128)(2,1)S(1)}, bf16[4,32,1280]{2,1,0:T(8,128)(2,1)S(1)}, u32[]{:S(2)}, u32[]{:S(2)}) collective-permute-start(bf16[4,32,1280]{2,1,0:T(8,128)(2,1)S(1)} %collective-permute-done.25.o2), channel_id=1, source_target_pairs={{0,1},{1,0},{2,3},{3,2},{4,5},{5,4},{6,7},{7,6},{8,9},{9,8},{10,11... | collective-permute-start | bytes 983048 | tf_op jit(solution)/shard_map/ppermute | solution.py:472
  90.9 13.8 %collective-permute-start.15 = (bf16[1024,128]{1,0:T(8,128)(2,1)S(1)}, bf16[1024,128]{1,0:T(8,128)(2,1)S(1)}, u32[]{:S(2)}, u32[]{:S(2)}) collective-permute-start(bf16[1024,128]{1,0:T(8,128)(2,1)S(1)} %shard_map.178.a0), channel_id=1, source_target_pairs={{0,2},{1,3},{2,0},{3,1},{4,6},{5,7},{6,4},{7,5},{8,10},{9,11},{10,... | collective-permute-start | bytes 786440 | tf_op jit(solution)/shard_map/ppermute | solution.py:472
  91.0 21.5 %collective-permute-start.17 = (bf16[1024,128]{1,0:T(8,128)(2,1)S(1)}, bf16[1024,128]{1,0:T(8,128)(2,1)S(1)}, u32[]{:S(2)}, u32[]{:S(2)}) collective-permute-start(bf16[1024,128]{1,0:T(8,128)(2,1)S(1)} %shard_map.178.a0), channel_id=1, source_target_pairs={{0,4},{1,5},{2,6},{3,7},{4,0},{5,1},{6,2},{7,3},{8,12},{9,13},{10,... | collective-permute-start | bytes 786440 | tf_op jit(solution)/shard_map/ppermute | solution.py:472
  94.1 18.4 %collective-permute-start.19 = (bf16[1024,128]{1,0:T(8,128)(2,1)S(1)}, bf16[1024,128]{1,0:T(8,128)(2,1)S(1)}, u32[]{:S(2)}, u32[]{:S(2)}) collective-permute-start(bf16[1024,128]{1,0:T(8,128)(2,1)S(1)} %shard_map.178.a0), channel_id=1, source_target_pairs={{0,6},{1,7},{2,4},{3,5},{4,2},{5,3},{6,0},{7,1},{8,14},{9,15},{10,... | collective-permute-start | bytes 786440 | tf_op jit(solution)/shard_map/ppermute | solution.py:472
  95.4 17.7 %collective-permute-start.30 = (bf16[4,32,1280]{2,1,0:T(8,128)(2,1)S(1)}, bf16[4,32,1280]{2,1,0:T(8,128)(2,1)S(1)}, u32[]{:S(2)}, u32[]{:S(2)}) collective-permute-start(bf16[4,32,1280]{2,1,0:T(8,128)(2,1)S(1)} %collective-permute-done.26.o3), channel_id=1, source_target_pairs={{0,1},{1,0},{2,3},{3,2},{4,5},{5,4},{6,7},{7,6},{8,9},{9,8},{10,11... | collective-permute-start | bytes 983048 | tf_op jit(solution)/shard_map/ppermute | solution.py:472
  95.4 18.5 %collective-permute-start.14 = (bf16[1024,128]{1,0:T(8,128)(2,1)S(1)}, bf16[1024,128]{1,0:T(8,128)(2,1)S(1)}, u32[]{:S(2)}, u32[]{:S(2)}) collective-permute-start(bf16[1024,128]{1,0:T(8,128)(2,1)S(1)} %shard_map.178.a0), channel_id=1, source_target_pairs={{0,1},{1,0},{2,3},{3,2},{4,5},{5,4},{6,7},{7,6},{8,9},{9,8},{10,11... | collective-permute-start | bytes 786440 | tf_op jit(solution)/shard_map/ppermute | solution.py:472
  104.7 9.2 %collective-permute-start.16 = (bf16[1024,128]{1,0:T(8,128)(2,1)S(1)}, bf16[1024,128]{1,0:T(8,128)(2,1)S(1)}, u32[]{:S(2)}, u32[]{:S(2)}) collective-permute-start(bf16[1024,128]{1,0:T(8,128)(2,1)S(1)} %collective-permute-done.15.a2), channel_id=1, source_target_pairs={{0,1},{1,0},{2,3},{3,2},{4,5},{5,4},{6,7},{7,6},{8,9},{9,8},{10,11... | collective-permute-start | bytes 786440 | tf_op jit(solution)/shard_map/ppermute | solution.py:472
  119.5 13.3 %collective-permute-start.36 = (bf16[128,1280]{1,0:T(8,128)(2,1)S(1)}, bf16[128,1280]{1,0:T(8,128)(2,1)S(1)}, u32[]{:S(2)}, u32[]{:S(2)}) collective-permute-start(bf16[128,1280]{1,0:T(8,128)(2,1)S(1)} %get-tuple-element.50), channel_id=1, source_target_pairs={{0,1},{1,0},{2,3},{3,2},{4,5},{5,4},{6,7},{7,6},{8,9},{9,8},{10,11... | collective-permute-start | bytes 983048 | tf_op jit(solution)/shard_map/ppermute | solution.py:472
  123.5 14.5 %collective-permute-start.34 = (bf16[128,1280]{1,0:T(8,128)(2,1)S(1)}, bf16[128,1280]{1,0:T(8,128)(2,1)S(1)}, u32[]{:S(2)}, u32[]{:S(2)}) collective-permute-start(bf16[128,1280]{1,0:T(8,128)(2,1)S(1)} %get-tuple-element.48), channel_id=1, source_target_pairs={{0,1},{1,0},{2,3},{3,2},{4,5},{5,4},{6,7},{7,6},{8,9},{9,8},{10,11... | collective-permute-start | bytes 983048 | tf_op jit(solution)/shard_map/ppermute | solution.py:472
  128.0 12.6 %collective-permute-start.32 = (bf16[128,1280]{1,0:T(8,128)(2,1)S(1)}, bf16[128,1280]{1,0:T(8,128)(2,1)S(1)}, u32[]{:S(2)}, u32[]{:S(2)}) collective-permute-start(bf16[128,1280]{1,0:T(8,128)(2,1)S(1)} %get-tuple-element.46), channel_id=1, source_target_pairs={{0,1},{1,0},{2,3},{3,2},{4,5},{5,4},{6,7},{7,6},{8,9},{9,8},{10,11... | collective-permute-start | bytes 983048 | tf_op jit(solution)/shard_map/ppermute | solution.py:472
  132.2 8.6 %collective-permute-start.31 = (bf16[128,1280]{1,0:T(8,128)(2,1)S(1)}, bf16[128,1280]{1,0:T(8,128)(2,1)S(1)}, u32[]{:S(2)}, u32[]{:S(2)}) collective-permute-start(bf16[128,1280]{1,0:T(8,128)(2,1)S(1)} %get-tuple-element.44), channel_id=1, source_target_pairs={{0,1},{1,0},{2,3},{3,2},{4,5},{5,4},{6,7},{7,6},{8,9},{9,8},{10,11... | collective-permute-start | bytes 983048 | tf_op jit(solution)/shard_map/ppermute | solution.py:472
  132.8 13.5 %collective-permute-start.37 = (bf16[128,1280]{1,0:T(8,128)(2,1)S(1)}, bf16[128,1280]{1,0:T(8,128)(2,1)S(1)}, u32[]{:S(2)}, u32[]{:S(2)}) collective-permute-start(bf16[128,1280]{1,0:T(8,128)(2,1)S(1)} %add_convert_fusion), channel_id=1, source_target_pairs={{0,2},{1,3},{2,0},{3,1},{4,6},{5,7},{6,4},{7,5},{8,10},{9,11},{10,... | collective-permute-start | bytes 983048 | tf_op jit(solution)/shard_map/ppermute | solution.py:472
  138.1 18.0 %collective-permute-start.35 = (bf16[128,1280]{1,0:T(8,128)(2,1)S(1)}, bf16[128,1280]{1,0:T(8,128)(2,1)S(1)}, u32[]{:S(2)}, u32[]{:S(2)}) collective-permute-start(bf16[128,1280]{1,0:T(8,128)(2,1)S(1)} %add_convert_fusion.1), channel_id=1, source_target_pairs={{0,6},{1,7},{2,4},{3,5},{4,2},{5,3},{6,0},{7,1},{8,14},{9,15},{10,... | collective-permute-start | bytes 983048 | tf_op jit(solution)/shard_map/ppermute | solution.py:472
  140.7 28.1 %collective-permute-start.33 = (bf16[128,1280]{1,0:T(8,128)(2,1)S(1)}, bf16[128,1280]{1,0:T(8,128)(2,1)S(1)}, u32[]{:S(2)}, u32[]{:S(2)}) collective-permute-start(bf16[128,1280]{1,0:T(8,128)(2,1)S(1)} %add_convert_fusion.2), channel_id=1, source_target_pairs={{0,4},{1,5},{2,6},{3,7},{4,0},{5,1},{6,2},{7,3},{8,12},{9,13},{10,... | collective-permute-start | bytes 983048 | tf_op jit(solution)/shard_map/ppermute | solution.py:472
  (24 other events, 353.7 us)

commit v2 on v1

--- a/solution.py
+++ b/solution.py
@@ -218,13 +218,38 @@
 F32 = jnp.float32
 
 
-def call(kernel, outs, operands, scalars, scratch=(), limit=32, flops=10**8, moved=10**6):
+def call(kernel, outs, operands, scalars, scratch=(), limit=12, flops=0, moved=0, far=()):
+    count = len(operands)
+    specs = [SMEM] * scalars + [VMEM] * (count - scalars)
+    for place in far:
+        specs[place] = pl.BlockSpec(memory_space=pltpu.HBM)
+    buffers = [pltpu.VMEM(operands[place].shape, operands[place].dtype) for place in far]
+    if far:
+        buffers.append(pltpu.SemaphoreType.DMA((len(far),)))
+
+    def whole(*refs):
+        refs = list(refs)
+        if far:
+            *near, arrivals = refs[len(refs) - len(far) - 1 :]
+            refs = refs[: len(refs) - len(far) - 1]
+            copies = [
+                pltpu.make_async_copy(refs[place], near[i], arrivals.at[i])
+                for i, place in enumerate(far)
+            ]
+            for copy in copies:
+                copy.start()
+            for copy in copies:
+                copy.wait()
+            for i, place in enumerate(far):
+                refs[place] = near[i]
+        kernel(*refs)
+
     return pl.pallas_call(
-        kernel,
+        whole,
         out_shape=outs,
-        in_specs=[SMEM] * scalars + [VMEM] * (len(operands) - scalars),
+        in_specs=specs,
         out_specs=jax.tree.map(lambda _: VMEM, outs),
-        scratch_shapes=list(scratch),
+        scratch_shapes=[*scratch, *buffers],
         compiler_params=pltpu.CompilerParams(vmem_limit_bytes=limit * 1024 * 1024),
         cost_estimate=pl.CostEstimate(flops=flops, bytes_accessed=moved, transcendentals=0),
     )(*operands)
@@ -267,14 +292,14 @@
     right = pages[:, 128:256].astype(F32)
     keys = jnp.where(low, left, pltpu.roll(right, HEAD_WIDTH, 1))
     values = jnp.where(low, pltpu.roll(left, HEAD_WIDTH, 1), right)
-    out[0:rows, 0:128] = unit_heads(keys, gain[...]).astype(BF16)
-    out[0:rows, 128:256] = values.astype(BF16)
-    out[0:rows, 256:640] = up[...]
-    row, column = iota((32, 256), 0), iota((32, 256), 1)
-    source = (row // 2) * ADAPTER_RANK + 2 * ids[0] + row % 2
+    out[0:256, 0:128] = unit_heads(keys, gain[...]).astype(BF16)
+    out[0:256, 128:256] = values.astype(BF16)
+    out[0:256, 256:640] = up[...]
+    row, column = iota((128, 256), 0), iota((128, 256), 1)
+    source = (row // 8) * ADAPTER_RANK + 8 * (ids[0] % 2) + row % 8
     picked = dot((column == source).astype(BF16), down[...]).astype(BF16)
-    out[rows : rows + 32, :] = picked[:, 0:640]
-    out[rows + 32 : rows + 64, :] = picked[:, 640:1280]
+    out[256:384, :] = picked[:, 0:640]
+    out[384:512, :] = picked[:, 640:1280]
 
 
 def by_request(index, scalars):
@@ -284,21 +309,22 @@
     return picked
 
 
-def select_kernel(ids, adapters, g0, g1, g2, g3, down_out, up_out):
-    tensor, dp = ids[0], ids[1]
-    row, column = iota((16, 32), 0), iota((16, 32), 1)
-    adapter = by_request(row // 2, adapters)
-    source = (adapter % 16) * 2 + row % 2
+def select_kernel(ids, adapters, g0, g1, g2, g3, g4, down_out, up_out):
+    core, dp = ids[0] % 2, ids[1]
+    row, column = iota((64, 128), 0), iota((64, 128), 1)
+    adapter = by_request(row // 8, adapters)
+    source = (adapter % 16) * 8 + row % 8
     owner = (adapter // 16) ^ dp
     up_row, up_column = iota((128, 256), 0), iota((128, 256), 1)
-    up_adapter = by_request((up_row % 16) // 2, adapters)
-    up_source = (up_adapter % 16) * 16 + 2 * ((up_row // 16) ^ tensor) + up_row % 2
+    up_adapter = by_request((up_row % 64) // 8, adapters)
+    up_source = (up_adapter % 16) * 16 + 8 * ((up_row // 64) ^ core) + up_row % 8
     up_owner = (up_adapter // 16) ^ dp
     left = right = up_total = 0.0
     for m, g in enumerate((g0, g1, g2, g3)):
+        lower, first = (g4, 0) if m == 3 else (g, 256)
         hot = ((column == source) & (owner == m)).astype(BF16)
-        left = left + dot(hot, g[256:288, :])
-        right = right + dot(hot, g[288:320, :])
+        left = left + dot(hot, lower[first : first + 128, :])
+        right = right + dot(hot, lower[first + 128 : first + 256, :])
         up_hot = ((up_column == up_source) & (up_owner == m)).astype(BF16)
         up_total = up_total + dot(up_hot, g[0:256, 256:640])
     down_out[:, 0:640] = left.astype(BF16)
@@ -306,69 +332,81 @@
     up_out[...] = up_total.astype(BF16)
 
 
-def qkv_kernel(j, ids, lengths, xa, xb, weight, down, up, cosines, sines, gain, q, k, v):
+def middle_chip(ids):
+    chip = ids[0] // 2
+    return (chip == 1) | (chip == 2)
+
+
+def arrived(ids, parts):
+    if len(parts) == 1:
+        return parts[0][0:128, :]
+    return jnp.where(middle_chip(ids), parts[0][0:128, :], parts[1][0:128, :])
+
+
+def piece_spots(ids, j):
     core = ids[0] % 2
-    block = (ids[0] // 2) ^ j
-    rows = jnp.concatenate([xa[...], xb[...]], axis=0)
-    own = pl.multiple_of(core * 128, 128)
-    other = pl.multiple_of((1 - core) * 128, 128)
-    row = iota((CHIP_ROWS, 128), 0)
-    row = block * CHIP_ROWS + jnp.where(row < 128, row + own, row - 128 + other)
-    request = (iota((CHIP_ROWS, 128), 1) % 16) // 2
-    start = jnp.int32(0)
-    first, end = jnp.zeros_like(row), jnp.zeros_like(row)
+    base = ((ids[0] // 2) ^ j) * CHIP_ROWS
+    return [pl.multiple_of(base + side * 128, 128) for side in (core, 1 - core)]
+
+
+def row_pieces(ids, refs, js):
+    pieces = []
+    for j in js:
+        count = 2 if j == 3 else 1
+        pieces += [arrived(ids, refs[:count]), arrived(ids, refs[count : 2 * count])]
+        refs = refs[2 * count :]
+    return pieces, refs
+
+
+def request_starts(lengths):
+    begins = [jnp.int32(0)]
     for i in range(GROUP_REQUESTS):
-        first = jnp.where(request == i, start, first)
-        start = start + lengths[0, i]
-        end = jnp.where(request == i, start, end)
-    middle = dot_nt(rows, down[...])
+        begins.append(begins[-1] + lengths[0, i])
+    return begins
+
+
+def project(j, ids, begins, pieces, weight, down, down_other, up, cosines, sines, gain):
+    rows = jnp.concatenate(pieces, axis=0)
+    count = rows.shape[0]
+    row = jnp.concatenate([spot + iota((128, 128), 0) for spot in piece_spots(ids, j)], axis=0)
+    request = (iota((1, 128), 1) % 64) // 8
+    first, end = jnp.zeros_like(request), jnp.zeros_like(request)
+    for i in range(GROUP_REQUESTS):
+        first = jnp.where(request == i, begins[i], first)
+        end = jnp.where(request == i, begins[i + 1], end)
+    middle = dot_nt(rows, jnp.concatenate([down[...], down_other[...]], axis=0))
     middle = jnp.where((row >= first) & (row < end), middle, 0.0).astype(BF16)
     total = dot(rows, weight[...]) + adapter_scale * dot(middle, up[...])
     part0, part1, part2 = total[:, 0:128], total[:, 128:256], total[:, 256:384]
-    low = first_head(CHIP_ROWS)
+    low = first_head(count)
     query = jnp.where(low, part0, part1)
     key = pltpu.roll(jnp.where(low, part2, part0), HEAD_WIDTH, 1)
     value = jnp.where(low, part1, part2).astype(BF16)
-    spots = [
-        pl.multiple_of(block * CHIP_ROWS + own, 128),
-        pl.multiple_of(block * CHIP_ROWS + other, 128),
-    ]
-    cosine = jnp.concatenate([cosines[pl.ds(s, 128), :] for s in spots], axis=0)
-    sine = jnp.concatenate([sines[pl.ds(s, 128), :] for s in spots], axis=0)
+    cosine = jnp.concatenate([cosines[pl.ds(spot, 128), :] for spot in piece_spots(ids, j)], axis=0)
+    sine = jnp.concatenate([sines[pl.ds(spot, 128), :] for spot in piece_spots(ids, j)], axis=0)
     half = HEAD_WIDTH // 2
-    head_low = (iota((CHIP_ROWS, 128), 1) % HEAD_WIDTH) < half
+    head_low = (iota((count, 128), 1) % HEAD_WIDTH) < half
 
     def finish(x):
         turned = jnp.where(head_low, pltpu.roll(x, 128 - half, 1), pltpu.roll(x, half, 1))
         return unit_heads(x * cosine + turned * sine, gain[...]).astype(BF16)
 
-    for out, result in ((q, finish(query)), (k, finish(key)), (v, value)):
-        out[pl.ds(own, 128), :] = result[0:128]
-        out[pl.ds(other, 128), :] = result[128:256]
-
-
-def attend_kernel(
-    ids, lengths, prompts, table,
-    q0, q1, q2, q3, k0, k1, k2, k3, v0, v1, v2, v3, g0, g1, g2, g3,
-    out, queries, keys, values, pages, starts,
-):
-    chip, dp = ids[0] // 2, ids[1]
-    for target, parts in (
-        (queries, (q0, q1, q2, q3)),
-        (keys, (k0, k1, k2, k3)),
-        (values, (v0, v1, v2, v3)),
-    ):
-        for j, part in enumerate(parts):
-            target[pl.ds(pl.multiple_of((chip ^ j) * CHIP_ROWS, CHIP_ROWS), CHIP_ROWS), :] = part[...]
+    return finish(query), finish(key), value
+
+
+def attend_kernel(ids, lengths, prompts, table, *refs):
+    pieces, refs = row_pieces(ids, refs, range(4))
+    *constants, g0, g1, g2, g3, out, queries, keys, values, pages, starts = refs
+    begins = request_starts(lengths)
+    for i, begin in enumerate(begins):
+        starts[i] = begin
+    for j in range(4):
+        parts = project(j, ids, begins, pieces[2 * j : 2 * j + 2], *constants)
+        for part, target in zip(parts, (queries, keys, values)):
+            for side, spot in enumerate(piece_spots(ids, j)):
+                target[pl.ds(spot, 128), :] = part[side * 128 : side * 128 + 128]
     for m, g in enumerate((g0, g1, g2, g3)):
-        pages[pl.ds(pl.multiple_of((dp ^ m) * 256, 256), 256), :] = g[0:256, 0:256]
-    begins = []
-    start = jnp.int32(0)
-    for i in range(GROUP_REQUESTS):
-        starts[i] = start
-        begins.append(start)
-        start = start + lengths[0, i]
-    starts[GROUP_REQUESTS] = start
+        pages[pl.ds(pl.multiple_of((ids[1] ^ m) * 256, 256), 256), :] = g[0:256, 0:256]
     low = first_head(128)
     tile_row = iota((256, 1), 0) % 128
 
@@ -422,45 +460,47 @@
     lax.fori_loop(0, out.shape[0] // 128, one_tile, 0)
 
 
-def collect_kernel(ids, o0, o1, o2, o3, p0, p1, p2, p3, out):
-    dp = ids[1]
-    for side, parts in enumerate(((o0, o1, o2, o3), (p0, p1, p2, p3))):
-        for m, part in enumerate(parts):
-            spot = pl.multiple_of((dp ^ m) * 32, 32)
-            for j in range(4):
-                out[2 * j + side, pl.ds(spot, 32), :] = part[j]
-
-
-def mlp_kernel(
-    j, ids, a0, a1, a2, a3, a4, a5, a6, a7, output, xa, xb, rate,
-    up, gate, up_scale, gate_scale, down, keep, send, *rest,
-):
-    result = rest[-1]
-    core = ids[0] % 2
-    spot = pl.multiple_of(((ids[0] // 2) ^ j) * CHIP_ROWS, CHIP_ROWS)
-    heads = jnp.concatenate(
-        [a[pl.ds(spot, CHIP_ROWS), :] for a in (a0, a1, a2, a3, a4, a5, a6, a7)], axis=1
-    )
-    attn_sum = dot(heads, output[...])
-    own = pl.multiple_of(core * 128, 128)
-    other = pl.multiple_of((1 - core) * 128, 128)
-    result[pl.ds(own, 128), :] = xa[...].astype(F32)
-    result[pl.ds(other, 128), :] = xb[...].astype(F32)
-    base = result[...]
-    mixed = renorm(base + rate[...] * (renorm(attn_sum) - base)).astype(BF16)
-    up_part = dot(mixed, up[...]) * up_scale[...]
-    gate_part = dot(mixed, gate[...]) * gate_scale[...]
-    unit_values = (up_part * (gate_part / (1.0 + jnp.exp(-gate_part)))).astype(BF16)
-    if j == 0:
-        result[...] = mixed.astype(F32)
-        rest[0][...] = result[pl.ds(own, 128), :].astype(BF16)
-    result[...] = dot(unit_values, down[...])
-    keep[...] = result[pl.ds(own, 128), :].astype(BF16)
-    send[...] = result[pl.ds(other, 128), :].astype(BF16)
+def collect_kernel(ids, o0, o1, o2, o3, out):
+    for m, part in enumerate((o0, o1, o2, o3)):
+        spot = pl.multiple_of((ids[1] ^ m) * 32, 32)
+        for j in range(4):
+            out[j, pl.ds(spot, 32), :] = part[j]
+
+
+def mlp_kernel(js, ids, *refs):
+    heads_in, refs = refs[:10], refs[10:]
+    pieces, refs = row_pieces(ids, refs, js)
+    output, output_other, rate, up, gate, up_scale, gate_scale, down, keep, send, *rest = refs
+    middle = middle_chip(ids)
+    for place, j in enumerate(js):
+        spots = piece_spots(ids, j)
+
+        def rows_of(heads):
+            return jnp.concatenate([heads[pl.ds(spot, 128), :] for spot in spots], axis=0)
+
+        attn_sum = 0.0
+        for side, matrix in enumerate((output, output_other)):
+            columns = [rows_of(heads_in[2 * distance + side]) for distance in range(4)]
+            columns[3] = jnp.where(middle, columns[3], rows_of(heads_in[8 + side]))
+            attn_sum = attn_sum + dot(jnp.concatenate(columns, axis=1), matrix[...])
+        base = jnp.concatenate(pieces[2 * place : 2 * place + 2], axis=0).astype(F32)
+        mixed = renorm(base + rate[...] * (renorm(attn_sum) - base)).astype(BF16)
+        up_part = dot(mixed, up[...]) * up_scale[...]
+        gate_part = dot(mixed, gate[...]) * gate_scale[...]
+        unit_values = (up_part * (gate_part / (1.0 + jnp.exp(-gate_part)))).astype(BF16)
+        result = dot(unit_values, down[...]).astype(BF16)
+        keep[place * 128 : place * 128 + 128, :] = result[0:128]
+        send[place * 128 : place * 128 + 128, :] = result[128:256]
+        if j == 0:
+            rest[0][...] = mixed[0:128]
+
+
+def add_kernel(keep, inward, out):
+    out[...] = keep[0:128, :].astype(F32) + inward[...].astype(F32)
 
 
 def final_kernel(mixed, keep, got, r1, r2, r3, rate, out):
-    mlp_sum = keep[...].astype(F32) + got[...].astype(F32)
+    mlp_sum = keep[256:384, :].astype(F32) + got[256:384, :].astype(F32)
     for r in (r1, r2, r3):
         mlp_sum = mlp_sum + r[...].astype(F32)
     base = mixed[...].astype(F32)
@@ -470,6 +510,17 @@
 def swap(values, distance, axis="tensor"):
     size = lax.axis_size(axis)
     return lax.ppermute(values, axis, [(i, i ^ distance) for i in range(size)])
+
+
+def chips(values, pairs):
+    return lax.ppermute(
+        values, "tensor", [(2 * a + core, 2 * b + core) for a, b in pairs for core in (0, 1)]
+    )
+
+
+MIDDLE = ((1, 2), (2, 1))
+OUTWARD = ((1, 0), (2, 3))
+INWARD = ((0, 1), (3, 2))
 
 
 def local_pairwise(
@@ -497,11 +548,28 @@
     ids = jnp.stack([tensor, dp]).astype(jnp.int32)
     gain = attention_scale.reshape(1, -1)
 
-    far = {j: swap(hidden, 2 * j) for j in (2, 3, 1)}
+    row_ids = jnp.arange(group_rows, dtype=jnp.int32)
+    starts = jnp.cumsum(lengths[0]) - lengths[0]
+    row_start = jnp.max(
+        jnp.where(row_ids[:, None] >= starts[None, :], starts[None, :], 0), axis=1
+    )
+    position = (row_ids - row_start).astype(F32) + PREFIX_LEN
+    half = HEAD_WIDTH // 2
+    lanes = jnp.arange(2 * HEAD_WIDTH, dtype=jnp.int32) % HEAD_WIDTH
+    frequency = jnp.exp((lanes % half).astype(F32) * (-2.0 * math.log(10000.0) / HEAD_WIDTH))
+    angles = position[:, None] * frequency[None, :]
+    cosines = jnp.cos(angles)
+    sines = jnp.where(lanes[None, :] < half, -1.0, 1.0) * jnp.sin(angles)
+
+    quarter = output_matrix.shape[0] // 4
+    own_quarter = lax.dynamic_slice_in_dim(output_matrix, dp * quarter, quarter, 0)
+    payload = jnp.concatenate([hidden, own_quarter], axis=0)
+    far2, far1 = swap(payload, 4), swap(payload, 2)
+    forwarded3, direct3 = chips(far2, OUTWARD), chips(payload, MIDDLE)
 
     prepared = call(
         prepare_kernel,
-        shape(320, 640),
+        shape(512, 640),
         (
             ids,
             prefix_page_cache.reshape(-1, prefix_page_cache.shape[2]),
@@ -510,60 +578,39 @@
             gain,
         ),
         1,
-    )
-    shared = [prepared] + [swap(prepared, m, "dp") for m in (1, 2, 3)]
+        far=(1, 2, 3),
+        limit=62,
+    )
+    near1, near2 = swap(prepared, 1, "dp"), swap(prepared, 2, "dp")
+    upper3, lower3 = swap(near2[0:256], 1, "dp"), swap(near1[256:512], 2, "dp")
+    shared = [prepared, near1, near2, upper3]
     down_own, up_all = call(
-        select_kernel, (shape(16, MODEL_WIDTH), shape(128, 384)), (ids, request_adapter, *shared), 2
-    )
-    down_pair = jnp.concatenate([down_own, swap(down_own, 1)], axis=0)
-    down_all = jnp.concatenate([down_pair] + [swap(down_pair, 2 * j) for j in (1, 2, 3)], axis=0)
-
-    row_ids = jnp.arange(group_rows, dtype=jnp.int32)
-    starts = jnp.cumsum(lengths[0]) - lengths[0]
-    row_start = jnp.max(
-        jnp.where(row_ids[:, None] >= starts[None, :], starts[None, :], 0), axis=1
-    )
-    position = (row_ids - row_start).astype(F32) + PREFIX_LEN
-    half = HEAD_WIDTH // 2
-    lanes = jnp.arange(2 * HEAD_WIDTH, dtype=jnp.int32) % HEAD_WIDTH
-    frequency = jnp.exp((lanes % half).astype(F32) * (-2.0 * math.log(10000.0) / HEAD_WIDTH))
-    angles = position[:, None] * frequency[None, :]
-    cosines = jnp.cos(angles)
-    sines = jnp.where(lanes[None, :] < half, -1.0, 1.0) * jnp.sin(angles)
-
-    rows = {0: (hidden, swap(hidden, 1))}
-    for j in (1, 2, 3):
-        rows[j] = (far[j], swap(far[j], 1))
-    query, key, value = {}, {}, {}
-    for j in range(4):
-        query[j], key[j], value[j] = call(
-            functools.partial(qkv_kernel, j),
-            (shape(CHIP_ROWS, 128),) * 3,
-            (ids, lengths, *rows[j], query_key_value_weight, down_all, up_all, cosines, sines, gain),
-            2,
-            flops=4 * 10**8,
-            moved=3 * 10**6,
-        )
-
-    quarter = output_matrix.shape[0] // 4
-    own_quarter = lax.dynamic_slice_in_dim(output_matrix, dp * quarter, quarter, 0)
-    quarters = jnp.stack([own_quarter] + [swap(own_quarter, 2 * j) for j in (1, 2, 3)])
-    blocks = [quarters] + [swap(quarters, m, "dp") for m in (1, 2, 3)]
-    others = [swap(b, 1) for b in blocks]
-    output_all = call(
-        collect_kernel,
-        jax.ShapeDtypeStruct((8, 4 * quarter, MODEL_WIDTH), BF16),
-        (ids, *blocks, *others),
-        1,
-    ).reshape(-1, MODEL_WIDTH)
+        select_kernel,
+        (shape(64, MODEL_WIDTH), shape(128, 384)),
+        (ids, request_adapter, *shared, lower3),
+        2,
+        flops=0,
+        moved=0,
+    )
+    down_other = swap(down_own, 1)
+
+    rows = {0: [payload, swap(payload, 1)]}
+    rows[1] = [far1, swap(far1, 1)]
+    rows[2] = [far2, swap(far2, 1)]
+    constants = (query_key_value_weight, down_own, down_other, up_all, cosines, sines, gain)
+    rows[3] = [direct3, forwarded3, swap(direct3, 1), swap(forwarded3, 1)]
+
+    chip = tensor // 2
+    last = jnp.where((chip == 1) | (chip == 2), direct3[128:], forwarded3[128:])
+    quarters = jnp.stack([payload[128:], far1[128:], far2[128:], last])
+    outputs = [quarters] + [swap(quarters, m, "dp") for m in (1, 2, 3)]
 
     attn = call(
         attend_kernel,
         shape(group_rows, 128),
         (
             ids, lengths, request_prompt, prompt_page_table,
-            *[query[j] for j in range(4)], *[key[j] for j in range(4)],
-            *[value[j] for j in range(4)], *shared,
+            *rows[0], *rows[1], *rows[2], *rows[3], *constants, *shared,
         ),
         4,
         scratch=(
@@ -573,42 +620,58 @@
             pltpu.VMEM((1024, 256), BF16),
             pltpu.SMEM((GROUP_REQUESTS + 1,), jnp.int32),
         ),
-        flops=4 * 10**9,
+        flops=2 * 10**10,
         moved=2 * 10**6,
-    )
-
-    heads = {0: (attn, swap(attn, 1))}
-    for j in (2, 3, 1):
-        got = swap(attn, 2 * j)
-        heads[j] = (got, swap(got, 1))
-    all_heads = [heads[j][side] for j in range(4) for side in (0, 1)]
-
-    keep, other = {}, {}
-    for j in (2, 3, 1, 0):
-        outs = (shape(128, MODEL_WIDTH),) * (3 if j == 0 else 2)
-        keep[j], send, *rest = call(
-            functools.partial(mlp_kernel, j),
-            outs,
-            (
-                ids, *all_heads, output_all, *rows[j], attention_rate.reshape(1, -1),
-                up_matrix, gate_matrix, up_scaling.reshape(1, -1), gate_scaling.reshape(1, -1),
-                down_matrix,
-            ),
+        limit=24,
+    )
+
+    attn, *outputs = lax.optimization_barrier((attn, *outputs))
+    heads2 = swap(attn, 4)
+    heads1 = swap(attn, 2)
+    heads3, heads3f = chips(attn, MIDDLE), chips(heads2, OUTWARD)
+    all_heads = [attn, swap(attn, 1), heads1, swap(heads1, 1), heads2, swap(heads2, 1)]
+    all_heads += [heads3, swap(heads3, 1), heads3f, swap(heads3f, 1)]
+
+    output_own = call(
+        collect_kernel,
+        jax.ShapeDtypeStruct((4, 4 * quarter, MODEL_WIDTH), BF16),
+        (ids, *outputs),
+        1,
+        flops=0,
+        moved=0,
+    ).reshape(-1, MODEL_WIDTH)
+    weights = (
+        output_own, swap(output_own, 1), attention_rate.reshape(1, -1), up_matrix, gate_matrix,
+        up_scaling.reshape(1, -1), gate_scaling.reshape(1, -1), down_matrix,
+    )
+    results = {}
+    for js in ((3,), (2, 1, 0)):
+        results[js] = call(
+            functools.partial(mlp_kernel, js),
+            (shape(128 * len(js), MODEL_WIDTH),) * 2 + (shape(128, MODEL_WIDTH),) * (0 in js),
+            (ids, *all_heads, *[piece for j in js for piece in rows[j]], *weights),
             1,
-            scratch=(pltpu.VMEM((CHIP_ROWS, MODEL_WIDTH), F32),),
-            limit=40,
-            flops=2 * 10**9,
+            limit=24,
+            flops=2 * 10**10,
             moved=10**7,
         )
-        other[j] = swap(send, 1)
-    mixed = rest[0]
-    received = [
-        swap((keep[j].astype(F32) + other[j].astype(F32)).astype(BF16), 2 * j) for j in (2, 3, 1)
-    ]
+    keep3, send3 = results[(3,)]
+    keep, send, mixed = results[(2, 1, 0)]
+    got = swap(send, 1)
+
+    def chunk(kept, swapped):
+        return (kept.astype(F32) + swapped.astype(F32)).astype(BF16)
+
+    chunk3 = chunk(keep3, swap(send3, 1))
+    inward = chips(chunk3, INWARD)
+    received3 = chips(chunk3, MIDDLE)
+    received1 = swap(chunk(keep[128:256], got[128:256]), 2)
+    joined = call(add_kernel, shape(128, MODEL_WIDTH, F32), (keep, inward), 0, flops=2 * 10**10)
+    received2 = swap(chunk(joined, got[0:128]), 4)
     return call(
         final_kernel,
         shape(*hidden.shape),
-        (mixed, keep[0], other[0], *received, feedforward_rate.reshape(1, -1)),
+        (mixed, keep, got, received1, received2, received3, feedforward_rate.reshape(1, -1)),
         0,
     )
 

time: 170 us -> 137 us (0.81)
  waiting for transfers between devices: 83.5 us -> 66.4 us
  starting transfers between devices: 36.4 us -> 28.3 us
  local copies, waits for them, and re-layouts: 6.51 us -> 0.96 us
  Pallas kernels: 39.3 us -> 35.5 us
    ppermute x38 -> x27, waiting for transfers between devices: 83.5 us -> 47.3 us  [swap(): return lax.ppermute(values, axis, [(i, i ^ distance) for i in range(size)])]
    ppermute x0 -> x6, waiting for transfers between devices: none -> 19.1 us  [chips(): lax.ppermute(values, 'tensor', [(2 * a + core, 2 * b + core) for a, b in...]
    ppermute x38 -> x27, starting transfers between devices: 36.4 us -> 21.4 us  [swap(): return lax.ppermute(values, axis, [(i, i ^ distance) for i in range(size)])]
    ppermute x0 -> x6, starting transfers between devices: none -> 6.97 us  [chips(): lax.ppermute(values, 'tensor', [(2 * a + core, 2 * b + core) for a, b in...]
    unnamed x40 -> x33, local copies, waits for them, and re-layouts: 6.47 us -> 0.85 us
    pallas_call x13 -> x8, Pallas kernels: 39.3 us -> 35.5 us  [call(): pl.pallas_call(whole, out_shape=outs, in_specs=specs, out_specs=jax.tree....]
  transfers between devices with their start and end apart: 38 -> 33, of which waited for: 13 -> 9; matrix products, arithmetic and copies ran while one was open for 3% -> 4% of each run, Pallas kernels for 20% -> 19%
where the time goes in v2:
time: 137 us
  waiting for transfers between devices  66.4 us (48%)
  Pallas kernels  35.5 us (26%)
  starting transfers between devices  28.3 us (21%)
  other arithmetic  5.2 us (4%)
    ppermute x27, waiting for transfers between devices, swap(): return lax.ppermute(values, axis, [(i, i ^ distance) for i in range(size)])  47.3 us
    pallas_call x8, Pallas kernels, call(): pl.pallas_call(whole, out_shape=outs, in_specs=specs, out_specs=jax.tree....  35.5 us
    ppermute x27, starting transfers between devices, swap(): return lax.ppermute(values, axis, [(i, i ^ distance) for i in range(size)])  21.4 us
    ppermute x6, waiting for transfers between devices, chips(): lax.ppermute(values, 'tensor', [(2 * a + core, 2 * b + core) for a, b in...  19.1 us
    ppermute x6, starting transfers between devices, chips(): lax.ppermute(values, 'tensor', [(2 * a + core, 2 * b + core) for a, b in...  6.97 us
  transfers between devices with their start and end apart: 33, of which 9 were waited for; matrix products, arithmetic and copies ran while one was open for 4% of the time, Pallas kernels for 19%

profile of v2, /device:TPU:0, one launch (start us, length us, event | category | flops | bytes accessed | tf_op | source)
XLA Modules:
  0.0 137.0 jit_solution(6362620565557223786)
XLA Ops:
  0.6 3.1 %shard_map.172.refs_2_.refs_21_ = bf16[512,640]{1,0:T(8,128)(2,1)} custom-call(s32[2]{0:T(128)} %pad_add_fusion.refs_0_, bf16[256,256]{1,0:T(8,128)(2,1)} %bitcast.26, bf16[256,384]{1,0:T(8,128)(2,1)} %bitcast.25, bf16[256,1280]{1,0:T(8,128)(2,1)} %bitcast.24, f32[1,128]{1,0:T(1,128)} %bitcast.22), custom_call_target="tpu_custom_call" | custom-call | tf_op jit(solution)/shard_map/pallas_call | solution.py:247
  3.7 3.0 %collective-permute-start.10 = (bf16[512,640]{1,0:T(8,128)(2,1)}, bf16[512,640]{1,0:T(8,128)(2,1)S(1)}, u32[]{:S(2)}, u32[]{:S(2)}) collective-permute-start(bf16[512,640]{1,0:T(8,128)(2,1)} %shard_map.172.refs_2_.refs_21_), channel_id=1, source_target_pairs={{0,16},{8,24},{16,0},{24,8},{1,17},{9,25},{17,1},{25,9},{2,18},{10... | collective-permute-start | bytes 1966088 | tf_op jit(solution)/shard_map/ppermute | solution.py:512
  6.8 1.5 %collective-permute-start.9 = (bf16[512,640]{1,0:T(8,128)(2,1)}, bf16[512,640]{1,0:T(8,128)(2,1)S(1)}, u32[]{:S(2)}, u32[]{:S(2)}) collective-permute-start(bf16[512,640]{1,0:T(8,128)(2,1)} %shard_map.172.refs_2_.refs_21_), channel_id=1, source_target_pairs={{0,8},{8,0},{16,24},{24,16},{1,9},{9,1},{17,25},{25,17},{2,10},{10... | collective-permute-start | bytes 1966088 | tf_op jit(solution)/shard_map/ppermute | solution.py:512
  8.3 2.7 %collective-permute-start.3 = (bf16[160,1280]{1,0:T(8,128)(2,1)S(1)}, bf16[160,1280]{1,0:T(8,128)(2,1)S(1)}, u32[]{:S(2)}, u32[]{:S(2)}) collective-permute-start(bf16[160,1280]{1,0:T(8,128)(2,1)S(1)} %pad_maximum_fusion.refs_4_.refs_15_), channel_id=1, source_target_pairs={{0,4},{1,5},{2,6},{3,7},{4,0},{5,1},{6,2},{7,3},{8,12},{9,13},{10,... | collective-permute-start | bytes 1228808 | tf_op jit(solution)/shard_map/ppermute | solution.py:512
  11.0 1.6 %collective-permute-start.1 = (bf16[160,1280]{1,0:T(8,128)(2,1)S(1)}, bf16[160,1280]{1,0:T(8,128)(2,1)S(1)}, u32[]{:S(2)}, u32[]{:S(2)}) collective-permute-start(bf16[160,1280]{1,0:T(8,128)(2,1)S(1)} %pad_maximum_fusion.refs_4_.refs_15_), channel_id=1, source_target_pairs={{0,2},{1,3},{2,0},{3,1},{4,6},{5,7},{6,4},{7,5},{8,10},{9,11},{10,... | collective-permute-start | bytes 1228808 | tf_op jit(solution)/shard_map/ppermute | solution.py:512
  12.6 1.4 %collective-permute-start.5 = (bf16[160,1280]{1,0:T(8,128)(2,1)S(1)}, bf16[160,1280]{1,0:T(8,128)(2,1)}, u32[]{:S(2)}, u32[]{:S(2)}) collective-permute-start(bf16[160,1280]{1,0:T(8,128)(2,1)S(1)} %pad_maximum_fusion.refs_4_.refs_15_), channel_id=1, source_target_pairs={{2,4},{3,5},{4,2},{5,3},{10,12},{11,13},{12,10},{13,11},{18,20},{1... | collective-permute-start | bytes 1228808 | tf_op jit(solution)/shard_map/ppermute | solution.py:516
  14.8 0.8 copy.20.refs_3_
  15.6 2.6 %fusion = (f32[1024,128]{1,0:T(8,128)S(1)}, f32[1024,128]{1,0:T(8,128)S(1)}) fusion(f32[128]{0:T(128)} %get-tuple-element.33, f32[128]{0:T(128)} %get-tuple-element.34, f32[1024]{0:T(1024)S(1)} %convert_add_fusion), kind=kLoop, calls=%fused_computation.5 | loop fusion | flops 262144 | bytes 1053696 | tf_op jit(solution)/shard_map/mul | solution.py:562
  18.1 11.8 %collective-permute-done.3.refs_8_.refs_11_ = bf16[160,1280]{1,0:T(8,128)(2,1)S(1)} collective-permute-done((bf16[160,1280]{1,0:T(8,128)(2,1)S(1)}, bf16[160,1280]{1,0:T(8,128)(2,1)S(1)}, u32[]{:S(2)}, u32[]{:S(2)}) %collective-permute-start.3) | collective-permute-done | bytes 409632 | tf_op jit(solution)/shard_map/ppermute | solution.py:512
  30.0 1.3 collective-permute-start.6
  32.6 11.1 %collective-permute-done.6.refs_11_.refs_12_ = bf16[160,1280]{1,0:T(8,128)(2,1)S(1)} collective-permute-done((bf16[160,1280]{1,0:T(8,128)(2,1)S(1)}, bf16[160,1280]{1,0:T(8,128)(2,1)S(1)}, u32[]{:S(2)}, u32[]{:S(2)}) %collective-permute-start.6) | collective-permute-done | bytes 409632 | tf_op jit(solution)/shard_map/ppermute | solution.py:516
  44.3 0.9 fusion.1
  45.3 1.1 shard_map.173
  48.1 2.5 %collective-permute-start.16 = (bf16[4,32,1280]{2,1,0:T(8,128)(2,1)S(1)}, bf16[4,32,1280]{2,1,0:T(8,128)(2,1)S(1)}, u32[]{:S(2)}, u32[]{:S(2)}) collective-permute-start(bf16[4,32,1280]{2,1,0:T(8,128)(2,1)S(1)} %pad_maximum_fusion.1.refs_1_), channel_id=1, source_target_pairs={{0,24},{8,16},{16,8},{24,0},{1,25},{9,17},{17,9},{25,1},{2,26},{10... | collective-permute-start | bytes 983048 | tf_op jit(solution)/shard_map/ppermute | solution.py:512
  50.6 15.6 %shard_map.174.refs_1_ = bf16[1024,128]{1,0:T(8,128)(2,1)S(1)} custom-call(s32[2]{0:T(128)S(1)} %copy-done.2, s32[1,8]{1,0:T(1,128)S(1)} %copy-done.9, s32[1,8]{1,0:T(1,128)S(1)} %copy-done.10, s32[32,4]{1,0:T(8,128)S(1)} %copy.20.refs_3_, bf16[160,1280]{1,0:T(8,128)(2,1)S(1)} %pad_maximum_fusion.refs_4_.refs_15_, ...), custom_call_target="tpu_custom_call" | custom-call | flops 20000000000 | bytes 2000000 | tf_op jit(solution)/shard_map/pallas_call | solution.py:247
  67.0 1.0 collective-permute-start.20
  67.9 2.0 %collective-permute-start.18 = (bf16[1024,128]{1,0:T(8,128)(2,1)S(1)}, bf16[1024,128]{1,0:T(8,128)(2,1)S(1)}, u32[]{:S(2)}, u32[]{:S(2)}) collective-permute-start(bf16[1024,128]{1,0:T(8,128)(2,1)S(1)} %shard_map.174.refs_1_), channel_id=1, source_target_pairs={{0,2},{1,3},{2,0},{3,1},{4,6},{5,7},{6,4},{7,5},{8,10},{9,11},{10,... | collective-permute-start | bytes 786440 | tf_op jit(solution)/shard_map/ppermute | solution.py:512
  70.0 0.7 collective-permute-start.22
  70.7 11.3 %collective-permute-done.20.refs_5_ = bf16[1024,128]{1,0:T(8,128)(2,1)S(1)} collective-permute-done((bf16[1024,128]{1,0:T(8,128)(2,1)S(1)}, bf16[1024,128]{1,0:T(8,128)(2,1)S(1)}, u32[]{:S(2)}, u32[]{:S(2)}) %collective-permute-start.20) | collective-permute-done | bytes 262176 | tf_op jit(solution)/shard_map/ppermute | solution.py:512
  82.0 1.5 %collective-permute-start.24 = (bf16[1024,128]{1,0:T(8,128)(2,1)S(1)}, bf16[1024,128]{1,0:T(8,128)(2,1)S(1)}, u32[]{:S(2)}, u32[]{:S(2)}) collective-permute-start(bf16[1024,128]{1,0:T(8,128)(2,1)S(1)} %collective-permute-done.20.refs_5_), channel_id=1, source_target_pairs={{2,0},{3,1},{4,6},{5,7},{10,8},{11,9},{12,14},{13,15},{18,16},{19,... | collective-permute-start | bytes 786440 | tf_op jit(solution)/shard_map/ppermute | solution.py:516
  84.2 7.9 %collective-permute-done.24.refs_9_ = bf16[1024,128]{1,0:T(8,128)(2,1)S(1)} collective-permute-done((bf16[1024,128]{1,0:T(8,128)(2,1)S(1)}, bf16[1024,128]{1,0:T(8,128)(2,1)S(1)}, u32[]{:S(2)}, u32[]{:S(2)}) %collective-permute-start.24) | collective-permute-done | bytes 262176 | tf_op jit(solution)/shard_map/ppermute | solution.py:516
  92.2 1.4 %collective-permute-done.25.refs_10_ = bf16[1024,128]{1,0:T(8,128)(2,1)S(1)} collective-permute-done((bf16[1024,128]{1,0:T(8,128)(2,1)S(1)}, bf16[1024,128]{1,0:T(8,128)(2,1)S(1)}, u32[]{:S(2)}, u32[]{:S(2)}) %collective-permute-start.25) | collective-permute-done | bytes 262176 | tf_op jit(solution)/shard_map/ppermute | solution.py:512
  93.7 4.3 %shard_map.177 = (bf16[128,1280]{1,0:T(8,128)(2,1)S(1)}, bf16[128,1280]{1,0:T(8,128)(2,1)S(1)}) custom-call(s32[2]{0:T(128)S(1)} %copy-done.2, bf16[1024,128]{1,0:T(8,128)(2,1)S(1)} %shard_map.174.refs_1_, bf16[1024,128]{1,0:T(8,128)(2,1)S(1)} %collective-permute-done.17.refs_2_, bf16[1024,128]{1,0:T(8,128)(2,1)S(1)} %collective-permute-done.18.refs_3_, ...), custom_call_target="tpu_custom_call" | custom-call | flops 20000000000 | bytes 10000000 | tf_op jit(solution)/shard_map/pallas_call | solution.py:247
  98.2 1.5 %collective-permute-done.29 = bf16[128,1280]{1,0:T(8,128)(2,1)S(1)} collective-permute-done((bf16[128,1280]{1,0:T(8,128)(2,1)S(1)}, bf16[128,1280]{1,0:T(8,128)(2,1)S(1)}, u32[]{:S(2)}, u32[]{:S(2)}) %collective-permute-start.29) | collective-permute-done | bytes 327712 | tf_op jit(solution)/shard_map/ppermute | solution.py:512
  99.7 1.4 %collective-permute-start.30 = (bf16[128,1280]{1,0:T(8,128)(2,1)S(1)}, bf16[128,1280]{1,0:T(8,128)(2,1)S(1)}, u32[]{:S(2)}, u32[]{:S(2)}) collective-permute-start(bf16[128,1280]{1,0:T(8,128)(2,1)S(1)} %add_convert_fusion.1), channel_id=1, source_target_pairs={{0,2},{1,3},{6,4},{7,5},{8,10},{9,11},{14,12},{15,13},{16,18},{17,... | collective-permute-start | bytes 983048 | tf_op jit(solution)/shard_map/ppermute | solution.py:516
  101.2 9.6 %shard_map.176 = (bf16[384,1280]{1,0:T(8,128)(2,1)S(1)}, bf16[384,1280]{1,0:T(8,128)(2,1)S(1)}, bf16[128,1280]{1,0:T(8,128)(2,1)S(1)}) custom-call(s32[2]{0:T(128)S(1)} %copy-done.2, bf16[1024,128]{1,0:T(8,128)(2,1)S(1)} %shard_map.174.refs_1_, bf16[1024,128]{1,0:T(8,128)(2,1)S(1)} %collective-permute-done.17.refs_2_, ...), custom_call_target="tpu_custom_call" | custom-call | flops 20000000000 | bytes 10000000 | tf_op jit(solution)/shard_map/pallas_call | solution.py:247
  110.9 0.7 collective-permute-start.32
  111.7 1.8 %collective-permute-done.27.refs_2_ = bf16[384,1280]{1,0:T(8,128)(2,1)S(1)} collective-permute-done((bf16[384,1280]{1,0:T(8,128)(2,1)S(1)}, bf16[384,1280]{1,0:T(8,128)(2,1)S(1)}, u32[]{:S(2)}, u32[]{:S(2)}) %collective-permute-start.27) | collective-permute-done | bytes 983072 | tf_op jit(solution)/shard_map/ppermute | solution.py:512
  113.8 2.5 %collective-permute-start.31 = (bf16[128,1280]{1,0:T(8,128)(2,1)S(1)}, bf16[128,1280]{1,0:T(8,128)(2,1)S(1)}, u32[]{:S(2)}, u32[]{:S(2)}) collective-permute-start(bf16[128,1280]{1,0:T(8,128)(2,1)S(1)} %get-tuple-element.29), channel_id=1, source_target_pairs={{0,4},{1,5},{2,6},{3,7},{4,0},{5,1},{6,2},{7,3},{8,12},{9,13},{10,... | collective-permute-start | bytes 983048 | tf_op jit(solution)/shard_map/ppermute | solution.py:512
  116.3 9.1 %collective-permute-done.28.refs_3_ = bf16[128,1280]{1,0:T(8,128)(2,1)S(1)} collective-permute-done((bf16[128,1280]{1,0:T(8,128)(2,1)S(1)}, bf16[128,1280]{1,0:T(8,128)(2,1)S(1)}, u32[]{:S(2)}, u32[]{:S(2)}) %collective-permute-start.28) | collective-permute-done | bytes 327712 | tf_op jit(solution)/shard_map/ppermute | solution.py:512
  125.4 10.3 %collective-permute-done.31.refs_4_ = bf16[128,1280]{1,0:T(8,128)(2,1)S(1)} collective-permute-done((bf16[128,1280]{1,0:T(8,128)(2,1)S(1)}, bf16[128,1280]{1,0:T(8,128)(2,1)S(1)}, u32[]{:S(2)}, u32[]{:S(2)}) %collective-permute-start.31) | collective-permute-done | bytes 327712 | tf_op jit(solution)/shard_map/ppermute | solution.py:512
  135.8 1.2 shard_map.179
  (97 shorter events, 7.4 us)
Async XLA Ops:
  3.7 26.2 %collective-permute-start.10 = (bf16[512,640]{1,0:T(8,128)(2,1)}, bf16[512,640]{1,0:T(8,128)(2,1)S(1)}, u32[]{:S(2)}, u32[]{:S(2)}) collective-permute-start(bf16[512,640]{1,0:T(8,128)(2,1)} %shard_map.172.refs_2_.refs_21_), channel_id=1, source_target_pairs={{0,16},{8,24},{16,0},{24,8},{1,17},{9,25},{17,1},{25,9},{2,18},{10... | collective-permute-start | bytes 1966088 | tf_op jit(solution)/shard_map/ppermute | solution.py:512
  6.8 24.6 %collective-permute-start.9 = (bf16[512,640]{1,0:T(8,128)(2,1)}, bf16[512,640]{1,0:T(8,128)(2,1)S(1)}, u32[]{:S(2)}, u32[]{:S(2)}) collective-permute-start(bf16[512,640]{1,0:T(8,128)(2,1)} %shard_map.172.refs_2_.refs_21_), channel_id=1, source_target_pairs={{0,8},{8,0},{16,24},{24,16},{1,9},{9,1},{17,25},{25,17},{2,10},{10... | collective-permute-start | bytes 1966088 | tf_op jit(solution)/shard_map/ppermute | solution.py:512
  8.3 21.6 %collective-permute-start.3 = (bf16[160,1280]{1,0:T(8,128)(2,1)S(1)}, bf16[160,1280]{1,0:T(8,128)(2,1)S(1)}, u32[]{:S(2)}, u32[]{:S(2)}) collective-permute-start(bf16[160,1280]{1,0:T(8,128)(2,1)S(1)} %pad_maximum_fusion.refs_4_.refs_15_), channel_id=1, source_target_pairs={{0,4},{1,5},{2,6},{3,7},{4,0},{5,1},{6,2},{7,3},{8,12},{9,13},{10,... | collective-permute-start | bytes 1228808 | tf_op jit(solution)/shard_map/ppermute | solution.py:512
  11.0 21.0 %collective-permute-start.1 = (bf16[160,1280]{1,0:T(8,128)(2,1)S(1)}, bf16[160,1280]{1,0:T(8,128)(2,1)S(1)}, u32[]{:S(2)}, u32[]{:S(2)}) collective-permute-start(bf16[160,1280]{1,0:T(8,128)(2,1)S(1)} %pad_maximum_fusion.refs_4_.refs_15_), channel_id=1, source_target_pairs={{0,2},{1,3},{2,0},{3,1},{4,6},{5,7},{6,4},{7,5},{8,10},{9,11},{10,... | collective-permute-start | bytes 1228808 | tf_op jit(solution)/shard_map/ppermute | solution.py:512
  12.6 20.0 %collective-permute-start.5 = (bf16[160,1280]{1,0:T(8,128)(2,1)S(1)}, bf16[160,1280]{1,0:T(8,128)(2,1)}, u32[]{:S(2)}, u32[]{:S(2)}) collective-permute-start(bf16[160,1280]{1,0:T(8,128)(2,1)S(1)} %pad_maximum_fusion.refs_4_.refs_15_), channel_id=1, source_target_pairs={{2,4},{3,5},{4,2},{5,3},{10,12},{11,13},{12,10},{13,11},{18,20},{1... | collective-permute-start | bytes 1228808 | tf_op jit(solution)/shard_map/ppermute | solution.py:516
  29.9 16.5 %collective-permute-start = (bf16[160,1280]{1,0:T(8,128)(2,1)S(1)}, bf16[160,1280]{1,0:T(8,128)(2,1)S(1)}, u32[]{:S(2)}, u32[]{:S(2)}) collective-permute-start(bf16[160,1280]{1,0:T(8,128)(2,1)S(1)} %pad_maximum_fusion.refs_4_.refs_15_), channel_id=1, source_target_pairs={{0,1},{1,0},{2,3},{3,2},{4,5},{5,4},{6,7},{7,6},{8,9},{9,8},{10,11... | collective-permute-start | bytes 1228808 | tf_op jit(solution)/shard_map/ppermute | solution.py:512
  30.0 13.8 %collective-permute-start.6 = (bf16[160,1280]{1,0:T(8,128)(2,1)S(1)}, bf16[160,1280]{1,0:T(8,128)(2,1)S(1)}, u32[]{:S(2)}, u32[]{:S(2)}) collective-permute-start(bf16[160,1280]{1,0:T(8,128)(2,1)S(1)} %collective-permute-done.3.refs_8_.refs_11_), channel_id=1, source_target_pairs={{2,0},{3,1},{4,6},{5,7},{10,8},{11,9},{12,14},{13,15},{18,16},{19,... | collective-permute-start | bytes 1228808 | tf_op jit(solution)/shard_map/ppermute | solution.py:516
  31.3 12.4 %collective-permute-start.11 = (bf16[256,640]{1,0:T(8,128)(2,1)S(1)}, bf16[256,640]{1,0:T(8,128)(2,1)S(1)}, u32[]{:S(2)}, u32[]{:S(2)}) collective-permute-start(bf16[256,640]{1,0:T(8,128)(2,1)S(1)} %slice.36), channel_id=1, source_target_pairs={{0,8},{8,0},{16,24},{24,16},{1,9},{9,1},{17,25},{25,17},{2,10},{10... | collective-permute-start | bytes 983048 | tf_op jit(solution)/shard_map/ppermute | solution.py:512
  32.0 12.3 %collective-permute-start.12 = (bf16[256,640]{1,0:T(8,128)(2,1)S(1)}, bf16[256,640]{1,0:T(8,128)(2,1)S(1)}, u32[]{:S(2)}, u32[]{:S(2)}) collective-permute-start(bf16[256,640]{1,0:T(8,128)(2,1)S(1)} %slice.37), channel_id=1, source_target_pairs={{0,16},{8,24},{16,0},{24,8},{1,17},{9,25},{17,1},{25,9},{2,18},{10... | collective-permute-start | bytes 983048 | tf_op jit(solution)/shard_map/ppermute | solution.py:512
  32.5 14.4 %collective-permute-start.4 = (bf16[160,1280]{1,0:T(8,128)(2,1)S(1)}, bf16[160,1280]{1,0:T(8,128)(2,1)S(1)}, u32[]{:S(2)}, u32[]{:S(2)}) collective-permute-start(bf16[160,1280]{1,0:T(8,128)(2,1)S(1)} %collective-permute-done.3.refs_8_.refs_11_), channel_id=1, source_target_pairs={{0,1},{1,0},{2,3},{3,2},{4,5},{5,4},{6,7},{7,6},{8,9},{9,8},{10,11... | collective-permute-start | bytes 1228808 | tf_op jit(solution)/shard_map/ppermute | solution.py:512
  43.7 3.8 %collective-permute-start.2 = (bf16[160,1280]{1,0:T(8,128)(2,1)S(1)}, bf16[160,1280]{1,0:T(8,128)(2,1)S(1)}, u32[]{:S(2)}, u32[]{:S(2)}) collective-permute-start(bf16[160,1280]{1,0:T(8,128)(2,1)S(1)} %collective-permute-done.1.refs_6_.refs_13_), channel_id=1, source_target_pairs={{0,1},{1,0},{2,3},{3,2},{4,5},{5,4},{6,7},{7,6},{8,9},{9,8},{10,11... | collective-permute-start | bytes 1228808 | tf_op jit(solution)/shard_map/ppermute | solution.py:512
  43.7 4.3 %collective-permute-start.7 = (bf16[160,1280]{1,0:T(8,128)(2,1)}, bf16[160,1280]{1,0:T(8,128)(2,1)S(1)}, u32[]{:S(2)}, u32[]{:S(2)}) collective-permute-start(bf16[160,1280]{1,0:T(8,128)(2,1)} %collective-permute-done.5.refs_10_.refs_11_), channel_id=1, source_target_pairs={{0,1},{1,0},{2,3},{3,2},{4,5},{5,4},{6,7},{7,6},{8,9},{9,8},{10,11... | collective-permute-start | bytes 1228808 | tf_op jit(solution)/shard_map/ppermute | solution.py:512
  44.2 6.3 %collective-permute-start.8 = (bf16[160,1280]{1,0:T(8,128)(2,1)S(1)}, bf16[160,1280]{1,0:T(8,128)(2,1)S(1)}, u32[]{:S(2)}, u32[]{:S(2)}) collective-permute-start(bf16[160,1280]{1,0:T(8,128)(2,1)S(1)} %collective-permute-done.6.refs_11_.refs_12_), channel_id=1, source_target_pairs={{0,1},{1,0},{2,3},{3,2},{4,5},{5,4},{6,7},{7,6},{8,9},{9,8},{10,11... | collective-permute-start | bytes 1228808 | tf_op jit(solution)/shard_map/ppermute | solution.py:512
  46.4 4.1 %collective-permute-start.13 = (bf16[64,1280]{1,0:T(8,128)(2,1)S(1)}, bf16[64,1280]{1,0:T(8,128)(2,1)S(1)}, u32[]{:S(2)}, u32[]{:S(2)}) collective-permute-start(bf16[64,1280]{1,0:T(8,128)(2,1)S(1)} %get-tuple-element.17.refs_15_), channel_id=1, source_target_pairs={{0,1},{1,0},{2,3},{3,2},{4,5},{5,4},{6,7},{7,6},{8,9},{9,8},{10,11... | collective-permute-start | bytes 491528 | tf_op jit(solution)/shard_map/ppermute | solution.py:512
  47.0 19.3 %collective-permute-start.14 = (bf16[4,32,1280]{2,1,0:T(8,128)(2,1)S(1)}, bf16[4,32,1280]{2,1,0:T(8,128)(2,1)S(1)}, u32[]{:S(2)}, u32[]{:S(2)}) collective-permute-start(bf16[4,32,1280]{2,1,0:T(8,128)(2,1)S(1)} %pad_maximum_fusion.1.refs_1_), channel_id=1, source_target_pairs={{0,8},{8,0},{16,24},{24,16},{1,9},{9,1},{17,25},{25,17},{2,10},{10... | collective-permute-start | bytes 983048 | tf_op jit(solution)/shard_map/ppermute | solution.py:512
  47.6 18.7 %collective-permute-start.15 = (bf16[4,32,1280]{2,1,0:T(8,128)(2,1)S(1)}, bf16[4,32,1280]{2,1,0:T(8,128)(2,1)S(1)}, u32[]{:S(2)}, u32[]{:S(2)}) collective-permute-start(bf16[4,32,1280]{2,1,0:T(8,128)(2,1)S(1)} %pad_maximum_fusion.1.refs_1_), channel_id=1, source_target_pairs={{0,16},{8,24},{16,0},{24,8},{1,17},{9,25},{17,1},{25,9},{2,18},{10... | collective-permute-start | bytes 983048 | tf_op jit(solution)/shard_map/ppermute | solution.py:512
  48.1 18.2 %collective-permute-start.16 = (bf16[4,32,1280]{2,1,0:T(8,128)(2,1)S(1)}, bf16[4,32,1280]{2,1,0:T(8,128)(2,1)S(1)}, u32[]{:S(2)}, u32[]{:S(2)}) collective-permute-start(bf16[4,32,1280]{2,1,0:T(8,128)(2,1)S(1)} %pad_maximum_fusion.1.refs_1_), channel_id=1, source_target_pairs={{0,24},{8,16},{16,8},{24,0},{1,25},{9,17},{17,9},{25,1},{2,26},{10... | collective-permute-start | bytes 983048 | tf_op jit(solution)/shard_map/ppermute | solution.py:512
  66.9 26.8 %collective-permute-start.26 = (bf16[512,1280]{1,0:T(8,128)(2,1)S(1)}, bf16[512,1280]{1,0:T(8,128)(2,1)S(1)}, u32[]{:S(2)}, u32[]{:S(2)}) collective-permute-start(bf16[512,1280]{1,0:T(8,128)(2,1)S(1)} %bitcast.19), channel_id=1, source_target_pairs={{0,1},{1,0},{2,3},{3,2},{4,5},{5,4},{6,7},{7,6},{8,9},{9,8},{10,11... | collective-permute-start | bytes 3932168 | tf_op jit(solution)/shard_map/ppermute | solution.py:512
  67.0 15.1 %collective-permute-start.20 = (bf16[1024,128]{1,0:T(8,128)(2,1)S(1)}, bf16[1024,128]{1,0:T(8,128)(2,1)S(1)}, u32[]{:S(2)}, u32[]{:S(2)}) collective-permute-start(bf16[1024,128]{1,0:T(8,128)(2,1)S(1)} %shard_map.174.refs_1_), channel_id=1, source_target_pairs={{0,4},{1,5},{2,6},{3,7},{4,0},{5,1},{6,2},{7,3},{8,12},{9,13},{10,... | collective-permute-start | bytes 786440 | tf_op jit(solution)/shard_map/ppermute | solution.py:512
  67.9 15.6 %collective-permute-start.18 = (bf16[1024,128]{1,0:T(8,128)(2,1)S(1)}, bf16[1024,128]{1,0:T(8,128)(2,1)S(1)}, u32[]{:S(2)}, u32[]{:S(2)}) collective-permute-start(bf16[1024,128]{1,0:T(8,128)(2,1)S(1)} %shard_map.174.refs_1_), channel_id=1, source_target_pairs={{0,2},{1,3},{2,0},{3,1},{4,6},{5,7},{6,4},{7,5},{8,10},{9,11},{10,... | collective-permute-start | bytes 786440 | tf_op jit(solution)/shard_map/ppermute | solution.py:512
  70.0 13.6 %collective-permute-start.22 = (bf16[1024,128]{1,0:T(8,128)(2,1)S(1)}, bf16[1024,128]{1,0:T(8,128)(2,1)S(1)}, u32[]{:S(2)}, u32[]{:S(2)}) collective-permute-start(bf16[1024,128]{1,0:T(8,128)(2,1)S(1)} %shard_map.174.refs_1_), channel_id=1, source_target_pairs={{2,4},{3,5},{4,2},{5,3},{10,12},{11,13},{12,10},{13,11},{18,20},{1... | collective-permute-start | bytes 786440 | tf_op jit(solution)/shard_map/ppermute | solution.py:516
  70.7 13.4 %collective-permute-start.17 = (bf16[1024,128]{1,0:T(8,128)(2,1)S(1)}, bf16[1024,128]{1,0:T(8,128)(2,1)S(1)}, u32[]{:S(2)}, u32[]{:S(2)}) collective-permute-start(bf16[1024,128]{1,0:T(8,128)(2,1)S(1)} %shard_map.174.refs_1_), channel_id=1, source_target_pairs={{0,1},{1,0},{2,3},{3,2},{4,5},{5,4},{6,7},{7,6},{8,9},{9,8},{10,11... | collective-permute-start | bytes 786440 | tf_op jit(solution)/shard_map/ppermute | solution.py:512
  82.0 10.1 %collective-permute-start.24 = (bf16[1024,128]{1,0:T(8,128)(2,1)S(1)}, bf16[1024,128]{1,0:T(8,128)(2,1)S(1)}, u32[]{:S(2)}, u32[]{:S(2)}) collective-permute-start(bf16[1024,128]{1,0:T(8,128)(2,1)S(1)} %collective-permute-done.20.refs_5_), channel_id=1, source_target_pairs={{2,0},{3,1},{4,6},{5,7},{10,8},{11,9},{12,14},{13,15},{18,16},{19,... | collective-permute-start | bytes 786440 | tf_op jit(solution)/shard_map/ppermute | solution.py:516
  83.5 8.7 %collective-permute-start.21 = (bf16[1024,128]{1,0:T(8,128)(2,1)S(1)}, bf16[1024,128]{1,0:T(8,128)(2,1)S(1)}, u32[]{:S(2)}, u32[]{:S(2)}) collective-permute-start(bf16[1024,128]{1,0:T(8,128)(2,1)S(1)} %collective-permute-done.20.refs_5_), channel_id=1, source_target_pairs={{0,1},{1,0},{2,3},{3,2},{4,5},{5,4},{6,7},{7,6},{8,9},{9,8},{10,11... | collective-permute-start | bytes 786440 | tf_op jit(solution)/shard_map/ppermute | solution.py:512
  83.6 8.6 %collective-permute-start.19 = (bf16[1024,128]{1,0:T(8,128)(2,1)S(1)}, bf16[1024,128]{1,0:T(8,128)(2,1)S(1)}, u32[]{:S(2)}, u32[]{:S(2)}) collective-permute-start(bf16[1024,128]{1,0:T(8,128)(2,1)S(1)} %collective-permute-done.18.refs_3_), channel_id=1, source_target_pairs={{0,1},{1,0},{2,3},{3,2},{4,5},{5,4},{6,7},{7,6},{8,9},{9,8},{10,11... | collective-permute-start | bytes 786440 | tf_op jit(solution)/shard_map/ppermute | solution.py:512
  84.1 8.1 %collective-permute-start.23 = (bf16[1024,128]{1,0:T(8,128)(2,1)S(1)}, bf16[1024,128]{1,0:T(8,128)(2,1)S(1)}, u32[]{:S(2)}, u32[]{:S(2)}) collective-permute-start(bf16[1024,128]{1,0:T(8,128)(2,1)S(1)} %collective-permute-done.22.refs_7_), channel_id=1, source_target_pairs={{0,1},{1,0},{2,3},{3,2},{4,5},{5,4},{6,7},{7,6},{8,9},{9,8},{10,11... | collective-permute-start | bytes 786440 | tf_op jit(solution)/shard_map/ppermute | solution.py:512
  98.0 1.7 %collective-permute-start.29 = (bf16[128,1280]{1,0:T(8,128)(2,1)S(1)}, bf16[128,1280]{1,0:T(8,128)(2,1)S(1)}, u32[]{:S(2)}, u32[]{:S(2)}) collective-permute-start(bf16[128,1280]{1,0:T(8,128)(2,1)S(1)} %get-tuple-element.28), channel_id=1, source_target_pairs={{0,1},{1,0},{2,3},{3,2},{4,5},{5,4},{6,7},{7,6},{8,9},{9,8},{10,11... | collective-permute-start | bytes 983048 | tf_op jit(solution)/shard_map/ppermute | solution.py:512
  99.7 11.8 %collective-permute-start.30 = (bf16[128,1280]{1,0:T(8,128)(2,1)S(1)}, bf16[128,1280]{1,0:T(8,128)(2,1)S(1)}, u32[]{:S(2)}, u32[]{:S(2)}) collective-permute-start(bf16[128,1280]{1,0:T(8,128)(2,1)S(1)} %add_convert_fusion.1), channel_id=1, source_target_pairs={{0,2},{1,3},{6,4},{7,5},{8,10},{9,11},{14,12},{15,13},{16,18},{17,... | collective-permute-start | bytes 983048 | tf_op jit(solution)/shard_map/ppermute | solution.py:516
  110.8 2.6 %collective-permute-start.27 = (bf16[384,1280]{1,0:T(8,128)(2,1)S(1)}, bf16[384,1280]{1,0:T(8,128)(2,1)S(1)}, u32[]{:S(2)}, u32[]{:S(2)}) collective-permute-start(bf16[384,1280]{1,0:T(8,128)(2,1)S(1)} %get-tuple-element.26), channel_id=1, source_target_pairs={{0,1},{1,0},{2,3},{3,2},{4,5},{5,4},{6,7},{7,6},{8,9},{9,8},{10,11... | collective-permute-start | bytes 2949128 | tf_op jit(solution)/shard_map/ppermute | solution.py:512
  110.9 5.4 %collective-permute-start.32 = (bf16[128,1280]{1,0:T(8,128)(2,1)S(1)}, bf16[128,1280]{1,0:T(8,128)(2,1)S(1)}, u32[]{:S(2)}, u32[]{:S(2)}) collective-permute-start(bf16[128,1280]{1,0:T(8,128)(2,1)S(1)} %add_convert_fusion.1), channel_id=1, source_target_pairs={{2,4},{3,5},{4,2},{5,3},{10,12},{11,13},{12,10},{13,11},{18,20},{1... | collective-permute-start | bytes 983048 | tf_op jit(solution)/shard_map/ppermute | solution.py:516
  113.6 11.8 %collective-permute-start.28 = (bf16[128,1280]{1,0:T(8,128)(2,1)S(1)}, bf16[128,1280]{1,0:T(8,128)(2,1)S(1)}, u32[]{:S(2)}, u32[]{:S(2)}) collective-permute-start(bf16[128,1280]{1,0:T(8,128)(2,1)S(1)} %get-tuple-element.30), channel_id=1, source_target_pairs={{0,2},{1,3},{2,0},{3,1},{4,6},{5,7},{6,4},{7,5},{8,10},{9,11},{10,... | collective-permute-start | bytes 983048 | tf_op jit(solution)/shard_map/ppermute | solution.py:512
  113.8 22.0 %collective-permute-start.31 = (bf16[128,1280]{1,0:T(8,128)(2,1)S(1)}, bf16[128,1280]{1,0:T(8,128)(2,1)S(1)}, u32[]{:S(2)}, u32[]{:S(2)}) collective-permute-start(bf16[128,1280]{1,0:T(8,128)(2,1)S(1)} %get-tuple-element.29), channel_id=1, source_target_pairs={{0,4},{1,5},{2,6},{3,7},{4,0},{5,1},{6,2},{7,3},{8,12},{9,13},{10,... | collective-permute-start | bytes 983048 | tf_op jit(solution)/shard_map/ppermute | solution.py:512
  (17 other events, 355.3 us)

commit v3 on v2

--- a/solution.py
+++ b/solution.py
@@ -218,11 +218,13 @@
 F32 = jnp.float32
 
 
-def call(kernel, outs, operands, scalars, scratch=(), limit=12, flops=0, moved=0, far=()):
+def call(kernel, outs, operands, scalars, scratch=(), limit=12, flops=0, moved=0, far=(), unread=()):
     count = len(operands)
     specs = [SMEM] * scalars + [VMEM] * (count - scalars)
     for place in far:
         specs[place] = pl.BlockSpec(memory_space=pltpu.HBM)
+    for place in unread:
+        specs[place] = pl.BlockSpec(memory_space=pl.ANY)
     buffers = [pltpu.VMEM(operands[place].shape, operands[place].dtype) for place in far]
     if far:
         buffers.append(pltpu.SemaphoreType.DMA((len(far),)))
@@ -396,7 +398,7 @@
 
 def attend_kernel(ids, lengths, prompts, table, *refs):
     pieces, refs = row_pieces(ids, refs, range(4))
-    *constants, g0, g1, g2, g3, out, queries, keys, values, pages, starts = refs
+    *constants, g0, g1, g2, g3, out, queries, keys, values, pages, starts, sums = refs
     begins = request_starts(lengths)
     for i, begin in enumerate(begins):
         starts[i] = begin
@@ -407,57 +409,82 @@
                 target[pl.ds(spot, 128), :] = part[side * 128 : side * 128 + 128]
     for m, g in enumerate((g0, g1, g2, g3)):
         pages[pl.ds(pl.multiple_of((ids[1] ^ m) * 256, 256), 256), :] = g[0:256, 0:256]
+    tiles = out.shape[0] // 128
     low = first_head(128)
-    tile_row = iota((256, 1), 0) % 128
-
-    def one_tile(tile, carry):
-        base = pl.multiple_of(tile * 128, 128)
-        query = queries[pl.ds(base, 128), :]
+    low_keys = first_head(256)
+    ones = jnp.ones((256, 128), BF16)
+
+    def tile_queries(tile):
+        query = queries[pl.ds(pl.multiple_of(tile * 128, 128), 128), :]
         zero = jnp.zeros_like(query)
         both = jnp.concatenate(
             [jnp.where(low, query, zero), jnp.where(low, zero, query)], axis=0
         )
-        row = base + tile_row
+        return both, tile * 128 + iota((256, 1), 0) % 128
+
+    def prefix(request):
+        prompt = prompts[0, request]
+        spots = [pl.multiple_of(table[prompt, p] * PAGE, PAGE) for p in range(PREFIX_LEN // PAGE)]
+        return (
+            jnp.concatenate([pages[pl.ds(s, PAGE), 0:128] for s in spots], axis=0),
+            jnp.concatenate([pages[pl.ds(s, PAGE), 128:256] for s in spots], axis=0),
+        )
+
+    def window(spot):
+        spot = pl.multiple_of(spot, 128)
+        return keys[pl.ds(spot, 256), :], values[pl.ds(spot, 256), :], spot + iota((256, 256), 1)
+
+    def products(both, key, value, mask):
+        weights = jnp.where(mask, jnp.exp2(dot_nt(both, key) * SCORE_LOG2), 0.0).astype(BF16)
+        return (
+            dot(weights[:128], jnp.where(low_keys, value, ones)),
+            dot(weights[128:], jnp.where(low_keys, ones, value)),
+        )
+
+    firsts = []
+    for tile in range(tiles):
+        base = tile * 128
+        both, row = tile_queries(tile)
+        first = jnp.int32(0)
         row_start = jnp.zeros_like(row)
-        first = jnp.int32(0)
-        last = jnp.int32(0)
-        for i in range(1, GROUP_REQUESTS):
-            row_start = jnp.where(row >= begins[i], begins[i], row_start)
-            first = first + (begins[i] <= base).astype(jnp.int32)
-            last = last + (begins[i] <= base + 127).astype(jnp.int32)
-
-        def add(state, key, value, mask):
-            total, norm = state
-            weights = jnp.where(mask, jnp.exp2(dot_nt(both, key) * SCORE_LOG2), 0.0)
-            return (
-                total + dot(weights.astype(BF16), value),
-                norm + jnp.sum(weights, axis=-1, keepdims=True),
-            )
-
-        def own_block(block, state):
-            spot = pl.multiple_of(block * 128, 128)
-            column = spot + iota((256, 128), 1)
-            mask = (column >= row_start) & (column <= row)
-            return add(state, keys[pl.ds(spot, 128), :], values[pl.ds(spot, 128), :], mask)
-
-        def prefix(request, state):
-            prompt = prompts[0, request]
-            spots = [pl.multiple_of(table[prompt, p] * PAGE, PAGE) for p in range(4)]
-            key = jnp.concatenate([pages[pl.ds(s, PAGE), 0:128] for s in spots], axis=0)
-            value = jnp.concatenate([pages[pl.ds(s, PAGE), 128:256] for s in spots], axis=0)
-            mask = (row >= starts[request]) & (row < starts[request + 1])
-            return add(state, key, value, jnp.broadcast_to(mask, (256, PREFIX_LEN)))
-
-        state = (jnp.zeros((256, 128), F32), jnp.zeros((256, 1), F32))
-        state = prefix(first, state)
-        state = own_block(tile, state)
-        state = lax.fori_loop(starts[first] // 128, tile, own_block, state)
-        total, norm = lax.fori_loop(first + 1, last + 1, prefix, state)
-        total = total / norm
-        out[pl.ds(base, 128), :] = jnp.where(low, total[0:128], total[128:256]).astype(BF16)
-        return carry
-
-    lax.fori_loop(0, out.shape[0] // 128, one_tile, 0)
+        for begin in begins[1:GROUP_REQUESTS]:
+            row_start = jnp.where(row >= begin, begin, row_start)
+            first = first + (begin <= base).astype(jnp.int32)
+        firsts.append(first)
+        mask = jnp.broadcast_to(row < starts[first + 1], (256, PREFIX_LEN))
+        shared = products(both, *prefix(first), mask)
+        key, value, column = window(max(base - 128, 0))
+        own = products(both, key, value, (column >= row_start) & (column <= row))
+        for head in (0, 1):
+            sums[tile, head] = shared[head] + own[head]
+    for i in range(1, GROUP_REQUESTS):
+        begin, end = begins[i], begins[i + 1]
+        tile = begin // 128
+        both, row = tile_queries(tile)
+        mask = (row >= begin) & (row < end) & (begin % 128 != 0)
+        more = products(both, *prefix(i), jnp.broadcast_to(mask, (256, PREFIX_LEN)))
+        for head in (0, 1):
+            sums[tile, head] += more[head]
+    for tile in range(2, tiles):
+        base = tile * 128
+        first = firsts[tile]
+        begin, end = starts[first], starts[first + 1]
+
+        def earlier(step, carry, tile=tile, base=base, begin=begin, end=end):
+            both, row = tile_queries(tile)
+            stop = base - 128 - 256 * step
+            key, value, column = window(jnp.maximum(stop - 256, 0))
+            mask = (column >= begin) & (column < stop) & (row < end)
+            more = products(both, key, value, mask)
+            for head in (0, 1):
+                sums[tile, head] += more[head]
+            return carry
+
+        lax.fori_loop(0, jnp.maximum(base + 127 - begin, 0) // 256, earlier, 0)
+    for tile in range(tiles):
+        left, right = sums[tile, 0], sums[tile, 1]
+        weight = pltpu.roll(jnp.where(low, right, left), HEAD_WIDTH, 1)
+        out[tile * 128 : tile * 128 + 128, :] = (jnp.where(low, left, right) / weight).astype(BF16)
 
 
 def collect_kernel(ids, o0, o1, o2, o3, out):
@@ -470,8 +497,8 @@
 def mlp_kernel(js, ids, *refs):
     heads_in, refs = refs[:10], refs[10:]
     pieces, refs = row_pieces(ids, refs, js)
-    output, output_other, rate, up, gate, up_scale, gate_scale, down, keep, send, *rest = refs
-    middle = middle_chip(ids)
+    output, output_other, rate, up, gate, up_scale, gate_scale, down, _, keep, send, *rest = refs
+    direct = middle_chip(ids)
     for place, j in enumerate(js):
         spots = piece_spots(ids, j)
 
@@ -481,7 +508,7 @@
         attn_sum = 0.0
         for side, matrix in enumerate((output, output_other)):
             columns = [rows_of(heads_in[2 * distance + side]) for distance in range(4)]
-            columns[3] = jnp.where(middle, columns[3], rows_of(heads_in[8 + side]))
+            columns[3] = jnp.where(direct, columns[3], rows_of(heads_in[8 + side]))
             attn_sum = attn_sum + dot(jnp.concatenate(columns, axis=1), matrix[...])
         base = jnp.concatenate(pieces[2 * place : 2 * place + 2], axis=0).astype(F32)
         mixed = renorm(base + rate[...] * (renorm(attn_sum) - base)).astype(BF16)
@@ -495,12 +522,13 @@
             rest[0][...] = mixed[0:128]
 
 
-def add_kernel(keep, inward, out):
-    out[...] = keep[0:128, :].astype(F32) + inward[...].astype(F32)
+def add_kernel(ids, keep, inward, direct, out):
+    more = inward[...].astype(F32)
+    out[...] = keep[0:128, :].astype(F32) + jnp.where(middle_chip(ids), more, 0.0)
 
 
 def final_kernel(mixed, keep, got, r1, r2, r3, rate, out):
-    mlp_sum = keep[256:384, :].astype(F32) + got[256:384, :].astype(F32)
+    mlp_sum = keep[...].astype(F32) + got[...].astype(F32)
     for r in (r1, r2, r3):
         mlp_sum = mlp_sum + r[...].astype(F32)
     base = mixed[...].astype(F32)
@@ -512,15 +540,8 @@
     return lax.ppermute(values, axis, [(i, i ^ distance) for i in range(size)])
 
 
-def chips(values, pairs):
-    return lax.ppermute(
-        values, "tensor", [(2 * a + core, 2 * b + core) for a, b in pairs for core in (0, 1)]
-    )
-
-
-MIDDLE = ((1, 2), (2, 1))
-OUTWARD = ((1, 0), (2, 3))
-INWARD = ((0, 1), (3, 2))
+def middle(values):
+    return lax.ppermute(values, "tensor", [(2, 4), (3, 5), (4, 2), (5, 3)])
 
 
 def local_pairwise(
@@ -565,7 +586,7 @@
     own_quarter = lax.dynamic_slice_in_dim(output_matrix, dp * quarter, quarter, 0)
     payload = jnp.concatenate([hidden, own_quarter], axis=0)
     far2, far1 = swap(payload, 4), swap(payload, 2)
-    forwarded3, direct3 = chips(far2, OUTWARD), chips(payload, MIDDLE)
+    forwarded3, direct3 = swap(far2, 2), middle(payload)
 
     prepared = call(
         prepare_kernel,
@@ -619,16 +640,17 @@
             pltpu.VMEM((group_rows, 128), BF16),
             pltpu.VMEM((1024, 256), BF16),
             pltpu.SMEM((GROUP_REQUESTS + 1,), jnp.int32),
+            pltpu.VMEM((group_rows // 128, 2, 128, 128), F32),
         ),
         flops=2 * 10**10,
         moved=2 * 10**6,
         limit=24,
     )
 
-    attn, *outputs = lax.optimization_barrier((attn, *outputs))
     heads2 = swap(attn, 4)
     heads1 = swap(attn, 2)
-    heads3, heads3f = chips(attn, MIDDLE), chips(heads2, OUTWARD)
+    heads1, heads2, *outputs = lax.optimization_barrier((heads1, heads2, *outputs))
+    heads3, heads3f = middle(attn), swap(heads2, 2)
     all_heads = [attn, swap(attn, 1), heads1, swap(heads1, 1), heads2, swap(heads2, 1)]
     all_heads += [heads3, swap(heads3, 1), heads3f, swap(heads3f, 1)]
 
@@ -644,34 +666,42 @@
         output_own, swap(output_own, 1), attention_rate.reshape(1, -1), up_matrix, gate_matrix,
         up_scaling.reshape(1, -1), gate_scaling.reshape(1, -1), down_matrix,
     )
-    results = {}
-    for js in ((3,), (2, 1, 0)):
-        results[js] = call(
+    def update(js, previous):
+        operands = (ids, *all_heads, *[piece for j in js for piece in rows[j]], *weights, previous)
+        return call(
             functools.partial(mlp_kernel, js),
             (shape(128 * len(js), MODEL_WIDTH),) * 2 + (shape(128, MODEL_WIDTH),) * (0 in js),
-            (ids, *all_heads, *[piece for j in js for piece in rows[j]], *weights),
+            operands,
             1,
             limit=24,
             flops=2 * 10**10,
             moved=10**7,
+            unread=(len(operands) - 1,),
         )
-    keep3, send3 = results[(3,)]
-    keep, send, mixed = results[(2, 1, 0)]
-    got = swap(send, 1)
 
     def chunk(kept, swapped):
         return (kept.astype(F32) + swapped.astype(F32)).astype(BF16)
 
+    keep3, send3 = update((3,), ids)
     chunk3 = chunk(keep3, swap(send3, 1))
-    inward = chips(chunk3, INWARD)
-    received3 = chips(chunk3, MIDDLE)
+    inward, received3 = swap(chunk3, 2), middle(chunk3)
+    keep, send = update((2, 1), keep3)
+    got = swap(send, 1)
     received1 = swap(chunk(keep[128:256], got[128:256]), 2)
-    joined = call(add_kernel, shape(128, MODEL_WIDTH, F32), (keep, inward), 0, flops=2 * 10**10)
+    joined = call(
+        add_kernel,
+        shape(128, MODEL_WIDTH, F32),
+        (ids, keep, inward, received3),
+        1,
+        flops=2 * 10**10,
+        unread=(3,),
+    )
     received2 = swap(chunk(joined, got[0:128]), 4)
+    keep0, send0, mixed = update((0,), joined)
     return call(
         final_kernel,
         shape(*hidden.shape),
-        (mixed, keep, got, received1, received2, received3, feedforward_rate.reshape(1, -1)),
+        (mixed, keep0, swap(send0, 1), received1, received2, received3, feedforward_rate.reshape(1, -1)),
         0,
     )
 

time: 137 us -> 124 us (0.905)
  waiting for transfers between devices: 66.4 us -> 56.9 us
  Pallas kernels: 35.5 us -> 30.5 us
    ppermute x6 -> x3, waiting for transfers between devices: 19.1 us -> 0.01 us  [middle(): return lax.ppermute(values, 'tensor', [(2, 4), (3, 5), (4, 2), (5, 3)])]
    ppermute x27 -> x31, waiting for transfers between devices: 47.3 us -> 56.9 us  [swap(): return lax.ppermute(values, axis, [(i, i ^ distance) for i in range(size)])]
    ppermute x27 -> x31, starting transfers between devices: 21.4 us -> 26.6 us  [swap(): return lax.ppermute(values, axis, [(i, i ^ distance) for i in range(size)])]
    pallas_call x8 -> x9, Pallas kernels: 35.5 us -> 30.5 us  [call(): pl.pallas_call(whole, out_shape=outs, in_specs=specs, out_specs=jax.tree....]
    ppermute x6 -> x3, starting transfers between devices: 6.97 us -> 2.75 us  [middle(): return lax.ppermute(values, 'tensor', [(2, 4), (3, 5), (4, 2), (5, 3)])]
  transfers between devices with their start and end apart: 33 -> 34, of which waited for: 9 -> 12; matrix products, arithmetic and copies ran while one was open for 4% -> 4% of each run, Pallas kernels for 19% -> 17%
where the time goes in v3:
time: 124 us; the launch traced here: 123 us
  waiting for transfers between devices  56.9 us (46%)
  Pallas kernels  30.5 us (25%)
  starting transfers between devices  29.3 us (24%)
  other arithmetic  5.22 us (4%)
    ppermute x31, waiting for transfers between devices, swap(): return lax.ppermute(values, axis, [(i, i ^ distance) for i in range(size)])  56.9 us
    pallas_call x9, Pallas kernels, call(): pl.pallas_call(whole, out_shape=outs, in_specs=specs, out_specs=jax.tree....  30.5 us
    ppermute x31, starting transfers between devices, swap(): return lax.ppermute(values, axis, [(i, i ^ distance) for i in range(size)])  26.6 us
    ppermute x3, starting transfers between devices, middle(): return lax.ppermute(values, 'tensor', [(2, 4), (3, 5), (4, 2), (5, 3)])  2.75 us
    mul x1, other arithmetic, local_pairwise(): sines = jnp.where(lanes[None, :] < half, -1.0, 1.0) * jnp.sin(angles)  2.58 us
  transfers between devices with their start and end apart: 34, of which 12 were waited for; matrix products, arithmetic and copies ran while one was open for 4% of the time, Pallas kernels for 17%

profile of v3, /device:TPU:0, one launch (start us, length us, event | category | flops | bytes accessed | tf_op | source)
XLA Modules:
  0.0 123.4 jit_solution(15222219103869230989)
XLA Ops:
  0.6 3.1 %shard_map.172.refs_2_.refs_21_ = bf16[512,640]{1,0:T(8,128)(2,1)} custom-call(s32[2]{0:T(128)} %pad_add_fusion.refs_0_.refs_23_, bf16[256,256]{1,0:T(8,128)(2,1)} %bitcast.27, bf16[256,384]{1,0:T(8,128)(2,1)} %bitcast.26, bf16[256,1280]{1,0:T(8,128)(2,1)} %bitcast.25, f32[1,128]{1,0:T(1,128)} %bitcast.23), custom_call_target="tpu_custom_call" | custom-call | tf_op jit(solution)/shard_map/pallas_call | solution.py:249
  3.6 3.0 %collective-permute-start.10 = (bf16[512,640]{1,0:T(8,128)(2,1)}, bf16[512,640]{1,0:T(8,128)(2,1)S(1)}, u32[]{:S(2)}, u32[]{:S(2)}) collective-permute-start(bf16[512,640]{1,0:T(8,128)(2,1)} %shard_map.172.refs_2_.refs_21_), channel_id=1, source_target_pairs={{0,16},{8,24},{16,0},{24,8},{1,17},{9,25},{17,1},{25,9},{2,18},{10... | collective-permute-start | bytes 1966088 | tf_op jit(solution)/shard_map/ppermute | solution.py:540
  6.7 1.5 %collective-permute-start.9 = (bf16[512,640]{1,0:T(8,128)(2,1)}, bf16[512,640]{1,0:T(8,128)(2,1)S(1)}, u32[]{:S(2)}, u32[]{:S(2)}) collective-permute-start(bf16[512,640]{1,0:T(8,128)(2,1)} %shard_map.172.refs_2_.refs_21_), channel_id=1, source_target_pairs={{0,8},{8,0},{16,24},{24,16},{1,9},{9,1},{17,25},{25,17},{2,10},{10... | collective-permute-start | bytes 1966088 | tf_op jit(solution)/shard_map/ppermute | solution.py:540
  8.2 2.7 %collective-permute-start.3 = (bf16[160,1280]{1,0:T(8,128)(2,1)S(1)}, bf16[160,1280]{1,0:T(8,128)(2,1)S(1)}, u32[]{:S(2)}, u32[]{:S(2)}) collective-permute-start(bf16[160,1280]{1,0:T(8,128)(2,1)S(1)} %pad_maximum_fusion.refs_4_.refs_11_), channel_id=1, source_target_pairs={{0,4},{1,5},{2,6},{3,7},{4,0},{5,1},{6,2},{7,3},{8,12},{9,13},{10,... | collective-permute-start | bytes 1228808 | tf_op jit(solution)/shard_map/ppermute | solution.py:540
  10.9 1.6 %collective-permute-start.1 = (bf16[160,1280]{1,0:T(8,128)(2,1)S(1)}, bf16[160,1280]{1,0:T(8,128)(2,1)S(1)}, u32[]{:S(2)}, u32[]{:S(2)}) collective-permute-start(bf16[160,1280]{1,0:T(8,128)(2,1)S(1)} %pad_maximum_fusion.refs_4_.refs_11_), channel_id=1, source_target_pairs={{0,2},{1,3},{2,0},{3,1},{4,6},{5,7},{6,4},{7,5},{8,10},{9,11},{10,... | collective-permute-start | bytes 1228808 | tf_op jit(solution)/shard_map/ppermute | solution.py:540
  12.5 1.4 %collective-permute-start.5 = (bf16[160,1280]{1,0:T(8,128)(2,1)S(1)}, bf16[160,1280]{1,0:T(8,128)(2,1)}, u32[]{:S(2)}, u32[]{:S(2)}) collective-permute-start(bf16[160,1280]{1,0:T(8,128)(2,1)S(1)} %pad_maximum_fusion.refs_4_.refs_11_), channel_id=1, source_target_pairs={{2,4},{3,5},{4,2},{5,3},{10,12},{11,13},{12,10},{13,11},{18,20},{1... | collective-permute-start | bytes 1228808 | tf_op jit(solution)/shard_map/ppermute | solution.py:544
  14.8 0.8 copy.20.refs_3_
  15.5 2.6 %fusion = (f32[1024,128]{1,0:T(8,128)S(1)}, f32[1024,128]{1,0:T(8,128)S(1)}) fusion(f32[128]{0:T(128)} %get-tuple-element.39, f32[128]{0:T(128)} %get-tuple-element.40, f32[1024]{0:T(1024)S(1)} %convert_add_fusion), kind=kLoop, calls=%fused_computation.5 | loop fusion | flops 262144 | bytes 1053696 | tf_op jit(solution)/shard_map/mul | solution.py:583
  18.1 11.7 %collective-permute-done.3.refs_8_.refs_11_ = bf16[160,1280]{1,0:T(8,128)(2,1)S(1)} collective-permute-done((bf16[160,1280]{1,0:T(8,128)(2,1)S(1)}, bf16[160,1280]{1,0:T(8,128)(2,1)S(1)}, u32[]{:S(2)}, u32[]{:S(2)}) %collective-permute-start.3) | collective-permute-done | bytes 409632 | tf_op jit(solution)/shard_map/ppermute | solution.py:540
  31.3 10.5 %collective-permute-done.6.refs_11_.refs_12_ = bf16[160,1280]{1,0:T(8,128)(2,1)S(1)} collective-permute-done((bf16[160,1280]{1,0:T(8,128)(2,1)S(1)}, bf16[160,1280]{1,0:T(8,128)(2,1)S(1)}, u32[]{:S(2)}, u32[]{:S(2)}) %collective-permute-start.6) | collective-permute-done | bytes 409632 | tf_op jit(solution)/shard_map/ppermute | solution.py:540
  42.4 0.9 fusion.1
  43.4 1.1 shard_map.173
  46.2 2.5 %collective-permute-start.19 = (bf16[4,32,1280]{2,1,0:T(8,128)(2,1)S(1)}, bf16[4,32,1280]{2,1,0:T(8,128)(2,1)S(1)}, u32[]{:S(2)}, u32[]{:S(2)}) collective-permute-start(bf16[4,32,1280]{2,1,0:T(8,128)(2,1)S(1)} %pad_maximum_fusion.1.refs_1_), channel_id=1, source_target_pairs={{0,24},{8,16},{16,8},{24,0},{1,25},{9,17},{17,9},{25,1},{2,26},{10... | collective-permute-start | bytes 983048 | tf_op jit(solution)/shard_map/ppermute | solution.py:540
  48.7 9.0 %shard_map.174.refs_1_ = bf16[1024,128]{1,0:T(8,128)(2,1)S(1)} custom-call(s32[2]{0:T(128)S(1)} %copy-done.2, s32[1,8]{1,0:T(1,128)S(1)} %copy-done.9, s32[1,8]{1,0:T(1,128)S(1)} %copy-done.10, s32[32,4]{1,0:T(8,128)S(1)} %copy.20.refs_3_, bf16[160,1280]{1,0:T(8,128)(2,1)S(1)} %pad_maximum_fusion.refs_4_.refs_11_, ...), custom_call_target="tpu_custom_call" | custom-call | flops 20000000000 | bytes 2000000 | tf_op jit(solution)/shard_map/pallas_call | solution.py:249
  58.1 2.6 %collective-permute-start.16 = (bf16[1024,128]{1,0:T(8,128)(2,1)S(1)}, bf16[1024,128]{1,0:T(8,128)(2,1)S(1)}, u32[]{:S(2)}, u32[]{:S(2)}) collective-permute-start(bf16[1024,128]{1,0:T(8,128)(2,1)S(1)} %shard_map.174.refs_1_), channel_id=1, source_target_pairs={{0,4},{1,5},{2,6},{3,7},{4,0},{5,1},{6,2},{7,3},{8,12},{9,13},{10,... | collective-permute-start | bytes 786440 | tf_op jit(solution)/shard_map/ppermute | solution.py:540
  60.8 1.3 %collective-permute-done.18.refs_3_ = bf16[4,32,1280]{2,1,0:T(8,128)(2,1)S(1)} collective-permute-done((bf16[4,32,1280]{2,1,0:T(8,128)(2,1)S(1)}, bf16[4,32,1280]{2,1,0:T(8,128)(2,1)S(1)}, u32[]{:S(2)}, u32[]{:S(2)}) %collective-permute-start.18) | collective-permute-done | bytes 327712 | tf_op jit(solution)/shard_map/ppermute | solution.py:540
  62.1 8.5 %collective-permute-done.15.refs_3_ = bf16[1024,128]{1,0:T(8,128)(2,1)S(1)} collective-permute-done((bf16[1024,128]{1,0:T(8,128)(2,1)S(1)}, bf16[1024,128]{1,0:T(8,128)(2,1)S(1)}, u32[]{:S(2)}, u32[]{:S(2)}) %collective-permute-start.15) | collective-permute-done | bytes 262176 | tf_op jit(solution)/shard_map/ppermute | solution.py:540
  70.6 1.3 %collective-permute-done.16.refs_5_ = bf16[1024,128]{1,0:T(8,128)(2,1)S(1)} collective-permute-done((bf16[1024,128]{1,0:T(8,128)(2,1)S(1)}, bf16[1024,128]{1,0:T(8,128)(2,1)S(1)}, u32[]{:S(2)}, u32[]{:S(2)}) %collective-permute-start.16) | collective-permute-done | bytes 262176 | tf_op jit(solution)/shard_map/ppermute | solution.py:540
  72.6 0.7 collective-permute-start.22
  73.9 1.8 %collective-permute-start.24 = (bf16[1024,128]{1,0:T(8,128)(2,1)S(1)}, bf16[1024,128]{1,0:T(8,128)(2,1)S(1)}, u32[]{:S(2)}, u32[]{:S(2)}) collective-permute-start(bf16[1024,128]{1,0:T(8,128)(2,1)S(1)} %collective-permute-done.16.refs_5_), channel_id=1, source_target_pairs={{0,2},{1,3},{2,0},{3,1},{4,6},{5,7},{6,4},{7,5},{8,10},{9,11},{10,... | collective-permute-start | bytes 786440 | tf_op jit(solution)/shard_map/ppermute | solution.py:540
  76.2 6.2 %collective-permute-done.24.refs_9_ = bf16[1024,128]{1,0:T(8,128)(2,1)S(1)} collective-permute-done((bf16[1024,128]{1,0:T(8,128)(2,1)S(1)}, bf16[1024,128]{1,0:T(8,128)(2,1)S(1)}, u32[]{:S(2)}, u32[]{:S(2)}) %collective-permute-start.24) | collective-permute-done | bytes 262176 | tf_op jit(solution)/shard_map/ppermute | solution.py:540
  82.5 1.4 %collective-permute-done.25.refs_10_ = bf16[1024,128]{1,0:T(8,128)(2,1)S(1)} collective-permute-done((bf16[1024,128]{1,0:T(8,128)(2,1)S(1)}, bf16[1024,128]{1,0:T(8,128)(2,1)S(1)}, u32[]{:S(2)}, u32[]{:S(2)}) %collective-permute-start.25) | collective-permute-done | bytes 262176 | tf_op jit(solution)/shard_map/ppermute | solution.py:540
  84.0 4.2 %shard_map.176 = (bf16[128,1280]{1,0:T(8,128)(2,1)S(1)}, bf16[128,1280]{1,0:T(8,128)(2,1)S(1)}) custom-call(s32[2]{0:T(128)S(1)} %copy-done.2, bf16[1024,128]{1,0:T(8,128)(2,1)S(1)} %shard_map.174.refs_1_, bf16[1024,128]{1,0:T(8,128)(2,1)S(1)} %collective-permute-done.14.refs_2_, bf16[1024,128]{1,0:T(8,128)(2,1)S(1)} %collective-permute-done.15.refs_3_, ...), custom_call_target="tpu_custom_call" | custom-call | flops 20000000000 | bytes 10000000 | tf_op jit(solution)/shard_map/pallas_call | solution.py:249
  88.4 1.5 %collective-permute-done.27 = bf16[128,1280]{1,0:T(8,128)(2,1)S(1)} collective-permute-done((bf16[128,1280]{1,0:T(8,128)(2,1)S(1)}, bf16[128,1280]{1,0:T(8,128)(2,1)S(1)}, u32[]{:S(2)}, u32[]{:S(2)}) %collective-permute-start.27) | collective-permute-done | bytes 327712 | tf_op jit(solution)/shard_map/ppermute | solution.py:540
  90.0 1.9 %collective-permute-start.28 = (bf16[128,1280]{1,0:T(8,128)(2,1)S(1)}, bf16[128,1280]{1,0:T(8,128)(2,1)S(1)}, u32[]{:S(2)}, u32[]{:S(2)}) collective-permute-start(bf16[128,1280]{1,0:T(8,128)(2,1)S(1)} %add_convert_fusion.2), channel_id=1, source_target_pairs={{0,2},{1,3},{2,0},{3,1},{4,6},{5,7},{6,4},{7,5},{8,10},{9,11},{10,... | collective-permute-start | bytes 983048 | tf_op jit(solution)/shard_map/ppermute | solution.py:540
  92.6 6.8 %shard_map.177 = (bf16[256,1280]{1,0:T(8,128)(2,1)S(1)}, bf16[256,1280]{1,0:T(8,128)(2,1)S(1)}) custom-call(s32[2]{0:T(128)S(1)} %copy-done.2, bf16[1024,128]{1,0:T(8,128)(2,1)S(1)} %shard_map.174.refs_1_, bf16[1024,128]{1,0:T(8,128)(2,1)S(1)} %collective-permute-done.14.refs_2_, bf16[1024,128]{1,0:T(8,128)(2,1)S(1)} %collective-permute-done.15.refs_3_, ...), custom_call_target="tpu_custom_call" | custom-call | flops 20000000000 | bytes 10000000 | tf_op jit(solution)/shard_map/pallas_call | solution.py:249
  100.6 1.0 collective-permute-done.31
  101.7 3.0 %collective-permute-start.32 = (bf16[128,1280]{1,0:T(8,128)(2,1)S(1)}, bf16[128,1280]{1,0:T(8,128)(2,1)S(1)}, u32[]{:S(2)}, u32[]{:S(2)}) collective-permute-start(bf16[128,1280]{1,0:T(8,128)(2,1)S(1)} %get-tuple-element.36), channel_id=1, source_target_pairs={{0,2},{1,3},{2,0},{3,1},{4,6},{5,7},{6,4},{7,5},{8,10},{9,11},{10,... | collective-permute-start | bytes 983048 | tf_op jit(solution)/shard_map/ppermute | solution.py:540
  105.4 3.7 %shard_map.179 = (bf16[128,1280]{1,0:T(8,128)(2,1)S(1)}, bf16[128,1280]{1,0:T(8,128)(2,1)S(1)}, bf16[128,1280]{1,0:T(8,128)(2,1)S(1)}) custom-call(s32[2]{0:T(128)S(1)} %copy-done.2, bf16[1024,128]{1,0:T(8,128)(2,1)S(1)} %shard_map.174.refs_1_, bf16[1024,128]{1,0:T(8,128)(2,1)S(1)} %collective-permute-done.14.refs_2_, ...), custom_call_target="tpu_custom_call" | custom-call | flops 20000000000 | bytes 10000000 | tf_op jit(solution)/shard_map/pallas_call | solution.py:249
  109.2 9.4 %collective-permute-done.32.refs_3_ = bf16[128,1280]{1,0:T(8,128)(2,1)S(1)} collective-permute-done((bf16[128,1280]{1,0:T(8,128)(2,1)S(1)}, bf16[128,1280]{1,0:T(8,128)(2,1)S(1)}, u32[]{:S(2)}, u32[]{:S(2)}) %collective-permute-start.32) | collective-permute-done | bytes 327712 | tf_op jit(solution)/shard_map/ppermute | solution.py:540
  118.6 3.5 %collective-permute-done.33.refs_4_ = bf16[128,1280]{1,0:T(8,128)(2,1)S(1)} collective-permute-done((bf16[128,1280]{1,0:T(8,128)(2,1)S(1)}, bf16[128,1280]{1,0:T(8,128)(2,1)S(1)}, u32[]{:S(2)}, u32[]{:S(2)}) %collective-permute-start.33) | collective-permute-done | bytes 327712 | tf_op jit(solution)/shard_map/ppermute | solution.py:540
  122.2 1.2 shard_map.180
  (100 shorter events, 10.4 us)
Async XLA Ops:
  3.6 26.2 %collective-permute-start.10 = (bf16[512,640]{1,0:T(8,128)(2,1)}, bf16[512,640]{1,0:T(8,128)(2,1)S(1)}, u32[]{:S(2)}, u32[]{:S(2)}) collective-permute-start(bf16[512,640]{1,0:T(8,128)(2,1)} %shard_map.172.refs_2_.refs_21_), channel_id=1, source_target_pairs={{0,16},{8,24},{16,0},{24,8},{1,17},{9,25},{17,1},{25,9},{2,18},{10... | collective-permute-start | bytes 1966088 | tf_op jit(solution)/shard_map/ppermute | solution.py:540
  6.7 23.3 %collective-permute-start.9 = (bf16[512,640]{1,0:T(8,128)(2,1)}, bf16[512,640]{1,0:T(8,128)(2,1)S(1)}, u32[]{:S(2)}, u32[]{:S(2)}) collective-permute-start(bf16[512,640]{1,0:T(8,128)(2,1)} %shard_map.172.refs_2_.refs_21_), channel_id=1, source_target_pairs={{0,8},{8,0},{16,24},{24,16},{1,9},{9,1},{17,25},{25,17},{2,10},{10... | collective-permute-start | bytes 1966088 | tf_op jit(solution)/shard_map/ppermute | solution.py:540
  8.2 21.6 %collective-permute-start.3 = (bf16[160,1280]{1,0:T(8,128)(2,1)S(1)}, bf16[160,1280]{1,0:T(8,128)(2,1)S(1)}, u32[]{:S(2)}, u32[]{:S(2)}) collective-permute-start(bf16[160,1280]{1,0:T(8,128)(2,1)S(1)} %pad_maximum_fusion.refs_4_.refs_11_), channel_id=1, source_target_pairs={{0,4},{1,5},{2,6},{3,7},{4,0},{5,1},{6,2},{7,3},{8,12},{9,13},{10,... | collective-permute-start | bytes 1228808 | tf_op jit(solution)/shard_map/ppermute | solution.py:540
  10.9 19.7 %collective-permute-start.1 = (bf16[160,1280]{1,0:T(8,128)(2,1)S(1)}, bf16[160,1280]{1,0:T(8,128)(2,1)S(1)}, u32[]{:S(2)}, u32[]{:S(2)}) collective-permute-start(bf16[160,1280]{1,0:T(8,128)(2,1)S(1)} %pad_maximum_fusion.refs_4_.refs_11_), channel_id=1, source_target_pairs={{0,2},{1,3},{2,0},{3,1},{4,6},{5,7},{6,4},{7,5},{8,10},{9,11},{10,... | collective-permute-start | bytes 1228808 | tf_op jit(solution)/shard_map/ppermute | solution.py:540
  12.5 18.7 %collective-permute-start.5 = (bf16[160,1280]{1,0:T(8,128)(2,1)S(1)}, bf16[160,1280]{1,0:T(8,128)(2,1)}, u32[]{:S(2)}, u32[]{:S(2)}) collective-permute-start(bf16[160,1280]{1,0:T(8,128)(2,1)S(1)} %pad_maximum_fusion.refs_4_.refs_11_), channel_id=1, source_target_pairs={{2,4},{3,5},{4,2},{5,3},{10,12},{11,13},{12,10},{13,11},{18,20},{1... | collective-permute-start | bytes 1228808 | tf_op jit(solution)/shard_map/ppermute | solution.py:544
  29.9 14.6 %collective-permute-start = (bf16[160,1280]{1,0:T(8,128)(2,1)S(1)}, bf16[160,1280]{1,0:T(8,128)(2,1)S(1)}, u32[]{:S(2)}, u32[]{:S(2)}) collective-permute-start(bf16[160,1280]{1,0:T(8,128)(2,1)S(1)} %pad_maximum_fusion.refs_4_.refs_11_), channel_id=1, source_target_pairs={{0,1},{1,0},{2,3},{3,2},{4,5},{5,4},{6,7},{7,6},{8,9},{9,8},{10,11... | collective-permute-start | bytes 1228808 | tf_op jit(solution)/shard_map/ppermute | solution.py:540
  29.9 11.9 %collective-permute-start.6 = (bf16[160,1280]{1,0:T(8,128)(2,1)S(1)}, bf16[160,1280]{1,0:T(8,128)(2,1)S(1)}, u32[]{:S(2)}, u32[]{:S(2)}) collective-permute-start(bf16[160,1280]{1,0:T(8,128)(2,1)S(1)} %collective-permute-done.3.refs_8_.refs_11_), channel_id=1, source_target_pairs={{0,2},{1,3},{2,0},{3,1},{4,6},{5,7},{6,4},{7,5},{8,10},{9,11},{10,... | collective-permute-start | bytes 1228808 | tf_op jit(solution)/shard_map/ppermute | solution.py:540
  30.0 11.8 %collective-permute-start.11 = (bf16[256,640]{1,0:T(8,128)(2,1)S(1)}, bf16[256,640]{1,0:T(8,128)(2,1)S(1)}, u32[]{:S(2)}, u32[]{:S(2)}) collective-permute-start(bf16[256,640]{1,0:T(8,128)(2,1)S(1)} %slice.36), channel_id=1, source_target_pairs={{0,8},{8,0},{16,24},{24,16},{1,9},{9,1},{17,25},{25,17},{2,10},{10... | collective-permute-start | bytes 983048 | tf_op jit(solution)/shard_map/ppermute | solution.py:540
  30.6 11.7 %collective-permute-start.12 = (bf16[256,640]{1,0:T(8,128)(2,1)S(1)}, bf16[256,640]{1,0:T(8,128)(2,1)S(1)}, u32[]{:S(2)}, u32[]{:S(2)}) collective-permute-start(bf16[256,640]{1,0:T(8,128)(2,1)S(1)} %slice.37), channel_id=1, source_target_pairs={{0,16},{8,24},{16,0},{24,8},{1,17},{9,25},{17,1},{25,9},{2,18},{10... | collective-permute-start | bytes 983048 | tf_op jit(solution)/shard_map/ppermute | solution.py:540
  31.2 13.8 %collective-permute-start.4 = (bf16[160,1280]{1,0:T(8,128)(2,1)S(1)}, bf16[160,1280]{1,0:T(8,128)(2,1)S(1)}, u32[]{:S(2)}, u32[]{:S(2)}) collective-permute-start(bf16[160,1280]{1,0:T(8,128)(2,1)S(1)} %collective-permute-done.3.refs_8_.refs_11_), channel_id=1, source_target_pairs={{0,1},{1,0},{2,3},{3,2},{4,5},{5,4},{6,7},{7,6},{8,9},{9,8},{10,11... | collective-permute-start | bytes 1228808 | tf_op jit(solution)/shard_map/ppermute | solution.py:540
  41.8 3.8 %collective-permute-start.2 = (bf16[160,1280]{1,0:T(8,128)(2,1)S(1)}, bf16[160,1280]{1,0:T(8,128)(2,1)S(1)}, u32[]{:S(2)}, u32[]{:S(2)}) collective-permute-start(bf16[160,1280]{1,0:T(8,128)(2,1)S(1)} %collective-permute-done.1.refs_6_.refs_13_), channel_id=1, source_target_pairs={{0,1},{1,0},{2,3},{3,2},{4,5},{5,4},{6,7},{7,6},{8,9},{9,8},{10,11... | collective-permute-start | bytes 1228808 | tf_op jit(solution)/shard_map/ppermute | solution.py:540
  41.8 4.3 %collective-permute-start.7 = (bf16[160,1280]{1,0:T(8,128)(2,1)}, bf16[160,1280]{1,0:T(8,128)(2,1)S(1)}, u32[]{:S(2)}, u32[]{:S(2)}) collective-permute-start(bf16[160,1280]{1,0:T(8,128)(2,1)} %collective-permute-done.5.refs_10_.refs_11_), channel_id=1, source_target_pairs={{0,1},{1,0},{2,3},{3,2},{4,5},{5,4},{6,7},{7,6},{8,9},{9,8},{10,11... | collective-permute-start | bytes 1228808 | tf_op jit(solution)/shard_map/ppermute | solution.py:540
  42.3 6.3 %collective-permute-start.8 = (bf16[160,1280]{1,0:T(8,128)(2,1)S(1)}, bf16[160,1280]{1,0:T(8,128)(2,1)S(1)}, u32[]{:S(2)}, u32[]{:S(2)}) collective-permute-start(bf16[160,1280]{1,0:T(8,128)(2,1)S(1)} %collective-permute-done.6.refs_11_.refs_12_), channel_id=1, source_target_pairs={{0,1},{1,0},{2,3},{3,2},{4,5},{5,4},{6,7},{7,6},{8,9},{9,8},{10,11... | collective-permute-start | bytes 1228808 | tf_op jit(solution)/shard_map/ppermute | solution.py:540
  44.5 4.1 %collective-permute-start.13 = (bf16[64,1280]{1,0:T(8,128)(2,1)S(1)}, bf16[64,1280]{1,0:T(8,128)(2,1)S(1)}, u32[]{:S(2)}, u32[]{:S(2)}) collective-permute-start(bf16[64,1280]{1,0:T(8,128)(2,1)S(1)} %get-tuple-element.20.refs_15_), channel_id=1, source_target_pairs={{0,1},{1,0},{2,3},{3,2},{4,5},{5,4},{6,7},{7,6},{8,9},{9,8},{10,11... | collective-permute-start | bytes 491528 | tf_op jit(solution)/shard_map/ppermute | solution.py:540
  45.1 15.7 %collective-permute-start.17 = (bf16[4,32,1280]{2,1,0:T(8,128)(2,1)S(1)}, bf16[4,32,1280]{2,1,0:T(8,128)(2,1)S(1)}, u32[]{:S(2)}, u32[]{:S(2)}) collective-permute-start(bf16[4,32,1280]{2,1,0:T(8,128)(2,1)S(1)} %pad_maximum_fusion.1.refs_1_), channel_id=1, source_target_pairs={{0,8},{8,0},{16,24},{24,16},{1,9},{9,1},{17,25},{25,17},{2,10},{10... | collective-permute-start | bytes 983048 | tf_op jit(solution)/shard_map/ppermute | solution.py:540
  45.7 16.4 %collective-permute-start.18 = (bf16[4,32,1280]{2,1,0:T(8,128)(2,1)S(1)}, bf16[4,32,1280]{2,1,0:T(8,128)(2,1)S(1)}, u32[]{:S(2)}, u32[]{:S(2)}) collective-permute-start(bf16[4,32,1280]{2,1,0:T(8,128)(2,1)S(1)} %pad_maximum_fusion.1.refs_1_), channel_id=1, source_target_pairs={{0,16},{8,24},{16,0},{24,8},{1,17},{9,25},{17,1},{25,9},{2,18},{10... | collective-permute-start | bytes 983048 | tf_op jit(solution)/shard_map/ppermute | solution.py:540
  46.2 15.9 %collective-permute-start.19 = (bf16[4,32,1280]{2,1,0:T(8,128)(2,1)S(1)}, bf16[4,32,1280]{2,1,0:T(8,128)(2,1)S(1)}, u32[]{:S(2)}, u32[]{:S(2)}) collective-permute-start(bf16[4,32,1280]{2,1,0:T(8,128)(2,1)S(1)} %pad_maximum_fusion.1.refs_1_), channel_id=1, source_target_pairs={{0,24},{8,16},{16,8},{24,0},{1,25},{9,17},{17,9},{25,1},{2,26},{10... | collective-permute-start | bytes 983048 | tf_op jit(solution)/shard_map/ppermute | solution.py:540
  57.8 12.8 %collective-permute-start.15 = (bf16[1024,128]{1,0:T(8,128)(2,1)S(1)}, bf16[1024,128]{1,0:T(8,128)(2,1)S(1)}, u32[]{:S(2)}, u32[]{:S(2)}) collective-permute-start(bf16[1024,128]{1,0:T(8,128)(2,1)S(1)} %shard_map.174.refs_1_), channel_id=1, source_target_pairs={{0,2},{1,3},{2,0},{3,1},{4,6},{5,7},{6,4},{7,5},{8,10},{9,11},{10,... | collective-permute-start | bytes 786440 | tf_op jit(solution)/shard_map/ppermute | solution.py:540
  58.1 13.8 %collective-permute-start.16 = (bf16[1024,128]{1,0:T(8,128)(2,1)S(1)}, bf16[1024,128]{1,0:T(8,128)(2,1)S(1)}, u32[]{:S(2)}, u32[]{:S(2)}) collective-permute-start(bf16[1024,128]{1,0:T(8,128)(2,1)S(1)} %shard_map.174.refs_1_), channel_id=1, source_target_pairs={{0,4},{1,5},{2,6},{3,7},{4,0},{5,1},{6,2},{7,3},{8,12},{9,13},{10,... | collective-permute-start | bytes 786440 | tf_op jit(solution)/shard_map/ppermute | solution.py:540
  72.6 11.4 %collective-permute-start.26 = (bf16[512,1280]{1,0:T(8,128)(2,1)S(1)}, bf16[512,1280]{1,0:T(8,128)(2,1)S(1)}, u32[]{:S(2)}, u32[]{:S(2)}) collective-permute-start(bf16[512,1280]{1,0:T(8,128)(2,1)S(1)} %bitcast.19), channel_id=1, source_target_pairs={{0,1},{1,0},{2,3},{3,2},{4,5},{5,4},{6,7},{7,6},{8,9},{9,8},{10,11... | collective-permute-start | bytes 3932168 | tf_op jit(solution)/shard_map/ppermute | solution.py:540
  72.6 3.1 %collective-permute-start.22 = (bf16[1024,128]{1,0:T(8,128)(2,1)S(1)}, bf16[1024,128]{1,0:T(8,128)(2,1)S(1)}, u32[]{:S(2)}, u32[]{:S(2)}) collective-permute-start(bf16[1024,128]{1,0:T(8,128)(2,1)S(1)} %shard_map.174.refs_1_), channel_id=1, source_target_pairs={{2,4},{3,5},{4,2},{5,3},{10,12},{11,13},{12,10},{13,11},{18,20},{1... | collective-permute-start | bytes 786440 | tf_op jit(solution)/shard_map/ppermute | solution.py:544
  73.3 2.9 %collective-permute-start.14 = (bf16[1024,128]{1,0:T(8,128)(2,1)S(1)}, bf16[1024,128]{1,0:T(8,128)(2,1)S(1)}, u32[]{:S(2)}, u32[]{:S(2)}) collective-permute-start(bf16[1024,128]{1,0:T(8,128)(2,1)S(1)} %shard_map.174.refs_1_), channel_id=1, source_target_pairs={{0,1},{1,0},{2,3},{3,2},{4,5},{5,4},{6,7},{7,6},{8,9},{9,8},{10,11... | collective-permute-start | bytes 786440 | tf_op jit(solution)/shard_map/ppermute | solution.py:540
  73.9 8.6 %collective-permute-start.24 = (bf16[1024,128]{1,0:T(8,128)(2,1)S(1)}, bf16[1024,128]{1,0:T(8,128)(2,1)S(1)}, u32[]{:S(2)}, u32[]{:S(2)}) collective-permute-start(bf16[1024,128]{1,0:T(8,128)(2,1)S(1)} %collective-permute-done.16.refs_5_), channel_id=1, source_target_pairs={{0,2},{1,3},{2,0},{3,1},{4,6},{5,7},{6,4},{7,5},{8,10},{9,11},{10,... | collective-permute-start | bytes 786440 | tf_op jit(solution)/shard_map/ppermute | solution.py:540
  75.7 6.8 %collective-permute-start.21 = (bf16[1024,128]{1,0:T(8,128)(2,1)S(1)}, bf16[1024,128]{1,0:T(8,128)(2,1)S(1)}, u32[]{:S(2)}, u32[]{:S(2)}) collective-permute-start(bf16[1024,128]{1,0:T(8,128)(2,1)S(1)} %collective-permute-done.16.refs_5_), channel_id=1, source_target_pairs={{0,1},{1,0},{2,3},{3,2},{4,5},{5,4},{6,7},{7,6},{8,9},{9,8},{10,11... | collective-permute-start | bytes 786440 | tf_op jit(solution)/shard_map/ppermute | solution.py:540
  75.7 6.8 %collective-permute-start.20 = (bf16[1024,128]{1,0:T(8,128)(2,1)S(1)}, bf16[1024,128]{1,0:T(8,128)(2,1)S(1)}, u32[]{:S(2)}, u32[]{:S(2)}) collective-permute-start(bf16[1024,128]{1,0:T(8,128)(2,1)S(1)} %collective-permute-done.15.refs_3_), channel_id=1, source_target_pairs={{0,1},{1,0},{2,3},{3,2},{4,5},{5,4},{6,7},{7,6},{8,9},{9,8},{10,11... | collective-permute-start | bytes 786440 | tf_op jit(solution)/shard_map/ppermute | solution.py:540
  76.2 6.3 %collective-permute-start.23 = (bf16[1024,128]{1,0:T(8,128)(2,1)S(1)}, bf16[1024,128]{1,0:T(8,128)(2,1)S(1)}, u32[]{:S(2)}, u32[]{:S(2)}) collective-permute-start(bf16[1024,128]{1,0:T(8,128)(2,1)S(1)} %collective-permute-done.22.refs_7_), channel_id=1, source_target_pairs={{0,1},{1,0},{2,3},{3,2},{4,5},{5,4},{6,7},{7,6},{8,9},{9,8},{10,11... | collective-permute-start | bytes 786440 | tf_op jit(solution)/shard_map/ppermute | solution.py:540
  90.0 9.9 %collective-permute-start.28 = (bf16[128,1280]{1,0:T(8,128)(2,1)S(1)}, bf16[128,1280]{1,0:T(8,128)(2,1)S(1)}, u32[]{:S(2)}, u32[]{:S(2)}) collective-permute-start(bf16[128,1280]{1,0:T(8,128)(2,1)S(1)} %add_convert_fusion.2), channel_id=1, source_target_pairs={{0,2},{1,3},{2,0},{3,1},{4,6},{5,7},{6,4},{7,5},{8,10},{9,11},{10,... | collective-permute-start | bytes 983048 | tf_op jit(solution)/shard_map/ppermute | solution.py:540
  91.9 8.0 %collective-permute-start.29 = (bf16[128,1280]{1,0:T(8,128)(2,1)S(1)}, bf16[128,1280]{1,0:T(8,128)(2,1)S(1)}, u32[]{:S(2)}, u32[]{:S(2)}) collective-permute-start(bf16[128,1280]{1,0:T(8,128)(2,1)S(1)} %add_convert_fusion.2), channel_id=1, source_target_pairs={{2,4},{3,5},{4,2},{5,3},{10,12},{11,13},{12,10},{13,11},{18,20},{1... | collective-permute-start | bytes 983048 | tf_op jit(solution)/shard_map/ppermute | solution.py:544
  99.4 2.2 %collective-permute-start.31 = (bf16[256,1280]{1,0:T(8,128)(2,1)S(1)}, bf16[256,1280]{1,0:T(8,128)(2,1)S(1)}, u32[]{:S(2)}, u32[]{:S(2)}) collective-permute-start(bf16[256,1280]{1,0:T(8,128)(2,1)S(1)} %get-tuple-element.34), channel_id=1, source_target_pairs={{0,1},{1,0},{2,3},{3,2},{4,5},{5,4},{6,7},{7,6},{8,9},{9,8},{10,11... | collective-permute-start | bytes 1966088 | tf_op jit(solution)/shard_map/ppermute | solution.py:540
  101.7 16.9 %collective-permute-start.32 = (bf16[128,1280]{1,0:T(8,128)(2,1)S(1)}, bf16[128,1280]{1,0:T(8,128)(2,1)S(1)}, u32[]{:S(2)}, u32[]{:S(2)}) collective-permute-start(bf16[128,1280]{1,0:T(8,128)(2,1)S(1)} %get-tuple-element.36), channel_id=1, source_target_pairs={{0,2},{1,3},{2,0},{3,1},{4,6},{5,7},{6,4},{7,5},{8,10},{9,11},{10,... | collective-permute-start | bytes 983048 | tf_op jit(solution)/shard_map/ppermute | solution.py:540
  104.7 17.4 %collective-permute-start.33 = (bf16[128,1280]{1,0:T(8,128)(2,1)S(1)}, bf16[128,1280]{1,0:T(8,128)(2,1)S(1)}, u32[]{:S(2)}, u32[]{:S(2)}) collective-permute-start(bf16[128,1280]{1,0:T(8,128)(2,1)S(1)} %get-tuple-element.35), channel_id=1, source_target_pairs={{0,4},{1,5},{2,6},{3,7},{4,0},{5,1},{6,2},{7,3},{8,12},{9,13},{10,... | collective-permute-start | bytes 983048 | tf_op jit(solution)/shard_map/ppermute | solution.py:540
  109.1 13.0 %collective-permute-start.30 = (bf16[128,1280]{1,0:T(8,128)(2,1)S(1)}, bf16[128,1280]{1,0:T(8,128)(2,1)S(1)}, u32[]{:S(2)}, u32[]{:S(2)}) collective-permute-start(bf16[128,1280]{1,0:T(8,128)(2,1)S(1)} %get-tuple-element.33), channel_id=1, source_target_pairs={{0,1},{1,0},{2,3},{3,2},{4,5},{5,4},{6,7},{7,6},{8,9},{9,8},{10,11... | collective-permute-start | bytes 983048 | tf_op jit(solution)/shard_map/ppermute | solution.py:540
  (18 other events, 330.7 us)

commit v4 on v3

--- a/solution.py
+++ b/solution.py
@@ -487,17 +487,18 @@
         out[tile * 128 : tile * 128 + 128, :] = (jnp.where(low, left, right) / weight).astype(BF16)
 
 
-def collect_kernel(ids, o0, o1, o2, o3, out):
+def collect_kernel(ids, o0, o1, o2, o3, *outs):
     for m, part in enumerate((o0, o1, o2, o3)):
         spot = pl.multiple_of((ids[1] ^ m) * 32, 32)
         for j in range(4):
-            out[j, pl.ds(spot, 32), :] = part[j]
+            outs[j // 2][j % 2, pl.ds(spot, 32), :] = part[j]
 
 
 def mlp_kernel(js, ids, *refs):
     heads_in, refs = refs[:10], refs[10:]
     pieces, refs = row_pieces(ids, refs, js)
-    output, output_other, rate, up, gate, up_scale, gate_scale, down, _, keep, send, *rest = refs
+    matrices, refs = refs[:4], refs[4:]
+    rate, up, gate, up_scale, gate_scale, down, _, keep, send, *rest = refs
     direct = middle_chip(ids)
     for place, j in enumerate(js):
         spots = piece_spots(ids, j)
@@ -506,10 +507,12 @@
             return jnp.concatenate([heads[pl.ds(spot, 128), :] for spot in spots], axis=0)
 
         attn_sum = 0.0
-        for side, matrix in enumerate((output, output_other)):
+        for side in (0, 1):
             columns = [rows_of(heads_in[2 * distance + side]) for distance in range(4)]
             columns[3] = jnp.where(direct, columns[3], rows_of(heads_in[8 + side]))
-            attn_sum = attn_sum + dot(jnp.concatenate(columns, axis=1), matrix[...])
+            for half in (0, 1):
+                pair = jnp.concatenate(columns[2 * half : 2 * half + 2], axis=1)
+                attn_sum = attn_sum + dot(pair, matrices[2 * side + half][...])
         base = jnp.concatenate(pieces[2 * place : 2 * place + 2], axis=0).astype(F32)
         mixed = renorm(base + rate[...] * (renorm(attn_sum) - base)).astype(BF16)
         up_part = dot(mixed, up[...]) * up_scale[...]
@@ -527,8 +530,9 @@
     out[...] = keep[0:128, :].astype(F32) + jnp.where(middle_chip(ids), more, 0.0)
 
 
-def final_kernel(mixed, keep, got, r1, r2, r3, rate, out):
-    mlp_sum = keep[...].astype(F32) + got[...].astype(F32)
+def final_kernel(mixed, keep, got0, got1, r1, r2, r3, rate, out):
+    got = jnp.concatenate([got0[...], got1[...]], axis=0)
+    mlp_sum = keep[...].astype(F32) + got.astype(F32)
     for r in (r1, r2, r3):
         mlp_sum = mlp_sum + r[...].astype(F32)
     base = mixed[...].astype(F32)
@@ -647,23 +651,21 @@
         limit=24,
     )
 
-    heads2 = swap(attn, 4)
-    heads1 = swap(attn, 2)
-    heads1, heads2, *outputs = lax.optimization_barrier((heads1, heads2, *outputs))
+    heads2, heads1 = swap(attn, 4), swap(attn, 2)
     heads3, heads3f = middle(attn), swap(heads2, 2)
     all_heads = [attn, swap(attn, 1), heads1, swap(heads1, 1), heads2, swap(heads2, 1)]
     all_heads += [heads3, swap(heads3, 1), heads3f, swap(heads3f, 1)]
 
-    output_own = call(
+    collected = call(
         collect_kernel,
-        jax.ShapeDtypeStruct((4, 4 * quarter, MODEL_WIDTH), BF16),
+        (jax.ShapeDtypeStruct((2, 4 * quarter, MODEL_WIDTH), BF16),) * 2,
         (ids, *outputs),
         1,
-        flops=0,
-        moved=0,
-    ).reshape(-1, MODEL_WIDTH)
+    )
+    collected = [part.reshape(-1, MODEL_WIDTH) for part in collected]
     weights = (
-        output_own, swap(output_own, 1), attention_rate.reshape(1, -1), up_matrix, gate_matrix,
+        *collected, *[swap(part, 1) for part in collected],
+        attention_rate.reshape(1, -1), up_matrix, gate_matrix,
         up_scaling.reshape(1, -1), gate_scaling.reshape(1, -1), down_matrix,
     )
     def update(js, previous):
@@ -696,12 +698,16 @@
         flops=2 * 10**10,
         unread=(3,),
     )
-    received2 = swap(chunk(joined, got[0:128]), 4)
-    keep0, send0, mixed = update((0,), joined)
+    chunk2 = chunk(joined, got[0:128])
+    received2 = swap(chunk2, 4)
+    keep0, send0, mixed = update((0,), chunk2)
     return call(
         final_kernel,
         shape(*hidden.shape),
-        (mixed, keep0, swap(send0, 1), received1, received2, received3, feedforward_rate.reshape(1, -1)),
+        (
+            mixed, keep0, swap(send0[0:64], 1), swap(send0[64:128], 1), received1, received2, received3,
+            feedforward_rate.reshape(1, -1),
+        ),
         0,
     )
 

time: 124 us -> 120 us (0.968)
  waiting for transfers between devices: 56.9 us -> 52.4 us
  Pallas kernels: 30.5 us -> 32 us
    ppermute x31 -> x33, waiting for transfers between devices: 56.9 us -> 52.4 us  [swap(): return lax.ppermute(values, axis, [(i, i ^ distance) for i in range(size)])]
    pallas_call x9, Pallas kernels: 30.5 us -> 32 us  [call(): pl.pallas_call(whole, out_shape=outs, in_specs=specs, out_specs=jax.tree....]
    ppermute x31 -> x33, starting transfers between devices: 26.6 us -> 26.2 us  [swap(): return lax.ppermute(values, axis, [(i, i ^ distance) for i in range(size)])]
  transfers between devices with their start and end apart: 34 -> 36, of which waited for: 12 -> 15; matrix products, arithmetic and copies ran while one was open for 4% -> 4% of each run, Pallas kernels for 17% -> 23%
where the time goes in v4:
time: 120 us
  waiting for transfers between devices  52.4 us (44%)
  Pallas kernels  32 us (27%)
  starting transfers between devices  28.2 us (24%)
  other arithmetic  5.38 us (4%)
  local copies, waits for them, and re-layouts  1.27 us (1%)
    ppermute x33, waiting for transfers between devices, swap(): return lax.ppermute(values, axis, [(i, i ^ distance) for i in range(size)])  52.4 us
    pallas_call x9, Pallas kernels, call(): pl.pallas_call(whole, out_shape=outs, in_specs=specs, out_specs=jax.tree....  32 us
    ppermute x33, starting transfers between devices, swap(): return lax.ppermute(values, axis, [(i, i ^ distance) for i in range(size)])  26.2 us
    mul x1, other arithmetic, local_pairwise(): sines = jnp.where(lanes[None, :] < half, -1.0, 1.0) * jnp.sin(angles)  2.59 us
  transfers between devices with their start and end apart: 36, of which 15 were waited for; matrix products, arithmetic and copies ran while one was open for 4% of the time, Pallas kernels for 23%

profile of v4, /device:TPU:0, one launch (start us, length us, event | category | flops | bytes accessed | tf_op | source)
XLA Modules:
  0.0 119.8 jit_solution(7201907359932995435)
XLA Ops:
  0.0 1.0 copy-done
  1.0 1.0 pad_maximum_fusion.refs_4_.refs_11_
  2.5 2.7 %collective-permute-start.1 = (bf16[160,1280]{1,0:T(8,128)(2,1)S(1)}, bf16[160,1280]{1,0:T(8,128)(2,1)S(1)}, u32[]{:S(2)}, u32[]{:S(2)}) collective-permute-start(bf16[160,1280]{1,0:T(8,128)(2,1)S(1)} %pad_maximum_fusion.refs_4_.refs_11_), channel_id=1, source_target_pairs={{0,2},{1,3},{2,0},{3,1},{4,6},{5,7},{6,4},{7,5},{8,10},{9,11},{10,... | collective-permute-start | bytes 1228808 | tf_op jit(solution)/shard_map/ppermute | solution.py:544
  5.2 2.6 %collective-permute-start.3 = (bf16[160,1280]{1,0:T(8,128)(2,1)S(1)}, bf16[160,1280]{1,0:T(8,128)(2,1)S(1)}, u32[]{:S(2)}, u32[]{:S(2)}) collective-permute-start(bf16[160,1280]{1,0:T(8,128)(2,1)S(1)} %pad_maximum_fusion.refs_4_.refs_11_), channel_id=1, source_target_pairs={{0,4},{1,5},{2,6},{3,7},{4,0},{5,1},{6,2},{7,3},{8,12},{9,13},{10,... | collective-permute-start | bytes 1228808 | tf_op jit(solution)/shard_map/ppermute | solution.py:544
  8.4 3.1 %shard_map.172.refs_2_.refs_21_ = bf16[512,640]{1,0:T(8,128)(2,1)} custom-call(s32[2]{0:T(128)} %pad_add_fusion.refs_0_.refs_25_, bf16[256,256]{1,0:T(8,128)(2,1)} %bitcast.32, bf16[256,384]{1,0:T(8,128)(2,1)} %bitcast.31, bf16[256,1280]{1,0:T(8,128)(2,1)} %bitcast.30, f32[1,128]{1,0:T(1,128)} %bitcast.20), custom_call_target="tpu_custom_call" | custom-call | tf_op jit(solution)/shard_map/pallas_call | solution.py:249
  11.5 1.6 %collective-permute-start.9 = (bf16[512,640]{1,0:T(8,128)(2,1)}, bf16[512,640]{1,0:T(8,128)(2,1)S(1)}, u32[]{:S(2)}, u32[]{:S(2)}) collective-permute-start(bf16[512,640]{1,0:T(8,128)(2,1)} %shard_map.172.refs_2_.refs_21_), channel_id=1, source_target_pairs={{0,8},{8,0},{16,24},{24,16},{1,9},{9,1},{17,25},{25,17},{2,10},{10... | collective-permute-start | bytes 1966088 | tf_op jit(solution)/shard_map/ppermute | solution.py:544
  13.1 1.5 %collective-permute-start.10 = (bf16[512,640]{1,0:T(8,128)(2,1)}, bf16[512,640]{1,0:T(8,128)(2,1)S(1)}, u32[]{:S(2)}, u32[]{:S(2)}) collective-permute-start(bf16[512,640]{1,0:T(8,128)(2,1)} %shard_map.172.refs_2_.refs_21_), channel_id=1, source_target_pairs={{0,16},{8,24},{16,0},{24,8},{1,17},{9,25},{17,1},{25,9},{2,18},{10... | collective-permute-start | bytes 1966088 | tf_op jit(solution)/shard_map/ppermute | solution.py:544
  15.6 2.6 %fusion = (f32[1024,128]{1,0:T(8,128)S(1)}, f32[1024,128]{1,0:T(8,128)S(1)}) fusion(f32[128]{0:T(128)} %get-tuple-element.33, f32[128]{0:T(128)} %get-tuple-element.34, f32[1024]{0:T(1024)S(1)} %convert_add_fusion), kind=kLoop, calls=%fused_computation.5 | loop fusion | flops 262144 | bytes 1053696 | tf_op jit(solution)/shard_map/mul | solution.py:587
  18.2 8.2 %collective-permute-done.3.refs_8_.refs_11_ = bf16[160,1280]{1,0:T(8,128)(2,1)S(1)} collective-permute-done((bf16[160,1280]{1,0:T(8,128)(2,1)S(1)}, bf16[160,1280]{1,0:T(8,128)(2,1)S(1)}, u32[]{:S(2)}, u32[]{:S(2)}) %collective-permute-start.3) | collective-permute-done | bytes 409632 | tf_op jit(solution)/shard_map/ppermute | solution.py:544
  27.1 2.4 %collective-permute-done.10.refs_4_.refs_23_ = bf16[512,640]{1,0:T(8,128)(2,1)S(1)} collective-permute-done((bf16[512,640]{1,0:T(8,128)(2,1)}, bf16[512,640]{1,0:T(8,128)(2,1)S(1)}, u32[]{:S(2)}, u32[]{:S(2)}) %collective-permute-start.10) | collective-permute-done | bytes 655392 | tf_op jit(solution)/shard_map/ppermute | solution.py:544
  30.0 0.9 collective-permute-start.11
  30.9 1.6 %collective-permute-start.12 = (bf16[256,640]{1,0:T(8,128)(2,1)S(1)}, bf16[256,640]{1,0:T(8,128)(2,1)S(1)}, u32[]{:S(2)}, u32[]{:S(2)}) collective-permute-start(bf16[256,640]{1,0:T(8,128)(2,1)S(1)} %slice.45), channel_id=1, source_target_pairs={{0,16},{8,24},{16,0},{24,8},{1,17},{9,25},{17,1},{25,9},{2,18},{10... | collective-permute-start | bytes 983048 | tf_op jit(solution)/shard_map/ppermute | solution.py:544
  32.6 7.0 %collective-permute-done.6.refs_11_.refs_12_ = bf16[160,1280]{1,0:T(8,128)(2,1)S(1)} collective-permute-done((bf16[160,1280]{1,0:T(8,128)(2,1)S(1)}, bf16[160,1280]{1,0:T(8,128)(2,1)S(1)}, u32[]{:S(2)}, u32[]{:S(2)}) %collective-permute-start.6) | collective-permute-done | bytes 409632 | tf_op jit(solution)/shard_map/ppermute | solution.py:544
  40.3 1.1 shard_map.173
  42.5 1.5 %collective-permute-start.24 = (bf16[4,32,1280]{2,1,0:T(8,128)(2,1)S(1)}, bf16[4,32,1280]{2,1,0:T(8,128)(2,1)S(1)}, u32[]{:S(2)}, u32[]{:S(2)}) collective-permute-start(bf16[4,32,1280]{2,1,0:T(8,128)(2,1)S(1)} %pad_maximum_fusion.1.refs_1_), channel_id=1, source_target_pairs={{0,16},{8,24},{16,0},{24,8},{1,17},{9,25},{17,1},{25,9},{2,18},{10... | collective-permute-start | bytes 983048 | tf_op jit(solution)/shard_map/ppermute | solution.py:544
  44.1 1.4 %collective-permute-start.25 = (bf16[4,32,1280]{2,1,0:T(8,128)(2,1)S(1)}, bf16[4,32,1280]{2,1,0:T(8,128)(2,1)S(1)}, u32[]{:S(2)}, u32[]{:S(2)}) collective-permute-start(bf16[4,32,1280]{2,1,0:T(8,128)(2,1)S(1)} %pad_maximum_fusion.1.refs_1_), channel_id=1, source_target_pairs={{0,24},{8,16},{16,8},{24,0},{1,25},{9,17},{17,9},{25,1},{2,26},{10... | collective-permute-start | bytes 983048 | tf_op jit(solution)/shard_map/ppermute | solution.py:544
  45.6 10.1 %shard_map.174.refs_1_ = bf16[1024,128]{1,0:T(8,128)(2,1)S(1)} custom-call(s32[2]{0:T(128)S(1)} %copy-done.2, s32[1,8]{1,0:T(1,128)S(1)} %copy-done.9, s32[1,8]{1,0:T(1,128)S(1)} %copy-done.10, s32[32,4]{1,0:T(8,128)S(1)} %copy.20.refs_3_, bf16[160,1280]{1,0:T(8,128)(2,1)S(1)} %pad_maximum_fusion.refs_4_.refs_11_, ...), custom_call_target="tpu_custom_call" | custom-call | flops 20000000000 | bytes 2000000 | tf_op jit(solution)/shard_map/pallas_call | solution.py:249
  56.3 1.9 %collective-permute-start.17 = (bf16[1024,128]{1,0:T(8,128)(2,1)S(1)}, bf16[1024,128]{1,0:T(8,128)(2,1)S(1)}, u32[]{:S(2)}, u32[]{:S(2)}) collective-permute-start(bf16[1024,128]{1,0:T(8,128)(2,1)S(1)} %shard_map.174.refs_1_), channel_id=1, source_target_pairs={{0,4},{1,5},{2,6},{3,7},{4,0},{5,1},{6,2},{7,3},{8,12},{9,13},{10,... | collective-permute-start | bytes 786440 | tf_op jit(solution)/shard_map/ppermute | solution.py:544
  58.2 1.5 %collective-permute-done.25.refs_4_ = bf16[4,32,1280]{2,1,0:T(8,128)(2,1)S(1)} collective-permute-done((bf16[4,32,1280]{2,1,0:T(8,128)(2,1)S(1)}, bf16[4,32,1280]{2,1,0:T(8,128)(2,1)S(1)}, u32[]{:S(2)}, u32[]{:S(2)}) %collective-permute-start.25) | collective-permute-done | bytes 327712 | tf_op jit(solution)/shard_map/ppermute | solution.py:544
  61.5 8.4 %collective-permute-done.15.refs_3_ = bf16[1024,128]{1,0:T(8,128)(2,1)S(1)} collective-permute-done((bf16[1024,128]{1,0:T(8,128)(2,1)S(1)}, bf16[1024,128]{1,0:T(8,128)(2,1)S(1)}, u32[]{:S(2)}, u32[]{:S(2)}) %collective-permute-start.15) | collective-permute-done | bytes 262176 | tf_op jit(solution)/shard_map/ppermute | solution.py:544
  69.9 1.5 %collective-permute-done.17.refs_5_ = bf16[1024,128]{1,0:T(8,128)(2,1)S(1)} collective-permute-done((bf16[1024,128]{1,0:T(8,128)(2,1)S(1)}, bf16[1024,128]{1,0:T(8,128)(2,1)S(1)}, u32[]{:S(2)}, u32[]{:S(2)}) %collective-permute-start.17) | collective-permute-done | bytes 262176 | tf_op jit(solution)/shard_map/ppermute | solution.py:544
  72.2 6.5 %collective-permute-done.21.refs_9_ = bf16[1024,128]{1,0:T(8,128)(2,1)S(1)} collective-permute-done((bf16[1024,128]{1,0:T(8,128)(2,1)S(1)}, bf16[1024,128]{1,0:T(8,128)(2,1)S(1)}, u32[]{:S(2)}, u32[]{:S(2)}) %collective-permute-start.21) | collective-permute-done | bytes 262176 | tf_op jit(solution)/shard_map/ppermute | solution.py:544
  78.8 1.4 %collective-permute-done.22.refs_10_ = bf16[1024,128]{1,0:T(8,128)(2,1)S(1)} collective-permute-done((bf16[1024,128]{1,0:T(8,128)(2,1)S(1)}, bf16[1024,128]{1,0:T(8,128)(2,1)S(1)}, u32[]{:S(2)}, u32[]{:S(2)}) %collective-permute-start.22) | collective-permute-done | bytes 262176 | tf_op jit(solution)/shard_map/ppermute | solution.py:544
  80.2 3.8 %shard_map.176 = (bf16[128,1280]{1,0:T(8,128)(2,1)S(1)}, bf16[128,1280]{1,0:T(8,128)(2,1)S(1)}) custom-call(s32[2]{0:T(128)S(1)} %copy-done.2, bf16[1024,128]{1,0:T(8,128)(2,1)S(1)} %shard_map.174.refs_1_, bf16[1024,128]{1,0:T(8,128)(2,1)S(1)} %collective-permute-done.14.refs_2_, bf16[1024,128]{1,0:T(8,128)(2,1)S(1)} %collective-permute-done.15.refs_3_, ...), custom_call_target="tpu_custom_call" | custom-call | flops 20000000000 | bytes 10000000 | tf_op jit(solution)/shard_map/pallas_call | solution.py:249
  84.2 1.5 %collective-permute-done.28 = bf16[128,1280]{1,0:T(8,128)(2,1)S(1)} collective-permute-done((bf16[128,1280]{1,0:T(8,128)(2,1)S(1)}, bf16[128,1280]{1,0:T(8,128)(2,1)S(1)}, u32[]{:S(2)}, u32[]{:S(2)}) %collective-permute-start.28) | collective-permute-done | bytes 327712 | tf_op jit(solution)/shard_map/ppermute | solution.py:544
  87.3 7.3 %shard_map.177 = (bf16[256,1280]{1,0:T(8,128)(2,1)S(1)}, bf16[256,1280]{1,0:T(8,128)(2,1)S(1)}) custom-call(s32[2]{0:T(128)S(1)} %copy-done.2, bf16[1024,128]{1,0:T(8,128)(2,1)S(1)} %shard_map.174.refs_1_, bf16[1024,128]{1,0:T(8,128)(2,1)S(1)} %collective-permute-done.14.refs_2_, bf16[1024,128]{1,0:T(8,128)(2,1)S(1)} %collective-permute-done.15.refs_3_, ...), custom_call_target="tpu_custom_call" | custom-call | flops 20000000000 | bytes 10000000 | tf_op jit(solution)/shard_map/pallas_call | solution.py:249
  96.9 4.2 %collective-permute-start.34 = (bf16[128,1280]{1,0:T(8,128)(2,1)S(1)}, bf16[128,1280]{1,0:T(8,128)(2,1)S(1)}, u32[]{:S(2)}, u32[]{:S(2)}) collective-permute-start(bf16[128,1280]{1,0:T(8,128)(2,1)S(1)} %get-tuple-element.27), channel_id=1, source_target_pairs={{0,2},{1,3},{2,0},{3,1},{4,6},{5,7},{6,4},{7,5},{8,10},{9,11},{10,... | collective-permute-start | bytes 983048 | tf_op jit(solution)/shard_map/ppermute | solution.py:544
  101.3 4.2 %shard_map.179 = (bf16[128,1280]{1,0:T(8,128)(2,1)S(1)}, bf16[128,1280]{1,0:T(8,128)(2,1)S(1)}, bf16[128,1280]{1,0:T(8,128)(2,1)S(1)}) custom-call(s32[2]{0:T(128)S(1)} %copy-done.2, bf16[1024,128]{1,0:T(8,128)(2,1)S(1)} %shard_map.174.refs_1_, bf16[1024,128]{1,0:T(8,128)(2,1)S(1)} %collective-permute-done.14.refs_2_, ...), custom_call_target="tpu_custom_call" | custom-call | flops 20000000000 | bytes 10000000 | tf_op jit(solution)/shard_map/pallas_call | solution.py:249
  106.1 0.9 collective-permute-done.32.refs_2_
  107.2 7.7 %collective-permute-done.34.refs_4_ = bf16[128,1280]{1,0:T(8,128)(2,1)S(1)} collective-permute-done((bf16[128,1280]{1,0:T(8,128)(2,1)S(1)}, bf16[128,1280]{1,0:T(8,128)(2,1)S(1)}, u32[]{:S(2)}, u32[]{:S(2)}) %collective-permute-start.34) | collective-permute-done | bytes 327712 | tf_op jit(solution)/shard_map/ppermute | solution.py:544
  114.8 3.7 %collective-permute-done.35.refs_5_ = bf16[128,1280]{1,0:T(8,128)(2,1)S(1)} collective-permute-done((bf16[128,1280]{1,0:T(8,128)(2,1)S(1)}, bf16[128,1280]{1,0:T(8,128)(2,1)S(1)}, u32[]{:S(2)}, u32[]{:S(2)}) %collective-permute-start.35) | collective-permute-done | bytes 327712 | tf_op jit(solution)/shard_map/ppermute | solution.py:544
  118.6 1.2 %shard_map.180 = bf16[128,1280]{1,0:T(8,128)(2,1)} custom-call(bf16[128,1280]{1,0:T(8,128)(2,1)S(1)} %get-tuple-element.24.refs_0_, bf16[128,1280]{1,0:T(8,128)(2,1)S(1)} %get-tuple-element.25.refs_1_, bf16[64,1280]{1,0:T(8,128)(2,1)S(1)} %collective-permute-done.32.refs_2_, bf16[64,1280]{1,0:T(8,128)(2,1)S(1)} %collective-permute-done.33.refs_3_, ...), custom_call_target="tpu_custom_call" | custom-call | tf_op jit(solution)/shard_map/pallas_call | solution.py:249
  (105 shorter events, 13.5 us)
Async XLA Ops:
  2.0 39.4 %collective-permute-start = (bf16[160,1280]{1,0:T(8,128)(2,1)S(1)}, bf16[160,1280]{1,0:T(8,128)(2,1)}, u32[]{:S(2)}, u32[]{:S(2)}) collective-permute-start(bf16[160,1280]{1,0:T(8,128)(2,1)S(1)} %pad_maximum_fusion.refs_4_.refs_11_), channel_id=1, source_target_pairs={{0,1},{1,0},{2,3},{3,2},{4,5},{5,4},{6,7},{7,6},{8,9},{9,8},{10,11... | collective-permute-start | bytes 1228808 | tf_op jit(solution)/shard_map/ppermute | solution.py:544
  2.5 28.4 %collective-permute-start.1 = (bf16[160,1280]{1,0:T(8,128)(2,1)S(1)}, bf16[160,1280]{1,0:T(8,128)(2,1)S(1)}, u32[]{:S(2)}, u32[]{:S(2)}) collective-permute-start(bf16[160,1280]{1,0:T(8,128)(2,1)S(1)} %pad_maximum_fusion.refs_4_.refs_11_), channel_id=1, source_target_pairs={{0,2},{1,3},{2,0},{3,1},{4,6},{5,7},{6,4},{7,5},{8,10},{9,11},{10,... | collective-permute-start | bytes 1228808 | tf_op jit(solution)/shard_map/ppermute | solution.py:544
  5.2 21.3 %collective-permute-start.3 = (bf16[160,1280]{1,0:T(8,128)(2,1)S(1)}, bf16[160,1280]{1,0:T(8,128)(2,1)S(1)}, u32[]{:S(2)}, u32[]{:S(2)}) collective-permute-start(bf16[160,1280]{1,0:T(8,128)(2,1)S(1)} %pad_maximum_fusion.refs_4_.refs_11_), channel_id=1, source_target_pairs={{0,4},{1,5},{2,6},{3,7},{4,0},{5,1},{6,2},{7,3},{8,12},{9,13},{10,... | collective-permute-start | bytes 1228808 | tf_op jit(solution)/shard_map/ppermute | solution.py:544
  11.5 18.5 %collective-permute-start.9 = (bf16[512,640]{1,0:T(8,128)(2,1)}, bf16[512,640]{1,0:T(8,128)(2,1)S(1)}, u32[]{:S(2)}, u32[]{:S(2)}) collective-permute-start(bf16[512,640]{1,0:T(8,128)(2,1)} %shard_map.172.refs_2_.refs_21_), channel_id=1, source_target_pairs={{0,8},{8,0},{16,24},{24,16},{1,9},{9,1},{17,25},{25,17},{2,10},{10... | collective-permute-start | bytes 1966088 | tf_op jit(solution)/shard_map/ppermute | solution.py:544
  13.1 16.5 %collective-permute-start.10 = (bf16[512,640]{1,0:T(8,128)(2,1)}, bf16[512,640]{1,0:T(8,128)(2,1)S(1)}, u32[]{:S(2)}, u32[]{:S(2)}) collective-permute-start(bf16[512,640]{1,0:T(8,128)(2,1)} %shard_map.172.refs_2_.refs_21_), channel_id=1, source_target_pairs={{0,16},{8,24},{16,0},{24,8},{1,17},{9,25},{17,1},{25,9},{2,18},{10... | collective-permute-start | bytes 1966088 | tf_op jit(solution)/shard_map/ppermute | solution.py:544
  26.4 6.1 %collective-permute-start.5 = (bf16[160,1280]{1,0:T(8,128)(2,1)S(1)}, bf16[160,1280]{1,0:T(8,128)(2,1)S(1)}, u32[]{:S(2)}, u32[]{:S(2)}) collective-permute-start(bf16[160,1280]{1,0:T(8,128)(2,1)S(1)} %pad_maximum_fusion.refs_4_.refs_11_), channel_id=1, source_target_pairs={{2,4},{3,5},{4,2},{5,3},{10,12},{11,13},{12,10},{13,11},{18,20},{1... | collective-permute-start | bytes 1228808 | tf_op jit(solution)/shard_map/ppermute | solution.py:548
  29.5 10.1 %collective-permute-start.6 = (bf16[160,1280]{1,0:T(8,128)(2,1)S(1)}, bf16[160,1280]{1,0:T(8,128)(2,1)S(1)}, u32[]{:S(2)}, u32[]{:S(2)}) collective-permute-start(bf16[160,1280]{1,0:T(8,128)(2,1)S(1)} %collective-permute-done.3.refs_8_.refs_11_), channel_id=1, source_target_pairs={{0,2},{1,3},{2,0},{3,1},{4,6},{5,7},{6,4},{7,5},{8,10},{9,11},{10,... | collective-permute-start | bytes 1228808 | tf_op jit(solution)/shard_map/ppermute | solution.py:544
  30.0 9.6 %collective-permute-start.11 = (bf16[256,640]{1,0:T(8,128)(2,1)S(1)}, bf16[256,640]{1,0:T(8,128)(2,1)S(1)}, u32[]{:S(2)}, u32[]{:S(2)}) collective-permute-start(bf16[256,640]{1,0:T(8,128)(2,1)S(1)} %slice.44), channel_id=1, source_target_pairs={{0,8},{8,0},{16,24},{24,16},{1,9},{9,1},{17,25},{25,17},{2,10},{10... | collective-permute-start | bytes 983048 | tf_op jit(solution)/shard_map/ppermute | solution.py:544
  30.9 9.2 %collective-permute-start.12 = (bf16[256,640]{1,0:T(8,128)(2,1)S(1)}, bf16[256,640]{1,0:T(8,128)(2,1)S(1)}, u32[]{:S(2)}, u32[]{:S(2)}) collective-permute-start(bf16[256,640]{1,0:T(8,128)(2,1)S(1)} %slice.45), channel_id=1, source_target_pairs={{0,16},{8,24},{16,0},{24,8},{1,17},{9,25},{17,1},{25,9},{2,18},{10... | collective-permute-start | bytes 983048 | tf_op jit(solution)/shard_map/ppermute | solution.py:544
  32.5 9.4 %collective-permute-start.2 = (bf16[160,1280]{1,0:T(8,128)(2,1)S(1)}, bf16[160,1280]{1,0:T(8,128)(2,1)S(1)}, u32[]{:S(2)}, u32[]{:S(2)}) collective-permute-start(bf16[160,1280]{1,0:T(8,128)(2,1)S(1)} %collective-permute-done.1.refs_6_.refs_13_), channel_id=1, source_target_pairs={{0,1},{1,0},{2,3},{3,2},{4,5},{5,4},{6,7},{7,6},{8,9},{9,8},{10,11... | collective-permute-start | bytes 1228808 | tf_op jit(solution)/shard_map/ppermute | solution.py:544
  39.6 3.0 %collective-permute-start.4 = (bf16[160,1280]{1,0:T(8,128)(2,1)S(1)}, bf16[160,1280]{1,0:T(8,128)(2,1)S(1)}, u32[]{:S(2)}, u32[]{:S(2)}) collective-permute-start(bf16[160,1280]{1,0:T(8,128)(2,1)S(1)} %collective-permute-done.3.refs_8_.refs_11_), channel_id=1, source_target_pairs={{0,1},{1,0},{2,3},{3,2},{4,5},{5,4},{6,7},{7,6},{8,9},{9,8},{10,11... | collective-permute-start | bytes 1228808 | tf_op jit(solution)/shard_map/ppermute | solution.py:544
  39.6 4.5 %collective-permute-start.7 = (bf16[160,1280]{1,0:T(8,128)(2,1)S(1)}, bf16[160,1280]{1,0:T(8,128)(2,1)S(1)}, u32[]{:S(2)}, u32[]{:S(2)}) collective-permute-start(bf16[160,1280]{1,0:T(8,128)(2,1)S(1)} %collective-permute-done.5.refs_10_.refs_11_), channel_id=1, source_target_pairs={{0,1},{1,0},{2,3},{3,2},{4,5},{5,4},{6,7},{7,6},{8,9},{9,8},{10,11... | collective-permute-start | bytes 1228808 | tf_op jit(solution)/shard_map/ppermute | solution.py:544
  40.1 5.4 %collective-permute-start.8 = (bf16[160,1280]{1,0:T(8,128)(2,1)S(1)}, bf16[160,1280]{1,0:T(8,128)(2,1)S(1)}, u32[]{:S(2)}, u32[]{:S(2)}) collective-permute-start(bf16[160,1280]{1,0:T(8,128)(2,1)S(1)} %collective-permute-done.6.refs_11_.refs_12_), channel_id=1, source_target_pairs={{0,1},{1,0},{2,3},{3,2},{4,5},{5,4},{6,7},{7,6},{8,9},{9,8},{10,11... | collective-permute-start | bytes 1228808 | tf_op jit(solution)/shard_map/ppermute | solution.py:544
  41.4 4.1 %collective-permute-start.13 = (bf16[64,1280]{1,0:T(8,128)(2,1)S(1)}, bf16[64,1280]{1,0:T(8,128)(2,1)S(1)}, u32[]{:S(2)}, u32[]{:S(2)}) collective-permute-start(bf16[64,1280]{1,0:T(8,128)(2,1)S(1)} %get-tuple-element.16.refs_15_), channel_id=1, source_target_pairs={{0,1},{1,0},{2,3},{3,2},{4,5},{5,4},{6,7},{7,6},{8,9},{9,8},{10,11... | collective-permute-start | bytes 491528 | tf_op jit(solution)/shard_map/ppermute | solution.py:544
  41.9 14.3 %collective-permute-start.23 = (bf16[4,32,1280]{2,1,0:T(8,128)(2,1)S(1)}, bf16[4,32,1280]{2,1,0:T(8,128)(2,1)S(1)}, u32[]{:S(2)}, u32[]{:S(2)}) collective-permute-start(bf16[4,32,1280]{2,1,0:T(8,128)(2,1)S(1)} %pad_maximum_fusion.1.refs_1_), channel_id=1, source_target_pairs={{0,8},{8,0},{16,24},{24,16},{1,9},{9,1},{17,25},{25,17},{2,10},{10... | collective-permute-start | bytes 983048 | tf_op jit(solution)/shard_map/ppermute | solution.py:544
  42.5 15.6 %collective-permute-start.24 = (bf16[4,32,1280]{2,1,0:T(8,128)(2,1)S(1)}, bf16[4,32,1280]{2,1,0:T(8,128)(2,1)S(1)}, u32[]{:S(2)}, u32[]{:S(2)}) collective-permute-start(bf16[4,32,1280]{2,1,0:T(8,128)(2,1)S(1)} %pad_maximum_fusion.1.refs_1_), channel_id=1, source_target_pairs={{0,16},{8,24},{16,0},{24,8},{1,17},{9,25},{17,1},{25,9},{2,18},{10... | collective-permute-start | bytes 983048 | tf_op jit(solution)/shard_map/ppermute | solution.py:544
  44.1 15.6 %collective-permute-start.25 = (bf16[4,32,1280]{2,1,0:T(8,128)(2,1)S(1)}, bf16[4,32,1280]{2,1,0:T(8,128)(2,1)S(1)}, u32[]{:S(2)}, u32[]{:S(2)}) collective-permute-start(bf16[4,32,1280]{2,1,0:T(8,128)(2,1)S(1)} %pad_maximum_fusion.1.refs_1_), channel_id=1, source_target_pairs={{0,24},{8,16},{16,8},{24,0},{1,25},{9,17},{17,9},{25,1},{2,26},{10... | collective-permute-start | bytes 983048 | tf_op jit(solution)/shard_map/ppermute | solution.py:544
  55.7 5.2 %collective-permute-start.14 = (bf16[1024,128]{1,0:T(8,128)(2,1)S(1)}, bf16[1024,128]{1,0:T(8,128)(2,1)S(1)}, u32[]{:S(2)}, u32[]{:S(2)}) collective-permute-start(bf16[1024,128]{1,0:T(8,128)(2,1)S(1)} %shard_map.174.refs_1_), channel_id=1, source_target_pairs={{0,1},{1,0},{2,3},{3,2},{4,5},{5,4},{6,7},{7,6},{8,9},{9,8},{10,11... | collective-permute-start | bytes 786440 | tf_op jit(solution)/shard_map/ppermute | solution.py:544
  55.8 14.2 %collective-permute-start.15 = (bf16[1024,128]{1,0:T(8,128)(2,1)S(1)}, bf16[1024,128]{1,0:T(8,128)(2,1)S(1)}, u32[]{:S(2)}, u32[]{:S(2)}) collective-permute-start(bf16[1024,128]{1,0:T(8,128)(2,1)S(1)} %shard_map.174.refs_1_), channel_id=1, source_target_pairs={{0,2},{1,3},{2,0},{3,1},{4,6},{5,7},{6,4},{7,5},{8,10},{9,11},{10,... | collective-permute-start | bytes 786440 | tf_op jit(solution)/shard_map/ppermute | solution.py:544
  56.3 15.2 %collective-permute-start.17 = (bf16[1024,128]{1,0:T(8,128)(2,1)S(1)}, bf16[1024,128]{1,0:T(8,128)(2,1)S(1)}, u32[]{:S(2)}, u32[]{:S(2)}) collective-permute-start(bf16[1024,128]{1,0:T(8,128)(2,1)S(1)} %shard_map.174.refs_1_), channel_id=1, source_target_pairs={{0,4},{1,5},{2,6},{3,7},{4,0},{5,1},{6,2},{7,3},{8,12},{9,13},{10,... | collective-permute-start | bytes 786440 | tf_op jit(solution)/shard_map/ppermute | solution.py:544
  60.3 18.4 %collective-permute-start.26 = (bf16[256,1280]{1,0:T(8,128)(2,1)S(1)}, bf16[256,1280]{1,0:T(8,128)(2,1)S(1)}, u32[]{:S(2)}, u32[]{:S(2)}) collective-permute-start(bf16[256,1280]{1,0:T(8,128)(2,1)S(1)} %bitcast.22), channel_id=1, source_target_pairs={{0,1},{1,0},{2,3},{3,2},{4,5},{5,4},{6,7},{7,6},{8,9},{9,8},{10,11... | collective-permute-start | bytes 1966088 | tf_op jit(solution)/shard_map/ppermute | solution.py:544
  60.4 18.4 %collective-permute-start.27 = (bf16[256,1280]{1,0:T(8,128)(2,1)S(1)}, bf16[256,1280]{1,0:T(8,128)(2,1)S(1)}, u32[]{:S(2)}, u32[]{:S(2)}) collective-permute-start(bf16[256,1280]{1,0:T(8,128)(2,1)S(1)} %bitcast.26), channel_id=1, source_target_pairs={{0,1},{1,0},{2,3},{3,2},{4,5},{5,4},{6,7},{7,6},{8,9},{9,8},{10,11... | collective-permute-start | bytes 1966088 | tf_op jit(solution)/shard_map/ppermute | solution.py:544
  60.9 10.8 %collective-permute-start.19 = (bf16[1024,128]{1,0:T(8,128)(2,1)S(1)}, bf16[1024,128]{1,0:T(8,128)(2,1)S(1)}, u32[]{:S(2)}, u32[]{:S(2)}) collective-permute-start(bf16[1024,128]{1,0:T(8,128)(2,1)S(1)} %shard_map.174.refs_1_), channel_id=1, source_target_pairs={{2,4},{3,5},{4,2},{5,3},{10,12},{11,13},{12,10},{13,11},{18,20},{1... | collective-permute-start | bytes 786440 | tf_op jit(solution)/shard_map/ppermute | solution.py:548
  69.9 1.7 %collective-permute-start.16 = (bf16[1024,128]{1,0:T(8,128)(2,1)S(1)}, bf16[1024,128]{1,0:T(8,128)(2,1)S(1)}, u32[]{:S(2)}, u32[]{:S(2)}) collective-permute-start(bf16[1024,128]{1,0:T(8,128)(2,1)S(1)} %collective-permute-done.15.refs_3_), channel_id=1, source_target_pairs={{0,1},{1,0},{2,3},{3,2},{4,5},{5,4},{6,7},{7,6},{8,9},{9,8},{10,11... | collective-permute-start | bytes 786440 | tf_op jit(solution)/shard_map/ppermute | solution.py:544
  71.4 7.2 %collective-permute-start.21 = (bf16[1024,128]{1,0:T(8,128)(2,1)S(1)}, bf16[1024,128]{1,0:T(8,128)(2,1)S(1)}, u32[]{:S(2)}, u32[]{:S(2)}) collective-permute-start(bf16[1024,128]{1,0:T(8,128)(2,1)S(1)} %collective-permute-done.17.refs_5_), channel_id=1, source_target_pairs={{0,2},{1,3},{2,0},{3,1},{4,6},{5,7},{6,4},{7,5},{8,10},{9,11},{10,... | collective-permute-start | bytes 786440 | tf_op jit(solution)/shard_map/ppermute | solution.py:544
  71.6 7.1 %collective-permute-start.18 = (bf16[1024,128]{1,0:T(8,128)(2,1)S(1)}, bf16[1024,128]{1,0:T(8,128)(2,1)S(1)}, u32[]{:S(2)}, u32[]{:S(2)}) collective-permute-start(bf16[1024,128]{1,0:T(8,128)(2,1)S(1)} %collective-permute-done.17.refs_5_), channel_id=1, source_target_pairs={{0,1},{1,0},{2,3},{3,2},{4,5},{5,4},{6,7},{7,6},{8,9},{9,8},{10,11... | collective-permute-start | bytes 786440 | tf_op jit(solution)/shard_map/ppermute | solution.py:544
  71.6 7.1 %collective-permute-start.20 = (bf16[1024,128]{1,0:T(8,128)(2,1)S(1)}, bf16[1024,128]{1,0:T(8,128)(2,1)S(1)}, u32[]{:S(2)}, u32[]{:S(2)}) collective-permute-start(bf16[1024,128]{1,0:T(8,128)(2,1)S(1)} %collective-permute-done.19.refs_7_), channel_id=1, source_target_pairs={{0,1},{1,0},{2,3},{3,2},{4,5},{5,4},{6,7},{7,6},{8,9},{9,8},{10,11... | collective-permute-start | bytes 786440 | tf_op jit(solution)/shard_map/ppermute | solution.py:544
  85.7 9.8 %collective-permute-start.29 = (bf16[128,1280]{1,0:T(8,128)(2,1)S(1)}, bf16[128,1280]{1,0:T(8,128)(2,1)S(1)}, u32[]{:S(2)}, u32[]{:S(2)}) collective-permute-start(bf16[128,1280]{1,0:T(8,128)(2,1)S(1)} %add_convert_fusion.2), channel_id=1, source_target_pairs={{0,2},{1,3},{2,0},{3,1},{4,6},{5,7},{6,4},{7,5},{8,10},{9,11},{10,... | collective-permute-start | bytes 983048 | tf_op jit(solution)/shard_map/ppermute | solution.py:544
  86.6 9.0 %collective-permute-start.30 = (bf16[128,1280]{1,0:T(8,128)(2,1)S(1)}, bf16[128,1280]{1,0:T(8,128)(2,1)S(1)}, u32[]{:S(2)}, u32[]{:S(2)}) collective-permute-start(bf16[128,1280]{1,0:T(8,128)(2,1)S(1)} %add_convert_fusion.2), channel_id=1, source_target_pairs={{2,4},{3,5},{4,2},{5,3},{10,12},{11,13},{12,10},{13,11},{18,20},{1... | collective-permute-start | bytes 983048 | tf_op jit(solution)/shard_map/ppermute | solution.py:548
  94.6 2.2 %collective-permute-start.31 = (bf16[256,1280]{1,0:T(8,128)(2,1)S(1)}, bf16[256,1280]{1,0:T(8,128)(2,1)S(1)}, u32[]{:S(2)}, u32[]{:S(2)}) collective-permute-start(bf16[256,1280]{1,0:T(8,128)(2,1)S(1)} %get-tuple-element.23), channel_id=1, source_target_pairs={{0,1},{1,0},{2,3},{3,2},{4,5},{5,4},{6,7},{7,6},{8,9},{9,8},{10,11... | collective-permute-start | bytes 1966088 | tf_op jit(solution)/shard_map/ppermute | solution.py:544
  96.9 17.9 %collective-permute-start.34 = (bf16[128,1280]{1,0:T(8,128)(2,1)S(1)}, bf16[128,1280]{1,0:T(8,128)(2,1)S(1)}, u32[]{:S(2)}, u32[]{:S(2)}) collective-permute-start(bf16[128,1280]{1,0:T(8,128)(2,1)S(1)} %get-tuple-element.27), channel_id=1, source_target_pairs={{0,2},{1,3},{2,0},{3,1},{4,6},{5,7},{6,4},{7,5},{8,10},{9,11},{10,... | collective-permute-start | bytes 983048 | tf_op jit(solution)/shard_map/ppermute | solution.py:544
  101.1 17.4 %collective-permute-start.35 = (bf16[128,1280]{1,0:T(8,128)(2,1)S(1)}, bf16[128,1280]{1,0:T(8,128)(2,1)S(1)}, u32[]{:S(2)}, u32[]{:S(2)}) collective-permute-start(bf16[128,1280]{1,0:T(8,128)(2,1)S(1)} %get-tuple-element.28.refs_23_), channel_id=1, source_target_pairs={{0,4},{1,5},{2,6},{3,7},{4,0},{5,1},{6,2},{7,3},{8,12},{9,13},{10,... | collective-permute-start | bytes 983048 | tf_op jit(solution)/shard_map/ppermute | solution.py:544
  (20 other events, 347.9 us)

commit v5 on v4

--- a/solution.py
+++ b/solution.py
@@ -367,7 +367,7 @@
     return begins
 
 
-def project(j, ids, begins, pieces, weight, down, down_other, up, cosines, sines, gain):
+def project(j, ids, begins, pieces, weight, down, up, cosines, sines, gain):
     rows = jnp.concatenate(pieces, axis=0)
     count = rows.shape[0]
     row = jnp.concatenate([spot + iota((128, 128), 0) for spot in piece_spots(ids, j)], axis=0)
@@ -376,9 +376,10 @@
     for i in range(GROUP_REQUESTS):
         first = jnp.where(request == i, begins[i], first)
         end = jnp.where(request == i, begins[i + 1], end)
-    middle = dot_nt(rows, jnp.concatenate([down[...], down_other[...]], axis=0))
+    total = dot(rows, jnp.concatenate([weight[...], down[...]], axis=1))
+    total, middle = total[:, 0:384], total[:, 384:512]
     middle = jnp.where((row >= first) & (row < end), middle, 0.0).astype(BF16)
-    total = dot(rows, weight[...]) + adapter_scale * dot(middle, up[...])
+    total = total + adapter_scale * dot(middle, up[...])
     part0, part1, part2 = total[:, 0:128], total[:, 128:256], total[:, 256:384]
     low = first_head(count)
     query = jnp.where(low, part0, part1)
@@ -398,12 +399,16 @@
 
 def attend_kernel(ids, lengths, prompts, table, *refs):
     pieces, refs = row_pieces(ids, refs, range(4))
-    *constants, g0, g1, g2, g3, out, queries, keys, values, pages, starts, sums = refs
+    weight, down, down_other, *constants, g0, g1, g2, g3, out = refs[:-7]
+    queries, keys, values, pages, starts, sums, turned = refs[-7:]
+    turned[:, 0:64] = jnp.transpose(down[...])
+    turned[:, 64:128] = jnp.transpose(down_other[...])
     begins = request_starts(lengths)
     for i, begin in enumerate(begins):
         starts[i] = begin
     for j in range(4):
-        parts = project(j, ids, begins, pieces[2 * j : 2 * j + 2], *constants)
+        rows = pieces[2 * j : 2 * j + 2]
+        parts = project(j, ids, begins, rows, weight, turned, *constants)
         for part, target in zip(parts, (queries, keys, values)):
             for side, spot in enumerate(piece_spots(ids, j)):
                 target[pl.ds(spot, 128), :] = part[side * 128 : side * 128 + 128]
@@ -506,17 +511,18 @@
         def rows_of(heads):
             return jnp.concatenate([heads[pl.ds(spot, 128), :] for spot in spots], axis=0)
 
-        attn_sum = 0.0
+        columns = []
         for side in (0, 1):
-            columns = [rows_of(heads_in[2 * distance + side]) for distance in range(4)]
-            columns[3] = jnp.where(direct, columns[3], rows_of(heads_in[8 + side]))
-            for half in (0, 1):
-                pair = jnp.concatenate(columns[2 * half : 2 * half + 2], axis=1)
-                attn_sum = attn_sum + dot(pair, matrices[2 * side + half][...])
+            for distance in range(4):
+                columns.append(rows_of(heads_in[2 * distance + side]))
+            columns[-1] = jnp.where(direct, columns[-1], rows_of(heads_in[8 + side]))
+        output = jnp.concatenate([matrix[...] for matrix in matrices], axis=0)
+        attn_sum = dot(jnp.concatenate(columns, axis=1), output)
         base = jnp.concatenate(pieces[2 * place : 2 * place + 2], axis=0).astype(F32)
         mixed = renorm(base + rate[...] * (renorm(attn_sum) - base)).astype(BF16)
-        up_part = dot(mixed, up[...]) * up_scale[...]
-        gate_part = dot(mixed, gate[...]) * gate_scale[...]
+        both = dot(mixed, jnp.concatenate([up[...], gate[...]], axis=1))
+        up_part = both[:, : up.shape[1]] * up_scale[...]
+        gate_part = both[:, up.shape[1] :] * gate_scale[...]
         unit_values = (up_part * (gate_part / (1.0 + jnp.exp(-gate_part)))).astype(BF16)
         result = dot(unit_values, down[...]).astype(BF16)
         keep[place * 128 : place * 128 + 128, :] = result[0:128]
@@ -645,6 +651,7 @@
             pltpu.VMEM((1024, 256), BF16),
             pltpu.SMEM((GROUP_REQUESTS + 1,), jnp.int32),
             pltpu.VMEM((group_rows // 128, 2, 128, 128), F32),
+            pltpu.VMEM((MODEL_WIDTH, 128), BF16),
         ),
         flops=2 * 10**10,
         moved=2 * 10**6,

time: 120 us -> 118 us (0.983)
  Pallas kernels: 32 us -> 29.9 us
    pallas_call x9, Pallas kernels: 32 us -> 29.9 us  [call(): pl.pallas_call(whole, out_shape=outs, in_specs=specs, out_specs=jax.tree....]
  transfers between devices with their start and end apart: 36 -> 36, of which waited for: 15 -> 15; matrix products, arithmetic and copies ran while one was open for 4% -> 4% of each run, Pallas kernels for 23% -> 21%
where the time goes in v5:
time: 118 us
  waiting for transfers between devices  51.6 us (44%)
  Pallas kernels  29.9 us (25%)
  starting transfers between devices  29 us (25%)
  other arithmetic  5.38 us (5%)
  local copies, waits for them, and re-layouts  1.27 us (1%)
    ppermute x33, waiting for transfers between devices, swap(): return lax.ppermute(values, axis, [(i, i ^ distance) for i in range(size)])  51.6 us
    pallas_call x9, Pallas kernels, call(): pl.pallas_call(whole, out_shape=outs, in_specs=specs, out_specs=jax.tree....  29.9 us
    ppermute x33, starting transfers between devices, swap(): return lax.ppermute(values, axis, [(i, i ^ distance) for i in range(size)])  26.8 us
    mul x1, other arithmetic, local_pairwise(): sines = jnp.where(lanes[None, :] < half, -1.0, 1.0) * jnp.sin(angles)  2.59 us
  transfers between devices with their start and end apart: 36, of which 15 were waited for; matrix products, arithmetic and copies ran while one was open for 4% of the time, Pallas kernels for 21%

profile of v5, /device:TPU:0, one launch (start us, length us, event | category | flops | bytes accessed | tf_op | source)
XLA Modules:
  0.0 117.7 jit_solution(14434198274041302449)
XLA Ops:
  0.0 1.0 copy-done
  1.0 1.0 pad_maximum_fusion.refs_4_.refs_11_
  2.5 2.7 %collective-permute-start.1 = (bf16[160,1280]{1,0:T(8,128)(2,1)S(1)}, bf16[160,1280]{1,0:T(8,128)(2,1)S(1)}, u32[]{:S(2)}, u32[]{:S(2)}) collective-permute-start(bf16[160,1280]{1,0:T(8,128)(2,1)S(1)} %pad_maximum_fusion.refs_4_.refs_11_), channel_id=1, source_target_pairs={{0,2},{1,3},{2,0},{3,1},{4,6},{5,7},{6,4},{7,5},{8,10},{9,11},{10,... | collective-permute-start | bytes 1228808 | tf_op jit(solution)/shard_map/ppermute | solution.py:550
  5.2 2.6 %collective-permute-start.3 = (bf16[160,1280]{1,0:T(8,128)(2,1)S(1)}, bf16[160,1280]{1,0:T(8,128)(2,1)S(1)}, u32[]{:S(2)}, u32[]{:S(2)}) collective-permute-start(bf16[160,1280]{1,0:T(8,128)(2,1)S(1)} %pad_maximum_fusion.refs_4_.refs_11_), channel_id=1, source_target_pairs={{0,4},{1,5},{2,6},{3,7},{4,0},{5,1},{6,2},{7,3},{8,12},{9,13},{10,... | collective-permute-start | bytes 1228808 | tf_op jit(solution)/shard_map/ppermute | solution.py:550
  8.4 3.1 %shard_map.172.refs_2_.refs_21_ = bf16[512,640]{1,0:T(8,128)(2,1)} custom-call(s32[2]{0:T(128)} %pad_add_fusion.refs_0_.refs_25_, bf16[256,256]{1,0:T(8,128)(2,1)} %bitcast.32, bf16[256,384]{1,0:T(8,128)(2,1)} %bitcast.31, bf16[256,1280]{1,0:T(8,128)(2,1)} %bitcast.30, f32[1,128]{1,0:T(1,128)} %bitcast.20), custom_call_target="tpu_custom_call" | custom-call | tf_op jit(solution)/shard_map/pallas_call | solution.py:249
  11.5 1.6 %collective-permute-start.9 = (bf16[512,640]{1,0:T(8,128)(2,1)}, bf16[512,640]{1,0:T(8,128)(2,1)S(1)}, u32[]{:S(2)}, u32[]{:S(2)}) collective-permute-start(bf16[512,640]{1,0:T(8,128)(2,1)} %shard_map.172.refs_2_.refs_21_), channel_id=1, source_target_pairs={{0,8},{8,0},{16,24},{24,16},{1,9},{9,1},{17,25},{25,17},{2,10},{10... | collective-permute-start | bytes 1966088 | tf_op jit(solution)/shard_map/ppermute | solution.py:550
  13.1 1.5 %collective-permute-start.10 = (bf16[512,640]{1,0:T(8,128)(2,1)}, bf16[512,640]{1,0:T(8,128)(2,1)S(1)}, u32[]{:S(2)}, u32[]{:S(2)}) collective-permute-start(bf16[512,640]{1,0:T(8,128)(2,1)} %shard_map.172.refs_2_.refs_21_), channel_id=1, source_target_pairs={{0,16},{8,24},{16,0},{24,8},{1,17},{9,25},{17,1},{25,9},{2,18},{10... | collective-permute-start | bytes 1966088 | tf_op jit(solution)/shard_map/ppermute | solution.py:550
  15.6 2.6 %fusion = (f32[1024,128]{1,0:T(8,128)S(1)}, f32[1024,128]{1,0:T(8,128)S(1)}) fusion(f32[128]{0:T(128)} %get-tuple-element.33, f32[128]{0:T(128)} %get-tuple-element.34, f32[1024]{0:T(1024)S(1)} %convert_add_fusion), kind=kLoop, calls=%fused_computation.5 | loop fusion | flops 262144 | bytes 1053696 | tf_op jit(solution)/shard_map/mul | solution.py:593
  18.2 8.2 %collective-permute-done.3.refs_8_.refs_11_ = bf16[160,1280]{1,0:T(8,128)(2,1)S(1)} collective-permute-done((bf16[160,1280]{1,0:T(8,128)(2,1)S(1)}, bf16[160,1280]{1,0:T(8,128)(2,1)S(1)}, u32[]{:S(2)}, u32[]{:S(2)}) %collective-permute-start.3) | collective-permute-done | bytes 409632 | tf_op jit(solution)/shard_map/ppermute | solution.py:550
  27.1 2.4 %collective-permute-done.10.refs_4_.refs_23_ = bf16[512,640]{1,0:T(8,128)(2,1)S(1)} collective-permute-done((bf16[512,640]{1,0:T(8,128)(2,1)}, bf16[512,640]{1,0:T(8,128)(2,1)S(1)}, u32[]{:S(2)}, u32[]{:S(2)}) %collective-permute-start.10) | collective-permute-done | bytes 655392 | tf_op jit(solution)/shard_map/ppermute | solution.py:550
  30.9 1.6 %collective-permute-start.12 = (bf16[256,640]{1,0:T(8,128)(2,1)S(1)}, bf16[256,640]{1,0:T(8,128)(2,1)S(1)}, u32[]{:S(2)}, u32[]{:S(2)}) collective-permute-start(bf16[256,640]{1,0:T(8,128)(2,1)S(1)} %slice.45), channel_id=1, source_target_pairs={{0,16},{8,24},{16,0},{24,8},{1,17},{9,25},{17,1},{25,9},{2,18},{10... | collective-permute-start | bytes 983048 | tf_op jit(solution)/shard_map/ppermute | solution.py:550
  32.6 7.0 %collective-permute-done.6.refs_11_.refs_12_ = bf16[160,1280]{1,0:T(8,128)(2,1)S(1)} collective-permute-done((bf16[160,1280]{1,0:T(8,128)(2,1)S(1)}, bf16[160,1280]{1,0:T(8,128)(2,1)S(1)}, u32[]{:S(2)}, u32[]{:S(2)}) %collective-permute-start.6) | collective-permute-done | bytes 409632 | tf_op jit(solution)/shard_map/ppermute | solution.py:550
  40.3 1.1 shard_map.173
  42.5 1.5 %collective-permute-start.24 = (bf16[4,32,1280]{2,1,0:T(8,128)(2,1)S(1)}, bf16[4,32,1280]{2,1,0:T(8,128)(2,1)S(1)}, u32[]{:S(2)}, u32[]{:S(2)}) collective-permute-start(bf16[4,32,1280]{2,1,0:T(8,128)(2,1)S(1)} %pad_maximum_fusion.1.refs_1_), channel_id=1, source_target_pairs={{0,16},{8,24},{16,0},{24,8},{1,17},{9,25},{17,1},{25,9},{2,18},{10... | collective-permute-start | bytes 983048 | tf_op jit(solution)/shard_map/ppermute | solution.py:550
  44.1 1.4 %collective-permute-start.25 = (bf16[4,32,1280]{2,1,0:T(8,128)(2,1)S(1)}, bf16[4,32,1280]{2,1,0:T(8,128)(2,1)S(1)}, u32[]{:S(2)}, u32[]{:S(2)}) collective-permute-start(bf16[4,32,1280]{2,1,0:T(8,128)(2,1)S(1)} %pad_maximum_fusion.1.refs_1_), channel_id=1, source_target_pairs={{0,24},{8,16},{16,8},{24,0},{1,25},{9,17},{17,9},{25,1},{2,26},{10... | collective-permute-start | bytes 983048 | tf_op jit(solution)/shard_map/ppermute | solution.py:550
  45.6 8.8 %shard_map.174.refs_1_ = bf16[1024,128]{1,0:T(8,128)(2,1)S(1)} custom-call(s32[2]{0:T(128)S(1)} %copy-done.2, s32[1,8]{1,0:T(1,128)S(1)} %copy-done.9, s32[1,8]{1,0:T(1,128)S(1)} %copy-done.10, s32[32,4]{1,0:T(8,128)S(1)} %copy.20.refs_3_, bf16[160,1280]{1,0:T(8,128)(2,1)S(1)} %pad_maximum_fusion.refs_4_.refs_11_, ...), custom_call_target="tpu_custom_call" | custom-call | flops 20000000000 | bytes 2000000 | tf_op jit(solution)/shard_map/pallas_call | solution.py:249
  55.0 1.9 %collective-permute-start.17 = (bf16[1024,128]{1,0:T(8,128)(2,1)S(1)}, bf16[1024,128]{1,0:T(8,128)(2,1)S(1)}, u32[]{:S(2)}, u32[]{:S(2)}) collective-permute-start(bf16[1024,128]{1,0:T(8,128)(2,1)S(1)} %shard_map.174.refs_1_), channel_id=1, source_target_pairs={{0,4},{1,5},{2,6},{3,7},{4,0},{5,1},{6,2},{7,3},{8,12},{9,13},{10,... | collective-permute-start | bytes 786440 | tf_op jit(solution)/shard_map/ppermute | solution.py:550
  56.9 1.1 collective-permute-done.24.refs_3_
  58.0 1.6 %collective-permute-done.25.refs_4_ = bf16[4,32,1280]{2,1,0:T(8,128)(2,1)S(1)} collective-permute-done((bf16[4,32,1280]{2,1,0:T(8,128)(2,1)S(1)}, bf16[4,32,1280]{2,1,0:T(8,128)(2,1)S(1)}, u32[]{:S(2)}, u32[]{:S(2)}) %collective-permute-start.25) | collective-permute-done | bytes 327712 | tf_op jit(solution)/shard_map/ppermute | solution.py:550
  61.7 7.0 %collective-permute-done.15.refs_3_ = bf16[1024,128]{1,0:T(8,128)(2,1)S(1)} collective-permute-done((bf16[1024,128]{1,0:T(8,128)(2,1)S(1)}, bf16[1024,128]{1,0:T(8,128)(2,1)S(1)}, u32[]{:S(2)}, u32[]{:S(2)}) %collective-permute-start.15) | collective-permute-done | bytes 262176 | tf_op jit(solution)/shard_map/ppermute | solution.py:550
  68.7 1.3 %collective-permute-done.17.refs_5_ = bf16[1024,128]{1,0:T(8,128)(2,1)S(1)} collective-permute-done((bf16[1024,128]{1,0:T(8,128)(2,1)S(1)}, bf16[1024,128]{1,0:T(8,128)(2,1)S(1)}, u32[]{:S(2)}, u32[]{:S(2)}) %collective-permute-start.17) | collective-permute-done | bytes 262176 | tf_op jit(solution)/shard_map/ppermute | solution.py:550
  70.9 6.5 %collective-permute-done.21.refs_9_ = bf16[1024,128]{1,0:T(8,128)(2,1)S(1)} collective-permute-done((bf16[1024,128]{1,0:T(8,128)(2,1)S(1)}, bf16[1024,128]{1,0:T(8,128)(2,1)S(1)}, u32[]{:S(2)}, u32[]{:S(2)}) %collective-permute-start.21) | collective-permute-done | bytes 262176 | tf_op jit(solution)/shard_map/ppermute | solution.py:550
  77.5 1.4 %collective-permute-done.22.refs_10_ = bf16[1024,128]{1,0:T(8,128)(2,1)S(1)} collective-permute-done((bf16[1024,128]{1,0:T(8,128)(2,1)S(1)}, bf16[1024,128]{1,0:T(8,128)(2,1)S(1)}, u32[]{:S(2)}, u32[]{:S(2)}) %collective-permute-start.22) | collective-permute-done | bytes 262176 | tf_op jit(solution)/shard_map/ppermute | solution.py:550
  79.0 3.7 %shard_map.176 = (bf16[128,1280]{1,0:T(8,128)(2,1)S(1)}, bf16[128,1280]{1,0:T(8,128)(2,1)S(1)}) custom-call(s32[2]{0:T(128)S(1)} %copy-done.2, bf16[1024,128]{1,0:T(8,128)(2,1)S(1)} %shard_map.174.refs_1_, bf16[1024,128]{1,0:T(8,128)(2,1)S(1)} %collective-permute-done.14.refs_2_, bf16[1024,128]{1,0:T(8,128)(2,1)S(1)} %collective-permute-done.15.refs_3_, ...), custom_call_target="tpu_custom_call" | custom-call | flops 20000000000 | bytes 10000000 | tf_op jit(solution)/shard_map/pallas_call | solution.py:249
  82.9 1.5 %collective-permute-done.28 = bf16[128,1280]{1,0:T(8,128)(2,1)S(1)} collective-permute-done((bf16[128,1280]{1,0:T(8,128)(2,1)S(1)}, bf16[128,1280]{1,0:T(8,128)(2,1)S(1)}, u32[]{:S(2)}, u32[]{:S(2)}) %collective-permute-start.28) | collective-permute-done | bytes 327712 | tf_op jit(solution)/shard_map/ppermute | solution.py:550
  86.0 6.6 %shard_map.177 = (bf16[256,1280]{1,0:T(8,128)(2,1)S(1)}, bf16[256,1280]{1,0:T(8,128)(2,1)S(1)}) custom-call(s32[2]{0:T(128)S(1)} %copy-done.2, bf16[1024,128]{1,0:T(8,128)(2,1)S(1)} %shard_map.174.refs_1_, bf16[1024,128]{1,0:T(8,128)(2,1)S(1)} %collective-permute-done.14.refs_2_, bf16[1024,128]{1,0:T(8,128)(2,1)S(1)} %collective-permute-done.15.refs_3_, ...), custom_call_target="tpu_custom_call" | custom-call | flops 20000000000 | bytes 10000000 | tf_op jit(solution)/shard_map/pallas_call | solution.py:249
  92.6 1.7 %collective-permute-done.29.refs_2_ = bf16[128,1280]{1,0:T(8,128)(2,1)S(1)} collective-permute-done((bf16[128,1280]{1,0:T(8,128)(2,1)S(1)}, bf16[128,1280]{1,0:T(8,128)(2,1)S(1)}, u32[]{:S(2)}, u32[]{:S(2)}) %collective-permute-start.29) | collective-permute-done | bytes 327712 | tf_op jit(solution)/shard_map/ppermute | solution.py:550
  95.1 3.9 %collective-permute-start.34 = (bf16[128,1280]{1,0:T(8,128)(2,1)S(1)}, bf16[128,1280]{1,0:T(8,128)(2,1)S(1)}, u32[]{:S(2)}, u32[]{:S(2)}) collective-permute-start(bf16[128,1280]{1,0:T(8,128)(2,1)S(1)} %get-tuple-element.27), channel_id=1, source_target_pairs={{0,2},{1,3},{2,0},{3,1},{4,6},{5,7},{6,4},{7,5},{8,10},{9,11},{10,... | collective-permute-start | bytes 983048 | tf_op jit(solution)/shard_map/ppermute | solution.py:550
  100.0 4.1 %shard_map.179 = (bf16[128,1280]{1,0:T(8,128)(2,1)S(1)}, bf16[128,1280]{1,0:T(8,128)(2,1)S(1)}, bf16[128,1280]{1,0:T(8,128)(2,1)S(1)}) custom-call(s32[2]{0:T(128)S(1)} %copy-done.2, bf16[1024,128]{1,0:T(8,128)(2,1)S(1)} %shard_map.174.refs_1_, bf16[1024,128]{1,0:T(8,128)(2,1)S(1)} %collective-permute-done.14.refs_2_, ...), custom_call_target="tpu_custom_call" | custom-call | flops 20000000000 | bytes 10000000 | tf_op jit(solution)/shard_map/pallas_call | solution.py:249
  105.8 7.0 %collective-permute-done.34.refs_4_ = bf16[128,1280]{1,0:T(8,128)(2,1)S(1)} collective-permute-done((bf16[128,1280]{1,0:T(8,128)(2,1)S(1)}, bf16[128,1280]{1,0:T(8,128)(2,1)S(1)}, u32[]{:S(2)}, u32[]{:S(2)}) %collective-permute-start.34) | collective-permute-done | bytes 327712 | tf_op jit(solution)/shard_map/ppermute | solution.py:550
  112.8 3.7 %collective-permute-done.35.refs_5_ = bf16[128,1280]{1,0:T(8,128)(2,1)S(1)} collective-permute-done((bf16[128,1280]{1,0:T(8,128)(2,1)S(1)}, bf16[128,1280]{1,0:T(8,128)(2,1)S(1)}, u32[]{:S(2)}, u32[]{:S(2)}) %collective-permute-start.35) | collective-permute-done | bytes 327712 | tf_op jit(solution)/shard_map/ppermute | solution.py:550
  116.5 1.2 %shard_map.180 = bf16[128,1280]{1,0:T(8,128)(2,1)} custom-call(bf16[128,1280]{1,0:T(8,128)(2,1)S(1)} %get-tuple-element.24.refs_0_, bf16[128,1280]{1,0:T(8,128)(2,1)S(1)} %get-tuple-element.25.refs_1_, bf16[64,1280]{1,0:T(8,128)(2,1)S(1)} %collective-permute-done.32.refs_2_, bf16[64,1280]{1,0:T(8,128)(2,1)S(1)} %collective-permute-done.33.refs_3_, ...), custom_call_target="tpu_custom_call" | custom-call | tf_op jit(solution)/shard_map/pallas_call | solution.py:249
  (105 shorter events, 14.9 us)
Async XLA Ops:
  2.0 39.4 %collective-permute-start = (bf16[160,1280]{1,0:T(8,128)(2,1)S(1)}, bf16[160,1280]{1,0:T(8,128)(2,1)}, u32[]{:S(2)}, u32[]{:S(2)}) collective-permute-start(bf16[160,1280]{1,0:T(8,128)(2,1)S(1)} %pad_maximum_fusion.refs_4_.refs_11_), channel_id=1, source_target_pairs={{0,1},{1,0},{2,3},{3,2},{4,5},{5,4},{6,7},{7,6},{8,9},{9,8},{10,11... | collective-permute-start | bytes 1228808 | tf_op jit(solution)/shard_map/ppermute | solution.py:550
  2.5 28.4 %collective-permute-start.1 = (bf16[160,1280]{1,0:T(8,128)(2,1)S(1)}, bf16[160,1280]{1,0:T(8,128)(2,1)S(1)}, u32[]{:S(2)}, u32[]{:S(2)}) collective-permute-start(bf16[160,1280]{1,0:T(8,128)(2,1)S(1)} %pad_maximum_fusion.refs_4_.refs_11_), channel_id=1, source_target_pairs={{0,2},{1,3},{2,0},{3,1},{4,6},{5,7},{6,4},{7,5},{8,10},{9,11},{10,... | collective-permute-start | bytes 1228808 | tf_op jit(solution)/shard_map/ppermute | solution.py:550
  5.2 21.3 %collective-permute-start.3 = (bf16[160,1280]{1,0:T(8,128)(2,1)S(1)}, bf16[160,1280]{1,0:T(8,128)(2,1)S(1)}, u32[]{:S(2)}, u32[]{:S(2)}) collective-permute-start(bf16[160,1280]{1,0:T(8,128)(2,1)S(1)} %pad_maximum_fusion.refs_4_.refs_11_), channel_id=1, source_target_pairs={{0,4},{1,5},{2,6},{3,7},{4,0},{5,1},{6,2},{7,3},{8,12},{9,13},{10,... | collective-permute-start | bytes 1228808 | tf_op jit(solution)/shard_map/ppermute | solution.py:550
  11.5 18.5 %collective-permute-start.9 = (bf16[512,640]{1,0:T(8,128)(2,1)}, bf16[512,640]{1,0:T(8,128)(2,1)S(1)}, u32[]{:S(2)}, u32[]{:S(2)}) collective-permute-start(bf16[512,640]{1,0:T(8,128)(2,1)} %shard_map.172.refs_2_.refs_21_), channel_id=1, source_target_pairs={{0,8},{8,0},{16,24},{24,16},{1,9},{9,1},{17,25},{25,17},{2,10},{10... | collective-permute-start | bytes 1966088 | tf_op jit(solution)/shard_map/ppermute | solution.py:550
  13.1 16.5 %collective-permute-start.10 = (bf16[512,640]{1,0:T(8,128)(2,1)}, bf16[512,640]{1,0:T(8,128)(2,1)S(1)}, u32[]{:S(2)}, u32[]{:S(2)}) collective-permute-start(bf16[512,640]{1,0:T(8,128)(2,1)} %shard_map.172.refs_2_.refs_21_), channel_id=1, source_target_pairs={{0,16},{8,24},{16,0},{24,8},{1,17},{9,25},{17,1},{25,9},{2,18},{10... | collective-permute-start | bytes 1966088 | tf_op jit(solution)/shard_map/ppermute | solution.py:550
  26.4 6.1 %collective-permute-start.5 = (bf16[160,1280]{1,0:T(8,128)(2,1)S(1)}, bf16[160,1280]{1,0:T(8,128)(2,1)S(1)}, u32[]{:S(2)}, u32[]{:S(2)}) collective-permute-start(bf16[160,1280]{1,0:T(8,128)(2,1)S(1)} %pad_maximum_fusion.refs_4_.refs_11_), channel_id=1, source_target_pairs={{2,4},{3,5},{4,2},{5,3},{10,12},{11,13},{12,10},{13,11},{18,20},{1... | collective-permute-start | bytes 1228808 | tf_op jit(solution)/shard_map/ppermute | solution.py:554
  29.5 10.1 %collective-permute-start.6 = (bf16[160,1280]{1,0:T(8,128)(2,1)S(1)}, bf16[160,1280]{1,0:T(8,128)(2,1)S(1)}, u32[]{:S(2)}, u32[]{:S(2)}) collective-permute-start(bf16[160,1280]{1,0:T(8,128)(2,1)S(1)} %collective-permute-done.3.refs_8_.refs_11_), channel_id=1, source_target_pairs={{0,2},{1,3},{2,0},{3,1},{4,6},{5,7},{6,4},{7,5},{8,10},{9,11},{10,... | collective-permute-start | bytes 1228808 | tf_op jit(solution)/shard_map/ppermute | solution.py:550
  30.0 9.6 %collective-permute-start.11 = (bf16[256,640]{1,0:T(8,128)(2,1)S(1)}, bf16[256,640]{1,0:T(8,128)(2,1)S(1)}, u32[]{:S(2)}, u32[]{:S(2)}) collective-permute-start(bf16[256,640]{1,0:T(8,128)(2,1)S(1)} %slice.44), channel_id=1, source_target_pairs={{0,8},{8,0},{16,24},{24,16},{1,9},{9,1},{17,25},{25,17},{2,10},{10... | collective-permute-start | bytes 983048 | tf_op jit(solution)/shard_map/ppermute | solution.py:550
  30.9 9.2 %collective-permute-start.12 = (bf16[256,640]{1,0:T(8,128)(2,1)S(1)}, bf16[256,640]{1,0:T(8,128)(2,1)S(1)}, u32[]{:S(2)}, u32[]{:S(2)}) collective-permute-start(bf16[256,640]{1,0:T(8,128)(2,1)S(1)} %slice.45), channel_id=1, source_target_pairs={{0,16},{8,24},{16,0},{24,8},{1,17},{9,25},{17,1},{25,9},{2,18},{10... | collective-permute-start | bytes 983048 | tf_op jit(solution)/shard_map/ppermute | solution.py:550
  32.5 9.4 %collective-permute-start.2 = (bf16[160,1280]{1,0:T(8,128)(2,1)S(1)}, bf16[160,1280]{1,0:T(8,128)(2,1)S(1)}, u32[]{:S(2)}, u32[]{:S(2)}) collective-permute-start(bf16[160,1280]{1,0:T(8,128)(2,1)S(1)} %collective-permute-done.1.refs_6_.refs_13_), channel_id=1, source_target_pairs={{0,1},{1,0},{2,3},{3,2},{4,5},{5,4},{6,7},{7,6},{8,9},{9,8},{10,11... | collective-permute-start | bytes 1228808 | tf_op jit(solution)/shard_map/ppermute | solution.py:550
  39.6 3.0 %collective-permute-start.4 = (bf16[160,1280]{1,0:T(8,128)(2,1)S(1)}, bf16[160,1280]{1,0:T(8,128)(2,1)S(1)}, u32[]{:S(2)}, u32[]{:S(2)}) collective-permute-start(bf16[160,1280]{1,0:T(8,128)(2,1)S(1)} %collective-permute-done.3.refs_8_.refs_11_), channel_id=1, source_target_pairs={{0,1},{1,0},{2,3},{3,2},{4,5},{5,4},{6,7},{7,6},{8,9},{9,8},{10,11... | collective-permute-start | bytes 1228808 | tf_op jit(solution)/shard_map/ppermute | solution.py:550
  39.6 4.5 %collective-permute-start.7 = (bf16[160,1280]{1,0:T(8,128)(2,1)S(1)}, bf16[160,1280]{1,0:T(8,128)(2,1)S(1)}, u32[]{:S(2)}, u32[]{:S(2)}) collective-permute-start(bf16[160,1280]{1,0:T(8,128)(2,1)S(1)} %collective-permute-done.5.refs_10_.refs_11_), channel_id=1, source_target_pairs={{0,1},{1,0},{2,3},{3,2},{4,5},{5,4},{6,7},{7,6},{8,9},{9,8},{10,11... | collective-permute-start | bytes 1228808 | tf_op jit(solution)/shard_map/ppermute | solution.py:550
  40.1 5.4 %collective-permute-start.8 = (bf16[160,1280]{1,0:T(8,128)(2,1)S(1)}, bf16[160,1280]{1,0:T(8,128)(2,1)S(1)}, u32[]{:S(2)}, u32[]{:S(2)}) collective-permute-start(bf16[160,1280]{1,0:T(8,128)(2,1)S(1)} %collective-permute-done.6.refs_11_.refs_12_), channel_id=1, source_target_pairs={{0,1},{1,0},{2,3},{3,2},{4,5},{5,4},{6,7},{7,6},{8,9},{9,8},{10,11... | collective-permute-start | bytes 1228808 | tf_op jit(solution)/shard_map/ppermute | solution.py:550
  41.4 4.1 %collective-permute-start.13 = (bf16[64,1280]{1,0:T(8,128)(2,1)S(1)}, bf16[64,1280]{1,0:T(8,128)(2,1)S(1)}, u32[]{:S(2)}, u32[]{:S(2)}) collective-permute-start(bf16[64,1280]{1,0:T(8,128)(2,1)S(1)} %get-tuple-element.16.refs_15_), channel_id=1, source_target_pairs={{0,1},{1,0},{2,3},{3,2},{4,5},{5,4},{6,7},{7,6},{8,9},{9,8},{10,11... | collective-permute-start | bytes 491528 | tf_op jit(solution)/shard_map/ppermute | solution.py:550
  41.9 13.1 %collective-permute-start.23 = (bf16[4,32,1280]{2,1,0:T(8,128)(2,1)S(1)}, bf16[4,32,1280]{2,1,0:T(8,128)(2,1)S(1)}, u32[]{:S(2)}, u32[]{:S(2)}) collective-permute-start(bf16[4,32,1280]{2,1,0:T(8,128)(2,1)S(1)} %pad_maximum_fusion.1.refs_1_), channel_id=1, source_target_pairs={{0,8},{8,0},{16,24},{24,16},{1,9},{9,1},{17,25},{25,17},{2,10},{10... | collective-permute-start | bytes 983048 | tf_op jit(solution)/shard_map/ppermute | solution.py:550
  42.5 15.5 %collective-permute-start.24 = (bf16[4,32,1280]{2,1,0:T(8,128)(2,1)S(1)}, bf16[4,32,1280]{2,1,0:T(8,128)(2,1)S(1)}, u32[]{:S(2)}, u32[]{:S(2)}) collective-permute-start(bf16[4,32,1280]{2,1,0:T(8,128)(2,1)S(1)} %pad_maximum_fusion.1.refs_1_), channel_id=1, source_target_pairs={{0,16},{8,24},{16,0},{24,8},{1,17},{9,25},{17,1},{25,9},{2,18},{10... | collective-permute-start | bytes 983048 | tf_op jit(solution)/shard_map/ppermute | solution.py:550
  44.1 15.6 %collective-permute-start.25 = (bf16[4,32,1280]{2,1,0:T(8,128)(2,1)S(1)}, bf16[4,32,1280]{2,1,0:T(8,128)(2,1)S(1)}, u32[]{:S(2)}, u32[]{:S(2)}) collective-permute-start(bf16[4,32,1280]{2,1,0:T(8,128)(2,1)S(1)} %pad_maximum_fusion.1.refs_1_), channel_id=1, source_target_pairs={{0,24},{8,16},{16,8},{24,0},{1,25},{9,17},{17,9},{25,1},{2,26},{10... | collective-permute-start | bytes 983048 | tf_op jit(solution)/shard_map/ppermute | solution.py:550
  54.4 6.4 %collective-permute-start.14 = (bf16[1024,128]{1,0:T(8,128)(2,1)S(1)}, bf16[1024,128]{1,0:T(8,128)(2,1)S(1)}, u32[]{:S(2)}, u32[]{:S(2)}) collective-permute-start(bf16[1024,128]{1,0:T(8,128)(2,1)S(1)} %shard_map.174.refs_1_), channel_id=1, source_target_pairs={{0,1},{1,0},{2,3},{3,2},{4,5},{5,4},{6,7},{7,6},{8,9},{9,8},{10,11... | collective-permute-start | bytes 786440 | tf_op jit(solution)/shard_map/ppermute | solution.py:550
  54.5 14.2 %collective-permute-start.15 = (bf16[1024,128]{1,0:T(8,128)(2,1)S(1)}, bf16[1024,128]{1,0:T(8,128)(2,1)S(1)}, u32[]{:S(2)}, u32[]{:S(2)}) collective-permute-start(bf16[1024,128]{1,0:T(8,128)(2,1)S(1)} %shard_map.174.refs_1_), channel_id=1, source_target_pairs={{0,2},{1,3},{2,0},{3,1},{4,6},{5,7},{6,4},{7,5},{8,10},{9,11},{10,... | collective-permute-start | bytes 786440 | tf_op jit(solution)/shard_map/ppermute | solution.py:550
  55.0 15.0 %collective-permute-start.17 = (bf16[1024,128]{1,0:T(8,128)(2,1)S(1)}, bf16[1024,128]{1,0:T(8,128)(2,1)S(1)}, u32[]{:S(2)}, u32[]{:S(2)}) collective-permute-start(bf16[1024,128]{1,0:T(8,128)(2,1)S(1)} %shard_map.174.refs_1_), channel_id=1, source_target_pairs={{0,4},{1,5},{2,6},{3,7},{4,0},{5,1},{6,2},{7,3},{8,12},{9,13},{10,... | collective-permute-start | bytes 786440 | tf_op jit(solution)/shard_map/ppermute | solution.py:550
  60.3 17.2 %collective-permute-start.26 = (bf16[256,1280]{1,0:T(8,128)(2,1)S(1)}, bf16[256,1280]{1,0:T(8,128)(2,1)S(1)}, u32[]{:S(2)}, u32[]{:S(2)}) collective-permute-start(bf16[256,1280]{1,0:T(8,128)(2,1)S(1)} %bitcast.22), channel_id=1, source_target_pairs={{0,1},{1,0},{2,3},{3,2},{4,5},{5,4},{6,7},{7,6},{8,9},{9,8},{10,11... | collective-permute-start | bytes 1966088 | tf_op jit(solution)/shard_map/ppermute | solution.py:550
  60.4 17.1 %collective-permute-start.27 = (bf16[256,1280]{1,0:T(8,128)(2,1)S(1)}, bf16[256,1280]{1,0:T(8,128)(2,1)S(1)}, u32[]{:S(2)}, u32[]{:S(2)}) collective-permute-start(bf16[256,1280]{1,0:T(8,128)(2,1)S(1)} %bitcast.26), channel_id=1, source_target_pairs={{0,1},{1,0},{2,3},{3,2},{4,5},{5,4},{6,7},{7,6},{8,9},{9,8},{10,11... | collective-permute-start | bytes 1966088 | tf_op jit(solution)/shard_map/ppermute | solution.py:550
  60.9 9.5 %collective-permute-start.19 = (bf16[1024,128]{1,0:T(8,128)(2,1)S(1)}, bf16[1024,128]{1,0:T(8,128)(2,1)S(1)}, u32[]{:S(2)}, u32[]{:S(2)}) collective-permute-start(bf16[1024,128]{1,0:T(8,128)(2,1)S(1)} %shard_map.174.refs_1_), channel_id=1, source_target_pairs={{2,4},{3,5},{4,2},{5,3},{10,12},{11,13},{12,10},{13,11},{18,20},{1... | collective-permute-start | bytes 786440 | tf_op jit(solution)/shard_map/ppermute | solution.py:554
  70.0 7.4 %collective-permute-start.21 = (bf16[1024,128]{1,0:T(8,128)(2,1)S(1)}, bf16[1024,128]{1,0:T(8,128)(2,1)S(1)}, u32[]{:S(2)}, u32[]{:S(2)}) collective-permute-start(bf16[1024,128]{1,0:T(8,128)(2,1)S(1)} %collective-permute-done.17.refs_5_), channel_id=1, source_target_pairs={{0,2},{1,3},{2,0},{3,1},{4,6},{5,7},{6,4},{7,5},{8,10},{9,11},{10,... | collective-permute-start | bytes 786440 | tf_op jit(solution)/shard_map/ppermute | solution.py:550
  70.4 7.1 %collective-permute-start.18 = (bf16[1024,128]{1,0:T(8,128)(2,1)S(1)}, bf16[1024,128]{1,0:T(8,128)(2,1)S(1)}, u32[]{:S(2)}, u32[]{:S(2)}) collective-permute-start(bf16[1024,128]{1,0:T(8,128)(2,1)S(1)} %collective-permute-done.17.refs_5_), channel_id=1, source_target_pairs={{0,1},{1,0},{2,3},{3,2},{4,5},{5,4},{6,7},{7,6},{8,9},{9,8},{10,11... | collective-permute-start | bytes 786440 | tf_op jit(solution)/shard_map/ppermute | solution.py:550
  70.4 7.1 %collective-permute-start.20 = (bf16[1024,128]{1,0:T(8,128)(2,1)S(1)}, bf16[1024,128]{1,0:T(8,128)(2,1)S(1)}, u32[]{:S(2)}, u32[]{:S(2)}) collective-permute-start(bf16[1024,128]{1,0:T(8,128)(2,1)S(1)} %collective-permute-done.19.refs_7_), channel_id=1, source_target_pairs={{0,1},{1,0},{2,3},{3,2},{4,5},{5,4},{6,7},{7,6},{8,9},{9,8},{10,11... | collective-permute-start | bytes 786440 | tf_op jit(solution)/shard_map/ppermute | solution.py:550
  82.7 1.7 %collective-permute-start.28 = (bf16[128,1280]{1,0:T(8,128)(2,1)S(1)}, bf16[128,1280]{1,0:T(8,128)(2,1)S(1)}, u32[]{:S(2)}, u32[]{:S(2)}) collective-permute-start(bf16[128,1280]{1,0:T(8,128)(2,1)S(1)} %get-tuple-element.22), channel_id=1, source_target_pairs={{0,1},{1,0},{2,3},{3,2},{4,5},{5,4},{6,7},{7,6},{8,9},{9,8},{10,11... | collective-permute-start | bytes 983048 | tf_op jit(solution)/shard_map/ppermute | solution.py:550
  84.5 9.8 %collective-permute-start.29 = (bf16[128,1280]{1,0:T(8,128)(2,1)S(1)}, bf16[128,1280]{1,0:T(8,128)(2,1)S(1)}, u32[]{:S(2)}, u32[]{:S(2)}) collective-permute-start(bf16[128,1280]{1,0:T(8,128)(2,1)S(1)} %add_convert_fusion.2), channel_id=1, source_target_pairs={{0,2},{1,3},{2,0},{3,1},{4,6},{5,7},{6,4},{7,5},{8,10},{9,11},{10,... | collective-permute-start | bytes 983048 | tf_op jit(solution)/shard_map/ppermute | solution.py:550
  85.3 9.0 %collective-permute-start.30 = (bf16[128,1280]{1,0:T(8,128)(2,1)S(1)}, bf16[128,1280]{1,0:T(8,128)(2,1)S(1)}, u32[]{:S(2)}, u32[]{:S(2)}) collective-permute-start(bf16[128,1280]{1,0:T(8,128)(2,1)S(1)} %add_convert_fusion.2), channel_id=1, source_target_pairs={{2,4},{3,5},{4,2},{5,3},{10,12},{11,13},{12,10},{13,11},{18,20},{1... | collective-permute-start | bytes 983048 | tf_op jit(solution)/shard_map/ppermute | solution.py:554
  92.6 2.4 %collective-permute-start.31 = (bf16[256,1280]{1,0:T(8,128)(2,1)S(1)}, bf16[256,1280]{1,0:T(8,128)(2,1)S(1)}, u32[]{:S(2)}, u32[]{:S(2)}) collective-permute-start(bf16[256,1280]{1,0:T(8,128)(2,1)S(1)} %get-tuple-element.23), channel_id=1, source_target_pairs={{0,1},{1,0},{2,3},{3,2},{4,5},{5,4},{6,7},{7,6},{8,9},{9,8},{10,11... | collective-permute-start | bytes 1966088 | tf_op jit(solution)/shard_map/ppermute | solution.py:550
  95.1 17.7 %collective-permute-start.34 = (bf16[128,1280]{1,0:T(8,128)(2,1)S(1)}, bf16[128,1280]{1,0:T(8,128)(2,1)S(1)}, u32[]{:S(2)}, u32[]{:S(2)}) collective-permute-start(bf16[128,1280]{1,0:T(8,128)(2,1)S(1)} %get-tuple-element.27), channel_id=1, source_target_pairs={{0,2},{1,3},{2,0},{3,1},{4,6},{5,7},{6,4},{7,5},{8,10},{9,11},{10,... | collective-permute-start | bytes 983048 | tf_op jit(solution)/shard_map/ppermute | solution.py:550
  99.1 17.4 %collective-permute-start.35 = (bf16[128,1280]{1,0:T(8,128)(2,1)S(1)}, bf16[128,1280]{1,0:T(8,128)(2,1)S(1)}, u32[]{:S(2)}, u32[]{:S(2)}) collective-permute-start(bf16[128,1280]{1,0:T(8,128)(2,1)S(1)} %get-tuple-element.28.refs_23_), channel_id=1, source_target_pairs={{0,4},{1,5},{2,6},{3,7},{4,0},{5,1},{6,2},{7,3},{8,12},{9,13},{10,... | collective-permute-start | bytes 983048 | tf_op jit(solution)/shard_map/ppermute | solution.py:550
  (20 other events, 341.2 us)

commit v6 on v5

--- a/solution.py
+++ b/solution.py
@@ -625,7 +625,7 @@
     )
     down_other = swap(down_own, 1)
 
-    rows = {0: [payload, swap(payload, 1)]}
+    rows = {0: [hidden, swap(hidden, 1)]}
     rows[1] = [far1, swap(far1, 1)]
     rows[2] = [far2, swap(far2, 1)]
     constants = (query_key_value_weight, down_own, down_other, up_all, cosines, sines, gain)

time: 118 us -> 117 us (level)
  starting transfers between devices: 29 us -> 30.2 us
where the time goes in v6:
time: 117 us
  waiting for transfers between devices  51.5 us (44%)
  starting transfers between devices  30.2 us (26%)
  Pallas kernels  29 us (25%)
  other arithmetic  4.83 us (4%)
    ppermute x33, waiting for transfers between devices, swap(): return lax.ppermute(values, axis, [(i, i ^ distance) for i in range(size)])  51.5 us
    pallas_call x9, Pallas kernels, call(): pl.pallas_call(whole, out_shape=outs, in_specs=specs, out_specs=jax.tree....  29 us
    ppermute x33, starting transfers between devices, swap(): return lax.ppermute(values, axis, [(i, i ^ distance) for i in range(size)])  28 us
  transfers between devices with their start and end apart: 36, of which 15 were waited for; matrix products, arithmetic and copies ran while one was open for 4% of the time, Pallas kernels for 21%

profile of v6, /device:TPU:0, one launch (start us, length us, event | category | flops | bytes accessed | tf_op | source)
XLA Modules:
  0.0 116.8 jit_solution(4037291469287465601)
XLA Ops:
  1.0 1.8 %pad_maximum_fusion = bf16[160,1280]{1,0:T(8,128)(2,1)} fusion(bf16[32,1280]{1,0:T(8,128)(2,1)S(1)} %constant_dynamic-slice_fusion, bf16[128,1280]{1,0:T(8,128)(2,1)} %refs_11_.1), kind=kLoop, calls=%fused_computation.6 | loop fusion | flops 819200 | bytes 819200 | tf_op jit(solution)/shard_map/concatenate | solution.py:597
  2.7 3.0 %collective-permute-start.1 = (bf16[160,1280]{1,0:T(8,128)(2,1)}, bf16[160,1280]{1,0:T(8,128)(2,1)S(1)}, u32[]{:S(2)}, u32[]{:S(2)}) collective-permute-start(bf16[160,1280]{1,0:T(8,128)(2,1)} %pad_maximum_fusion), channel_id=1, source_target_pairs={{0,2},{1,3},{2,0},{3,1},{4,6},{5,7},{6,4},{7,5},{8,10},{9,11},{10,... | collective-permute-start | bytes 1228808 | tf_op jit(solution)/shard_map/ppermute | solution.py:550
  5.8 2.6 %collective-permute-start.3 = (bf16[160,1280]{1,0:T(8,128)(2,1)}, bf16[160,1280]{1,0:T(8,128)(2,1)S(1)}, u32[]{:S(2)}, u32[]{:S(2)}) collective-permute-start(bf16[160,1280]{1,0:T(8,128)(2,1)} %pad_maximum_fusion), channel_id=1, source_target_pairs={{0,4},{1,5},{2,6},{3,7},{4,0},{5,1},{6,2},{7,3},{8,12},{9,13},{10,... | collective-permute-start | bytes 1228808 | tf_op jit(solution)/shard_map/ppermute | solution.py:550
  9.0 3.1 %shard_map.172.refs_2_.refs_21_ = bf16[512,640]{1,0:T(8,128)(2,1)} custom-call(s32[2]{0:T(128)} %pad_add_fusion.refs_0_.refs_25_, bf16[256,256]{1,0:T(8,128)(2,1)} %bitcast.32, bf16[256,384]{1,0:T(8,128)(2,1)} %bitcast.31, bf16[256,1280]{1,0:T(8,128)(2,1)} %bitcast.30, f32[1,128]{1,0:T(1,128)} %bitcast.20), custom_call_target="tpu_custom_call" | custom-call | tf_op jit(solution)/shard_map/pallas_call | solution.py:249
  12.1 1.6 %collective-permute-start.9 = (bf16[512,640]{1,0:T(8,128)(2,1)}, bf16[512,640]{1,0:T(8,128)(2,1)S(1)}, u32[]{:S(2)}, u32[]{:S(2)}) collective-permute-start(bf16[512,640]{1,0:T(8,128)(2,1)} %shard_map.172.refs_2_.refs_21_), channel_id=1, source_target_pairs={{0,8},{8,0},{16,24},{24,16},{1,9},{9,1},{17,25},{25,17},{2,10},{10... | collective-permute-start | bytes 1966088 | tf_op jit(solution)/shard_map/ppermute | solution.py:550
  13.6 1.5 %collective-permute-start.10 = (bf16[512,640]{1,0:T(8,128)(2,1)}, bf16[512,640]{1,0:T(8,128)(2,1)S(1)}, u32[]{:S(2)}, u32[]{:S(2)}) collective-permute-start(bf16[512,640]{1,0:T(8,128)(2,1)} %shard_map.172.refs_2_.refs_21_), channel_id=1, source_target_pairs={{0,16},{8,24},{16,0},{24,8},{1,17},{9,25},{17,1},{25,9},{2,18},{10... | collective-permute-start | bytes 1966088 | tf_op jit(solution)/shard_map/ppermute | solution.py:550
  15.6 1.9 %fusion = (f32[1024,128]{1,0:T(8,128)S(1)}, f32[1024,128]{1,0:T(8,128)S(1)}) fusion(f32[128]{0:T(128)S(1)} %get-tuple-element.33, f32[128]{0:T(128)S(1)} %get-tuple-element.34, f32[1024]{0:T(1024)S(1)} %convert_add_fusion), kind=kLoop, calls=%fused_computation.5 | loop fusion | flops 262144 | bytes 1053696 | tf_op jit(solution)/shard_map/mul | solution.py:593
  17.5 9.1 %collective-permute-done.3.refs_8_.refs_11_ = bf16[160,1280]{1,0:T(8,128)(2,1)S(1)} collective-permute-done((bf16[160,1280]{1,0:T(8,128)(2,1)}, bf16[160,1280]{1,0:T(8,128)(2,1)S(1)}, u32[]{:S(2)}, u32[]{:S(2)}) %collective-permute-start.3) | collective-permute-done | bytes 409632 | tf_op jit(solution)/shard_map/ppermute | solution.py:550
  27.3 2.1 %collective-permute-done.10.refs_4_.refs_23_ = bf16[512,640]{1,0:T(8,128)(2,1)S(1)} collective-permute-done((bf16[512,640]{1,0:T(8,128)(2,1)}, bf16[512,640]{1,0:T(8,128)(2,1)S(1)}, u32[]{:S(2)}, u32[]{:S(2)}) %collective-permute-start.10) | collective-permute-done | bytes 655392 | tf_op jit(solution)/shard_map/ppermute | solution.py:550
  30.0 1.1 collective-permute-start.11
  31.2 1.6 %collective-permute-start.12 = (bf16[256,640]{1,0:T(8,128)(2,1)S(1)}, bf16[256,640]{1,0:T(8,128)(2,1)S(1)}, u32[]{:S(2)}, u32[]{:S(2)}) collective-permute-start(bf16[256,640]{1,0:T(8,128)(2,1)S(1)} %slice.45), channel_id=1, source_target_pairs={{0,16},{8,24},{16,0},{24,8},{1,17},{9,25},{17,1},{25,9},{2,18},{10... | collective-permute-start | bytes 983048 | tf_op jit(solution)/shard_map/ppermute | solution.py:550
  32.8 6.1 %collective-permute-done.6.refs_11_.refs_12_ = bf16[160,1280]{1,0:T(8,128)(2,1)S(1)} collective-permute-done((bf16[160,1280]{1,0:T(8,128)(2,1)S(1)}, bf16[160,1280]{1,0:T(8,128)(2,1)S(1)}, u32[]{:S(2)}, u32[]{:S(2)}) %collective-permute-start.6) | collective-permute-done | bytes 409632 | tf_op jit(solution)/shard_map/ppermute | solution.py:550
  39.6 1.1 shard_map.173
  41.9 1.5 %collective-permute-start.24 = (bf16[4,32,1280]{2,1,0:T(8,128)(2,1)S(1)}, bf16[4,32,1280]{2,1,0:T(8,128)(2,1)S(1)}, u32[]{:S(2)}, u32[]{:S(2)}) collective-permute-start(bf16[4,32,1280]{2,1,0:T(8,128)(2,1)S(1)} %pad_maximum_fusion.1.refs_1_), channel_id=1, source_target_pairs={{0,16},{8,24},{16,0},{24,8},{1,17},{9,25},{17,1},{25,9},{2,18},{10... | collective-permute-start | bytes 983048 | tf_op jit(solution)/shard_map/ppermute | solution.py:550
  43.4 1.4 %collective-permute-start.25 = (bf16[4,32,1280]{2,1,0:T(8,128)(2,1)S(1)}, bf16[4,32,1280]{2,1,0:T(8,128)(2,1)S(1)}, u32[]{:S(2)}, u32[]{:S(2)}) collective-permute-start(bf16[4,32,1280]{2,1,0:T(8,128)(2,1)S(1)} %pad_maximum_fusion.1.refs_1_), channel_id=1, source_target_pairs={{0,24},{8,16},{16,8},{24,0},{1,25},{9,17},{17,9},{25,1},{2,26},{10... | collective-permute-start | bytes 983048 | tf_op jit(solution)/shard_map/ppermute | solution.py:550
  45.0 8.3 %shard_map.174.refs_1_ = bf16[1024,128]{1,0:T(8,128)(2,1)S(1)} custom-call(s32[2]{0:T(128)S(1)} %copy-done.3, s32[1,8]{1,0:T(1,128)S(1)} %copy-done.10, s32[1,8]{1,0:T(1,128)S(1)} %copy-done.11, s32[32,4]{1,0:T(8,128)S(1)} %copy.20.refs_3_, bf16[128,1280]{1,0:T(8,128)(2,1)S(1)} %copy-done.2, bf16[128,1280]{1,0:T(8,128)(2,1)S(1)} %collective-permute-done.refs_5_.refs_12_, ...), custom_call_target="tpu_custom_call" | custom-call | flops 20000000000 | bytes 2000000 | tf_op jit(solution)/shard_map/pallas_call | solution.py:249
  54.0 1.9 %collective-permute-start.17 = (bf16[1024,128]{1,0:T(8,128)(2,1)S(1)}, bf16[1024,128]{1,0:T(8,128)(2,1)S(1)}, u32[]{:S(2)}, u32[]{:S(2)}) collective-permute-start(bf16[1024,128]{1,0:T(8,128)(2,1)S(1)} %shard_map.174.refs_1_), channel_id=1, source_target_pairs={{0,4},{1,5},{2,6},{3,7},{4,0},{5,1},{6,2},{7,3},{8,12},{9,13},{10,... | collective-permute-start | bytes 786440 | tf_op jit(solution)/shard_map/ppermute | solution.py:550
  56.0 1.4 %collective-permute-done.24.refs_3_ = bf16[4,32,1280]{2,1,0:T(8,128)(2,1)S(1)} collective-permute-done((bf16[4,32,1280]{2,1,0:T(8,128)(2,1)S(1)}, bf16[4,32,1280]{2,1,0:T(8,128)(2,1)S(1)}, u32[]{:S(2)}, u32[]{:S(2)}) %collective-permute-start.24) | collective-permute-done | bytes 327712 | tf_op jit(solution)/shard_map/ppermute | solution.py:550
  57.4 1.6 %collective-permute-done.25.refs_4_ = bf16[4,32,1280]{2,1,0:T(8,128)(2,1)S(1)} collective-permute-done((bf16[4,32,1280]{2,1,0:T(8,128)(2,1)S(1)}, bf16[4,32,1280]{2,1,0:T(8,128)(2,1)S(1)}, u32[]{:S(2)}, u32[]{:S(2)}) %collective-permute-start.25) | collective-permute-done | bytes 327712 | tf_op jit(solution)/shard_map/ppermute | solution.py:550
  61.1 6.5 %collective-permute-done.15.refs_3_ = bf16[1024,128]{1,0:T(8,128)(2,1)S(1)} collective-permute-done((bf16[1024,128]{1,0:T(8,128)(2,1)S(1)}, bf16[1024,128]{1,0:T(8,128)(2,1)S(1)}, u32[]{:S(2)}, u32[]{:S(2)}) %collective-permute-start.15) | collective-permute-done | bytes 262176 | tf_op jit(solution)/shard_map/ppermute | solution.py:550
  67.6 1.4 %collective-permute-done.17.refs_5_ = bf16[1024,128]{1,0:T(8,128)(2,1)S(1)} collective-permute-done((bf16[1024,128]{1,0:T(8,128)(2,1)S(1)}, bf16[1024,128]{1,0:T(8,128)(2,1)S(1)}, u32[]{:S(2)}, u32[]{:S(2)}) %collective-permute-start.17) | collective-permute-done | bytes 262176 | tf_op jit(solution)/shard_map/ppermute | solution.py:550
  69.9 6.4 %collective-permute-done.21.refs_9_ = bf16[1024,128]{1,0:T(8,128)(2,1)S(1)} collective-permute-done((bf16[1024,128]{1,0:T(8,128)(2,1)S(1)}, bf16[1024,128]{1,0:T(8,128)(2,1)S(1)}, u32[]{:S(2)}, u32[]{:S(2)}) %collective-permute-start.21) | collective-permute-done | bytes 262176 | tf_op jit(solution)/shard_map/ppermute | solution.py:550
  76.4 1.4 %collective-permute-done.22.refs_10_ = bf16[1024,128]{1,0:T(8,128)(2,1)S(1)} collective-permute-done((bf16[1024,128]{1,0:T(8,128)(2,1)S(1)}, bf16[1024,128]{1,0:T(8,128)(2,1)S(1)}, u32[]{:S(2)}, u32[]{:S(2)}) %collective-permute-start.22) | collective-permute-done | bytes 262176 | tf_op jit(solution)/shard_map/ppermute | solution.py:550
  77.9 3.7 %shard_map.176 = (bf16[128,1280]{1,0:T(8,128)(2,1)S(1)}, bf16[128,1280]{1,0:T(8,128)(2,1)S(1)}) custom-call(s32[2]{0:T(128)S(1)} %copy-done.3, bf16[1024,128]{1,0:T(8,128)(2,1)S(1)} %shard_map.174.refs_1_, bf16[1024,128]{1,0:T(8,128)(2,1)S(1)} %collective-permute-done.14.refs_2_, bf16[1024,128]{1,0:T(8,128)(2,1)S(1)} %collective-permute-done.15.refs_3_, ...), custom_call_target="tpu_custom_call" | custom-call | flops 20000000000 | bytes 10000000 | tf_op jit(solution)/shard_map/pallas_call | solution.py:249
  81.8 1.5 %collective-permute-done.28 = bf16[128,1280]{1,0:T(8,128)(2,1)S(1)} collective-permute-done((bf16[128,1280]{1,0:T(8,128)(2,1)S(1)}, bf16[128,1280]{1,0:T(8,128)(2,1)S(1)}, u32[]{:S(2)}, u32[]{:S(2)}) %collective-permute-start.28) | collective-permute-done | bytes 327712 | tf_op jit(solution)/shard_map/ppermute | solution.py:550
  85.0 6.6 %shard_map.177 = (bf16[256,1280]{1,0:T(8,128)(2,1)S(1)}, bf16[256,1280]{1,0:T(8,128)(2,1)S(1)}) custom-call(s32[2]{0:T(128)S(1)} %copy-done.3, bf16[1024,128]{1,0:T(8,128)(2,1)S(1)} %shard_map.174.refs_1_, bf16[1024,128]{1,0:T(8,128)(2,1)S(1)} %collective-permute-done.14.refs_2_, bf16[1024,128]{1,0:T(8,128)(2,1)S(1)} %collective-permute-done.15.refs_3_, ...), custom_call_target="tpu_custom_call" | custom-call | flops 20000000000 | bytes 10000000 | tf_op jit(solution)/shard_map/pallas_call | solution.py:249
  91.7 1.5 %collective-permute-done.29.refs_2_ = bf16[128,1280]{1,0:T(8,128)(2,1)S(1)} collective-permute-done((bf16[128,1280]{1,0:T(8,128)(2,1)S(1)}, bf16[128,1280]{1,0:T(8,128)(2,1)S(1)}, u32[]{:S(2)}, u32[]{:S(2)}) %collective-permute-start.29) | collective-permute-done | bytes 327712 | tf_op jit(solution)/shard_map/ppermute | solution.py:550
  94.0 4.1 %collective-permute-start.34 = (bf16[128,1280]{1,0:T(8,128)(2,1)S(1)}, bf16[128,1280]{1,0:T(8,128)(2,1)S(1)}, u32[]{:S(2)}, u32[]{:S(2)}) collective-permute-start(bf16[128,1280]{1,0:T(8,128)(2,1)S(1)} %get-tuple-element.27), channel_id=1, source_target_pairs={{0,2},{1,3},{2,0},{3,1},{4,6},{5,7},{6,4},{7,5},{8,10},{9,11},{10,... | collective-permute-start | bytes 983048 | tf_op jit(solution)/shard_map/ppermute | solution.py:550
  99.0 3.7 %shard_map.179 = (bf16[128,1280]{1,0:T(8,128)(2,1)S(1)}, bf16[128,1280]{1,0:T(8,128)(2,1)S(1)}, bf16[128,1280]{1,0:T(8,128)(2,1)S(1)}) custom-call(s32[2]{0:T(128)S(1)} %copy-done.3, bf16[1024,128]{1,0:T(8,128)(2,1)S(1)} %shard_map.174.refs_1_, bf16[1024,128]{1,0:T(8,128)(2,1)S(1)} %collective-permute-done.14.refs_2_, ...), custom_call_target="tpu_custom_call" | custom-call | flops 20000000000 | bytes 10000000 | tf_op jit(solution)/shard_map/pallas_call | solution.py:249
  104.4 7.3 %collective-permute-done.34.refs_4_ = bf16[128,1280]{1,0:T(8,128)(2,1)S(1)} collective-permute-done((bf16[128,1280]{1,0:T(8,128)(2,1)S(1)}, bf16[128,1280]{1,0:T(8,128)(2,1)S(1)}, u32[]{:S(2)}, u32[]{:S(2)}) %collective-permute-start.34) | collective-permute-done | bytes 327712 | tf_op jit(solution)/shard_map/ppermute | solution.py:550
  111.7 3.9 %collective-permute-done.35.refs_5_ = bf16[128,1280]{1,0:T(8,128)(2,1)S(1)} collective-permute-done((bf16[128,1280]{1,0:T(8,128)(2,1)S(1)}, bf16[128,1280]{1,0:T(8,128)(2,1)S(1)}, u32[]{:S(2)}, u32[]{:S(2)}) %collective-permute-start.35) | collective-permute-done | bytes 327712 | tf_op jit(solution)/shard_map/ppermute | solution.py:550
  115.6 1.2 %shard_map.180 = bf16[128,1280]{1,0:T(8,128)(2,1)} custom-call(bf16[128,1280]{1,0:T(8,128)(2,1)S(1)} %get-tuple-element.24.refs_0_, bf16[128,1280]{1,0:T(8,128)(2,1)S(1)} %get-tuple-element.25.refs_1_, bf16[64,1280]{1,0:T(8,128)(2,1)S(1)} %collective-permute-done.32.refs_2_, bf16[64,1280]{1,0:T(8,128)(2,1)S(1)} %collective-permute-done.33.refs_3_, ...), custom_call_target="tpu_custom_call" | custom-call | tf_op jit(solution)/shard_map/pallas_call | solution.py:249
  (107 shorter events, 14.1 us)
Async XLA Ops:
  0.0 40.7 %collective-permute-start = (bf16[128,1280]{1,0:T(8,128)(2,1)}, bf16[128,1280]{1,0:T(8,128)(2,1)S(1)}, u32[]{:S(2)}, u32[]{:S(2)}) collective-permute-start(bf16[128,1280]{1,0:T(8,128)(2,1)} %refs_11_.1), channel_id=1, source_target_pairs={{0,1},{1,0},{2,3},{3,2},{4,5},{5,4},{6,7},{7,6},{8,9},{9,8},{10,11... | collective-permute-start | bytes 983048 | tf_op jit(solution)/shard_map/ppermute | solution.py:550
  2.7 28.4 %collective-permute-start.1 = (bf16[160,1280]{1,0:T(8,128)(2,1)}, bf16[160,1280]{1,0:T(8,128)(2,1)S(1)}, u32[]{:S(2)}, u32[]{:S(2)}) collective-permute-start(bf16[160,1280]{1,0:T(8,128)(2,1)} %pad_maximum_fusion), channel_id=1, source_target_pairs={{0,2},{1,3},{2,0},{3,1},{4,6},{5,7},{6,4},{7,5},{8,10},{9,11},{10,... | collective-permute-start | bytes 1228808 | tf_op jit(solution)/shard_map/ppermute | solution.py:550
  5.8 20.9 %collective-permute-start.3 = (bf16[160,1280]{1,0:T(8,128)(2,1)}, bf16[160,1280]{1,0:T(8,128)(2,1)S(1)}, u32[]{:S(2)}, u32[]{:S(2)}) collective-permute-start(bf16[160,1280]{1,0:T(8,128)(2,1)} %pad_maximum_fusion), channel_id=1, source_target_pairs={{0,4},{1,5},{2,6},{3,7},{4,0},{5,1},{6,2},{7,3},{8,12},{9,13},{10,... | collective-permute-start | bytes 1228808 | tf_op jit(solution)/shard_map/ppermute | solution.py:550
  12.1 17.9 %collective-permute-start.9 = (bf16[512,640]{1,0:T(8,128)(2,1)}, bf16[512,640]{1,0:T(8,128)(2,1)S(1)}, u32[]{:S(2)}, u32[]{:S(2)}) collective-permute-start(bf16[512,640]{1,0:T(8,128)(2,1)} %shard_map.172.refs_2_.refs_21_), channel_id=1, source_target_pairs={{0,8},{8,0},{16,24},{24,16},{1,9},{9,1},{17,25},{25,17},{2,10},{10... | collective-permute-start | bytes 1966088 | tf_op jit(solution)/shard_map/ppermute | solution.py:550
  13.6 15.8 %collective-permute-start.10 = (bf16[512,640]{1,0:T(8,128)(2,1)}, bf16[512,640]{1,0:T(8,128)(2,1)S(1)}, u32[]{:S(2)}, u32[]{:S(2)}) collective-permute-start(bf16[512,640]{1,0:T(8,128)(2,1)} %shard_map.172.refs_2_.refs_21_), channel_id=1, source_target_pairs={{0,16},{8,24},{16,0},{24,8},{1,17},{9,25},{17,1},{25,9},{2,18},{10... | collective-permute-start | bytes 1966088 | tf_op jit(solution)/shard_map/ppermute | solution.py:550
  26.6 6.1 %collective-permute-start.5 = (bf16[160,1280]{1,0:T(8,128)(2,1)}, bf16[160,1280]{1,0:T(8,128)(2,1)S(1)}, u32[]{:S(2)}, u32[]{:S(2)}) collective-permute-start(bf16[160,1280]{1,0:T(8,128)(2,1)} %pad_maximum_fusion), channel_id=1, source_target_pairs={{2,4},{3,5},{4,2},{5,3},{10,12},{11,13},{12,10},{13,11},{18,20},{1... | collective-permute-start | bytes 1228808 | tf_op jit(solution)/shard_map/ppermute | solution.py:554
  29.5 9.4 %collective-permute-start.6 = (bf16[160,1280]{1,0:T(8,128)(2,1)S(1)}, bf16[160,1280]{1,0:T(8,128)(2,1)S(1)}, u32[]{:S(2)}, u32[]{:S(2)}) collective-permute-start(bf16[160,1280]{1,0:T(8,128)(2,1)S(1)} %collective-permute-done.3.refs_8_.refs_11_), channel_id=1, source_target_pairs={{0,2},{1,3},{2,0},{3,1},{4,6},{5,7},{6,4},{7,5},{8,10},{9,11},{10,... | collective-permute-start | bytes 1228808 | tf_op jit(solution)/shard_map/ppermute | solution.py:550
  30.0 9.0 %collective-permute-start.11 = (bf16[256,640]{1,0:T(8,128)(2,1)S(1)}, bf16[256,640]{1,0:T(8,128)(2,1)S(1)}, u32[]{:S(2)}, u32[]{:S(2)}) collective-permute-start(bf16[256,640]{1,0:T(8,128)(2,1)S(1)} %slice.44), channel_id=1, source_target_pairs={{0,8},{8,0},{16,24},{24,16},{1,9},{9,1},{17,25},{25,17},{2,10},{10... | collective-permute-start | bytes 983048 | tf_op jit(solution)/shard_map/ppermute | solution.py:550
  31.2 8.3 %collective-permute-start.12 = (bf16[256,640]{1,0:T(8,128)(2,1)S(1)}, bf16[256,640]{1,0:T(8,128)(2,1)S(1)}, u32[]{:S(2)}, u32[]{:S(2)}) collective-permute-start(bf16[256,640]{1,0:T(8,128)(2,1)S(1)} %slice.45), channel_id=1, source_target_pairs={{0,16},{8,24},{16,0},{24,8},{1,17},{9,25},{17,1},{25,9},{2,18},{10... | collective-permute-start | bytes 983048 | tf_op jit(solution)/shard_map/ppermute | solution.py:550
  32.7 8.5 %collective-permute-start.2 = (bf16[160,1280]{1,0:T(8,128)(2,1)S(1)}, bf16[160,1280]{1,0:T(8,128)(2,1)S(1)}, u32[]{:S(2)}, u32[]{:S(2)}) collective-permute-start(bf16[160,1280]{1,0:T(8,128)(2,1)S(1)} %collective-permute-done.1.refs_6_.refs_13_), channel_id=1, source_target_pairs={{0,1},{1,0},{2,3},{3,2},{4,5},{5,4},{6,7},{7,6},{8,9},{9,8},{10,11... | collective-permute-start | bytes 1228808 | tf_op jit(solution)/shard_map/ppermute | solution.py:550
  38.9 3.0 %collective-permute-start.4 = (bf16[160,1280]{1,0:T(8,128)(2,1)S(1)}, bf16[160,1280]{1,0:T(8,128)(2,1)S(1)}, u32[]{:S(2)}, u32[]{:S(2)}) collective-permute-start(bf16[160,1280]{1,0:T(8,128)(2,1)S(1)} %collective-permute-done.3.refs_8_.refs_11_), channel_id=1, source_target_pairs={{0,1},{1,0},{2,3},{3,2},{4,5},{5,4},{6,7},{7,6},{8,9},{9,8},{10,11... | collective-permute-start | bytes 1228808 | tf_op jit(solution)/shard_map/ppermute | solution.py:550
  38.9 4.5 %collective-permute-start.7 = (bf16[160,1280]{1,0:T(8,128)(2,1)S(1)}, bf16[160,1280]{1,0:T(8,128)(2,1)S(1)}, u32[]{:S(2)}, u32[]{:S(2)}) collective-permute-start(bf16[160,1280]{1,0:T(8,128)(2,1)S(1)} %collective-permute-done.5.refs_10_.refs_11_), channel_id=1, source_target_pairs={{0,1},{1,0},{2,3},{3,2},{4,5},{5,4},{6,7},{7,6},{8,9},{9,8},{10,11... | collective-permute-start | bytes 1228808 | tf_op jit(solution)/shard_map/ppermute | solution.py:550
  39.4 5.4 %collective-permute-start.8 = (bf16[160,1280]{1,0:T(8,128)(2,1)S(1)}, bf16[160,1280]{1,0:T(8,128)(2,1)S(1)}, u32[]{:S(2)}, u32[]{:S(2)}) collective-permute-start(bf16[160,1280]{1,0:T(8,128)(2,1)S(1)} %collective-permute-done.6.refs_11_.refs_12_), channel_id=1, source_target_pairs={{0,1},{1,0},{2,3},{3,2},{4,5},{5,4},{6,7},{7,6},{8,9},{9,8},{10,11... | collective-permute-start | bytes 1228808 | tf_op jit(solution)/shard_map/ppermute | solution.py:550
  40.7 4.1 %collective-permute-start.13 = (bf16[64,1280]{1,0:T(8,128)(2,1)S(1)}, bf16[64,1280]{1,0:T(8,128)(2,1)S(1)}, u32[]{:S(2)}, u32[]{:S(2)}) collective-permute-start(bf16[64,1280]{1,0:T(8,128)(2,1)S(1)} %get-tuple-element.16.refs_15_), channel_id=1, source_target_pairs={{0,1},{1,0},{2,3},{3,2},{4,5},{5,4},{6,7},{7,6},{8,9},{9,8},{10,11... | collective-permute-start | bytes 491528 | tf_op jit(solution)/shard_map/ppermute | solution.py:550
  41.3 12.8 %collective-permute-start.23 = (bf16[4,32,1280]{2,1,0:T(8,128)(2,1)S(1)}, bf16[4,32,1280]{2,1,0:T(8,128)(2,1)S(1)}, u32[]{:S(2)}, u32[]{:S(2)}) collective-permute-start(bf16[4,32,1280]{2,1,0:T(8,128)(2,1)S(1)} %pad_maximum_fusion.1.refs_1_), channel_id=1, source_target_pairs={{0,8},{8,0},{16,24},{24,16},{1,9},{9,1},{17,25},{25,17},{2,10},{10... | collective-permute-start | bytes 983048 | tf_op jit(solution)/shard_map/ppermute | solution.py:550
  41.9 15.5 %collective-permute-start.24 = (bf16[4,32,1280]{2,1,0:T(8,128)(2,1)S(1)}, bf16[4,32,1280]{2,1,0:T(8,128)(2,1)S(1)}, u32[]{:S(2)}, u32[]{:S(2)}) collective-permute-start(bf16[4,32,1280]{2,1,0:T(8,128)(2,1)S(1)} %pad_maximum_fusion.1.refs_1_), channel_id=1, source_target_pairs={{0,16},{8,24},{16,0},{24,8},{1,17},{9,25},{17,1},{25,9},{2,18},{10... | collective-permute-start | bytes 983048 | tf_op jit(solution)/shard_map/ppermute | solution.py:550
  43.4 15.6 %collective-permute-start.25 = (bf16[4,32,1280]{2,1,0:T(8,128)(2,1)S(1)}, bf16[4,32,1280]{2,1,0:T(8,128)(2,1)S(1)}, u32[]{:S(2)}, u32[]{:S(2)}) collective-permute-start(bf16[4,32,1280]{2,1,0:T(8,128)(2,1)S(1)} %pad_maximum_fusion.1.refs_1_), channel_id=1, source_target_pairs={{0,24},{8,16},{16,8},{24,0},{1,25},{9,17},{17,9},{25,1},{2,26},{10... | collective-permute-start | bytes 983048 | tf_op jit(solution)/shard_map/ppermute | solution.py:550
  53.3 6.9 %collective-permute-start.14 = (bf16[1024,128]{1,0:T(8,128)(2,1)S(1)}, bf16[1024,128]{1,0:T(8,128)(2,1)S(1)}, u32[]{:S(2)}, u32[]{:S(2)}) collective-permute-start(bf16[1024,128]{1,0:T(8,128)(2,1)S(1)} %shard_map.174.refs_1_), channel_id=1, source_target_pairs={{0,1},{1,0},{2,3},{3,2},{4,5},{5,4},{6,7},{7,6},{8,9},{9,8},{10,11... | collective-permute-start | bytes 786440 | tf_op jit(solution)/shard_map/ppermute | solution.py:550
  53.4 14.2 %collective-permute-start.15 = (bf16[1024,128]{1,0:T(8,128)(2,1)S(1)}, bf16[1024,128]{1,0:T(8,128)(2,1)S(1)}, u32[]{:S(2)}, u32[]{:S(2)}) collective-permute-start(bf16[1024,128]{1,0:T(8,128)(2,1)S(1)} %shard_map.174.refs_1_), channel_id=1, source_target_pairs={{0,2},{1,3},{2,0},{3,1},{4,6},{5,7},{6,4},{7,5},{8,10},{9,11},{10,... | collective-permute-start | bytes 786440 | tf_op jit(solution)/shard_map/ppermute | solution.py:550
  54.0 15.0 %collective-permute-start.17 = (bf16[1024,128]{1,0:T(8,128)(2,1)S(1)}, bf16[1024,128]{1,0:T(8,128)(2,1)S(1)}, u32[]{:S(2)}, u32[]{:S(2)}) collective-permute-start(bf16[1024,128]{1,0:T(8,128)(2,1)S(1)} %shard_map.174.refs_1_), channel_id=1, source_target_pairs={{0,4},{1,5},{2,6},{3,7},{4,0},{5,1},{6,2},{7,3},{8,12},{9,13},{10,... | collective-permute-start | bytes 786440 | tf_op jit(solution)/shard_map/ppermute | solution.py:550
  59.6 16.8 %collective-permute-start.26 = (bf16[256,1280]{1,0:T(8,128)(2,1)S(1)}, bf16[256,1280]{1,0:T(8,128)(2,1)S(1)}, u32[]{:S(2)}, u32[]{:S(2)}) collective-permute-start(bf16[256,1280]{1,0:T(8,128)(2,1)S(1)} %bitcast.22), channel_id=1, source_target_pairs={{0,1},{1,0},{2,3},{3,2},{4,5},{5,4},{6,7},{7,6},{8,9},{9,8},{10,11... | collective-permute-start | bytes 1966088 | tf_op jit(solution)/shard_map/ppermute | solution.py:550
  59.7 16.7 %collective-permute-start.27 = (bf16[256,1280]{1,0:T(8,128)(2,1)S(1)}, bf16[256,1280]{1,0:T(8,128)(2,1)S(1)}, u32[]{:S(2)}, u32[]{:S(2)}) collective-permute-start(bf16[256,1280]{1,0:T(8,128)(2,1)S(1)} %bitcast.26), channel_id=1, source_target_pairs={{0,1},{1,0},{2,3},{3,2},{4,5},{5,4},{6,7},{7,6},{8,9},{9,8},{10,11... | collective-permute-start | bytes 1966088 | tf_op jit(solution)/shard_map/ppermute | solution.py:550
  60.2 9.2 %collective-permute-start.19 = (bf16[1024,128]{1,0:T(8,128)(2,1)S(1)}, bf16[1024,128]{1,0:T(8,128)(2,1)S(1)}, u32[]{:S(2)}, u32[]{:S(2)}) collective-permute-start(bf16[1024,128]{1,0:T(8,128)(2,1)S(1)} %shard_map.174.refs_1_), channel_id=1, source_target_pairs={{2,4},{3,5},{4,2},{5,3},{10,12},{11,13},{12,10},{13,11},{18,20},{1... | collective-permute-start | bytes 786440 | tf_op jit(solution)/shard_map/ppermute | solution.py:554
  67.6 1.8 %collective-permute-start.16 = (bf16[1024,128]{1,0:T(8,128)(2,1)S(1)}, bf16[1024,128]{1,0:T(8,128)(2,1)S(1)}, u32[]{:S(2)}, u32[]{:S(2)}) collective-permute-start(bf16[1024,128]{1,0:T(8,128)(2,1)S(1)} %collective-permute-done.15.refs_3_), channel_id=1, source_target_pairs={{0,1},{1,0},{2,3},{3,2},{4,5},{5,4},{6,7},{7,6},{8,9},{9,8},{10,11... | collective-permute-start | bytes 786440 | tf_op jit(solution)/shard_map/ppermute | solution.py:550
  69.0 7.3 %collective-permute-start.21 = (bf16[1024,128]{1,0:T(8,128)(2,1)S(1)}, bf16[1024,128]{1,0:T(8,128)(2,1)S(1)}, u32[]{:S(2)}, u32[]{:S(2)}) collective-permute-start(bf16[1024,128]{1,0:T(8,128)(2,1)S(1)} %collective-permute-done.17.refs_5_), channel_id=1, source_target_pairs={{0,2},{1,3},{2,0},{3,1},{4,6},{5,7},{6,4},{7,5},{8,10},{9,11},{10,... | collective-permute-start | bytes 786440 | tf_op jit(solution)/shard_map/ppermute | solution.py:550
  69.4 7.0 %collective-permute-start.18 = (bf16[1024,128]{1,0:T(8,128)(2,1)S(1)}, bf16[1024,128]{1,0:T(8,128)(2,1)S(1)}, u32[]{:S(2)}, u32[]{:S(2)}) collective-permute-start(bf16[1024,128]{1,0:T(8,128)(2,1)S(1)} %collective-permute-done.17.refs_5_), channel_id=1, source_target_pairs={{0,1},{1,0},{2,3},{3,2},{4,5},{5,4},{6,7},{7,6},{8,9},{9,8},{10,11... | collective-permute-start | bytes 786440 | tf_op jit(solution)/shard_map/ppermute | solution.py:550
  69.4 7.0 %collective-permute-start.20 = (bf16[1024,128]{1,0:T(8,128)(2,1)S(1)}, bf16[1024,128]{1,0:T(8,128)(2,1)S(1)}, u32[]{:S(2)}, u32[]{:S(2)}) collective-permute-start(bf16[1024,128]{1,0:T(8,128)(2,1)S(1)} %collective-permute-done.19.refs_7_), channel_id=1, source_target_pairs={{0,1},{1,0},{2,3},{3,2},{4,5},{5,4},{6,7},{7,6},{8,9},{9,8},{10,11... | collective-permute-start | bytes 786440 | tf_op jit(solution)/shard_map/ppermute | solution.py:550
  83.4 9.8 %collective-permute-start.29 = (bf16[128,1280]{1,0:T(8,128)(2,1)S(1)}, bf16[128,1280]{1,0:T(8,128)(2,1)S(1)}, u32[]{:S(2)}, u32[]{:S(2)}) collective-permute-start(bf16[128,1280]{1,0:T(8,128)(2,1)S(1)} %add_convert_fusion.2), channel_id=1, source_target_pairs={{0,2},{1,3},{2,0},{3,1},{4,6},{5,7},{6,4},{7,5},{8,10},{9,11},{10,... | collective-permute-start | bytes 983048 | tf_op jit(solution)/shard_map/ppermute | solution.py:550
  84.4 8.9 %collective-permute-start.30 = (bf16[128,1280]{1,0:T(8,128)(2,1)S(1)}, bf16[128,1280]{1,0:T(8,128)(2,1)S(1)}, u32[]{:S(2)}, u32[]{:S(2)}) collective-permute-start(bf16[128,1280]{1,0:T(8,128)(2,1)S(1)} %add_convert_fusion.2), channel_id=1, source_target_pairs={{2,4},{3,5},{4,2},{5,3},{10,12},{11,13},{12,10},{13,11},{18,20},{1... | collective-permute-start | bytes 983048 | tf_op jit(solution)/shard_map/ppermute | solution.py:554
  91.7 2.2 %collective-permute-start.31 = (bf16[256,1280]{1,0:T(8,128)(2,1)S(1)}, bf16[256,1280]{1,0:T(8,128)(2,1)S(1)}, u32[]{:S(2)}, u32[]{:S(2)}) collective-permute-start(bf16[256,1280]{1,0:T(8,128)(2,1)S(1)} %get-tuple-element.23), channel_id=1, source_target_pairs={{0,1},{1,0},{2,3},{3,2},{4,5},{5,4},{6,7},{7,6},{8,9},{9,8},{10,11... | collective-permute-start | bytes 1966088 | tf_op jit(solution)/shard_map/ppermute | solution.py:550
  94.0 17.7 %collective-permute-start.34 = (bf16[128,1280]{1,0:T(8,128)(2,1)S(1)}, bf16[128,1280]{1,0:T(8,128)(2,1)S(1)}, u32[]{:S(2)}, u32[]{:S(2)}) collective-permute-start(bf16[128,1280]{1,0:T(8,128)(2,1)S(1)} %get-tuple-element.27), channel_id=1, source_target_pairs={{0,2},{1,3},{2,0},{3,1},{4,6},{5,7},{6,4},{7,5},{8,10},{9,11},{10,... | collective-permute-start | bytes 983048 | tf_op jit(solution)/shard_map/ppermute | solution.py:550
  98.2 17.4 %collective-permute-start.35 = (bf16[128,1280]{1,0:T(8,128)(2,1)S(1)}, bf16[128,1280]{1,0:T(8,128)(2,1)S(1)}, u32[]{:S(2)}, u32[]{:S(2)}) collective-permute-start(bf16[128,1280]{1,0:T(8,128)(2,1)S(1)} %get-tuple-element.28.refs_23_), channel_id=1, source_target_pairs={{0,4},{1,5},{2,6},{3,7},{4,0},{5,1},{6,2},{7,3},{8,12},{9,13},{10,... | collective-permute-start | bytes 983048 | tf_op jit(solution)/shard_map/ppermute | solution.py:550
  (21 other events, 339.7 us)
